TPU v7x, 512 devices: a whole 4x4x16 slice. The times are simulated.
512 devices in a mesh: ctx: 32 (over z, core), head: 8 (over y, x_hi), grp: 2 (over x_lo).
Axes of the slice: x: 4 (x_hi: 2, x_lo: 2; x = x_hi * 2 + x_lo), y: 4, z: 16, core: 2. Of those that a mesh axis runs over, the one named last changes fastest.
Arguments:
- new_queries: bfloat16 [3072, 16384], P('ctx', ('head', 'grp')), may hold values from -6 to 6
- new_keys: bfloat16 [3072, 1024], P('ctx', 'head'), may hold values from -6 to 6
- new_values: bfloat16 [3072, 1024], P('ctx', 'head'), may hold values from -6 to 6
- segment_ids: int32 [3072], replicated, may hold values from 0 to 1, never falling along the last dimension, each value on 1 to 2304 neighbouring positions
- page_table: int32 [192], replicated, may hold values from 0 to 191, as said below
- decode_query_rows: bfloat16 [64, 16384], P(None, 'head'), may hold values from -6 to 6
- resident_keys: bfloat16 [64, 2048, 1024], P(None, ('ctx', 'grp'), 'head'), may hold values from -6 to 6
- resident_values: bfloat16 [64, 2048, 1024], P(None, ('ctx', 'grp'), 'head'), may hold values from -6 to 6
- res_len: int32 [64], replicated, may hold values from 1 to 2048, as said below
Outputs:
- prefill_out: bfloat16 [3072, 16384], P('ctx', ('head', 'grp'))
- paged_keys: bfloat16 [192, 16, 1024], P('ctx', None, 'head')
- paged_values: bfloat16 [192, 16, 1024], P('ctx', None, 'head')
- decode_out: bfloat16 [64, 16384], P(None, 'head')
Inputs may be any that keep to these rules, and one draw needn't show every extreme that they name: The entries are a permutation of the page slots; page b lives on the ctx index b // 6 before the re-paging and on the ctx index page_table[b] // 6 after it; every ctx index receives exactly 6 pages, at most 1 from any one ctx index, and exactly 1 from some. `res_len`: some row has every resident position live and some row only one.
All inputs are finite; a program needn't handle non-finite values.
Results may differ from a plain program's by a relative error of at most 0.007.
Values may be sent and summed in bfloat16 or wider, within the bound.
No kernel may reach another device: no remote copies, remote signals or barrier semaphores. Data moves between devices by JAX's collectives and lax.ppermute only.
A program may use at most 128 MiB of HBM per device.

v0:
```python
import jax
import jax.numpy as jnp
from jax import lax
from jax.sharding import PartitionSpec as P

QUERY_HEADS = 128
KEY_VALUE_HEADS = 8
HEAD_SIZE = 128
PAGE_TOKENS = 16


NEG_FILL = -1e30


def joined(part, axis, combine):
    gathered = jax.tree.map(lambda a: lax.all_gather(a, axis), part)

    def take(source):
        return jax.tree.map(lambda a: lax.dynamic_index_in_dim(a, source, 0, False), gathered)

    return lax.fori_loop(
        1, lax.axis_size(axis), lambda source, state: combine(state, take(source)), take(0)
    )


def attend_keys(state_now, queries, key_rows, value_rows, allowed, score_scale):
    running_max, running_sum, weighted = state_now
    scores = (
        jnp.einsum("tgqd,ngd->tgqn", queries, key_rows, preferred_element_type=jnp.float32)
        * score_scale
    )
    wide_mask = allowed[:, None, None, :]
    scores = jnp.where(wide_mask, scores, NEG_FILL)
    fresh_max = jnp.maximum(running_max, jnp.max(scores, axis=-1))
    weights = jnp.where(wide_mask, jnp.exp(scores - fresh_max[..., None]), 0.0).astype(jnp.bfloat16)
    rescale = jnp.exp(running_max - fresh_max)
    running_sum = running_sum * rescale + jnp.sum(weights.astype(jnp.float32), axis=-1)
    weighted = weighted * rescale[..., None] + jnp.einsum(
        "tgqn,ngd->tgqd", weights, value_rows, preferred_element_type=jnp.float32
    )
    return (fresh_max, running_sum, weighted)


def combine_states(earlier, later):
    max_a, sum_a, weighted_a = earlier
    max_b, sum_b, weighted_b = later
    joined_max = jnp.maximum(max_a, max_b)
    factor_a = jnp.exp(max_a - joined_max)
    factor_b = jnp.exp(max_b - joined_max)
    joined_sum = sum_a * factor_a + sum_b * factor_b
    joined_weighted = weighted_a * factor_a[..., None] + weighted_b * factor_b[..., None]
    return (joined_max, joined_sum, joined_weighted)


def local(
    new_queries,
    new_keys,
    new_values,
    segment_ids,
    page_table,
    decode_query_rows,
    resident_keys,
    resident_values,
    res_len,
):
    tok_rows = new_queries.shape[0]
    ctx_count = lax.axis_size("ctx")
    grp_count = lax.axis_size("grp")
    ctx_index = lax.axis_index("ctx")
    grp_index = lax.axis_index("grp")
    score_scale = HEAD_SIZE ** (-0.5)
    kv_dev = new_keys.shape[1] // HEAD_SIZE
    q_dev = new_queries.shape[1] // HEAD_SIZE
    kv_used = max(kv_dev // grp_count, 1)
    heads_per = q_dev // kv_used
    queries = new_queries.reshape(tok_rows, kv_used, heads_per, HEAD_SIZE)
    query_first = ctx_index * tok_rows
    query_pos = query_first + jnp.arange(tok_rows, dtype=jnp.int32)
    query_seg = lax.dynamic_slice_in_dim(segment_ids, query_first, tok_rows)
    initial = (
        jnp.full((tok_rows, kv_used, heads_per), NEG_FILL, jnp.float32),
        jnp.zeros((tok_rows, kv_used, heads_per), jnp.float32),
        jnp.zeros((tok_rows, kv_used, heads_per, HEAD_SIZE), jnp.float32),
    )
    key_part = lax.all_gather(new_keys, "ctx", axis=0, tiled=True)
    value_part = lax.all_gather(new_values, "ctx", axis=0, tiled=True)
    shard_count = key_part.shape[0] // tok_rows
    group_size = 1
    for trial in range(1, shard_count + 1):
        if shard_count % trial == 0 and trial * tok_rows <= 768:
            group_size = trial
    block_rows = group_size * tok_rows

    def one_block(step_index, carried):
        row_begin = step_index * block_rows
        key_rows = lax.dynamic_slice_in_dim(key_part, row_begin, block_rows, 0).reshape(
            block_rows, kv_used, HEAD_SIZE
        )
        value_rows = lax.dynamic_slice_in_dim(value_part, row_begin, block_rows, 0).reshape(
            block_rows, kv_used, HEAD_SIZE
        )
        key_pos = row_begin + jnp.arange(block_rows, dtype=jnp.int32)
        key_seg = lax.dynamic_slice_in_dim(segment_ids, row_begin, block_rows)
        allowed = (key_pos[None, :] <= query_pos[:, None]) & (
            key_seg[None, :] == query_seg[:, None]
        )
        return attend_keys(carried, queries, key_rows, value_rows, allowed, score_scale)

    final_max, final_sum, final_weighted = lax.fori_loop(
        0, shard_count // group_size, one_block, initial
    )
    prefill_out = (
        (final_weighted / final_sum[..., None])
        .astype(jnp.bfloat16)
        .reshape(tok_rows, q_dev * HEAD_SIZE)
    )
    pages_dev = tok_rows // PAGE_TOKENS
    page_rows = PAGE_TOKENS
    capacity = (pages_dev + ctx_count - 1) // ctx_count
    columns = new_keys.shape[1]
    stacked = jnp.stack((new_keys, new_values)).reshape(2, pages_dev, page_rows * columns)
    slot_table = page_table.reshape(ctx_count, pages_dev)
    all_targets = slot_table // pages_dev
    page_ids = jnp.arange(pages_dev, dtype=jnp.int32)
    before_mask = page_ids[None, :] < page_ids[:, None]
    same_target = (all_targets[:, :, None] == all_targets[:, None, :]) & before_mask[None, :, :]
    send_rank = jnp.sum(same_target.astype(jnp.int32), axis=2)
    my_targets = lax.dynamic_index_in_dim(all_targets, ctx_index, 0, keepdims=False)
    my_ranks = lax.dynamic_index_in_dim(send_rank, ctx_index, 0, keepdims=False)
    send_slot = my_targets * capacity + my_ranks
    slot_ids = jnp.arange(ctx_count * capacity, dtype=jnp.int32)
    ordering = (send_slot[None, :] == slot_ids[:, None]).astype(jnp.bfloat16)
    outgoing = jnp.einsum(
        "dj,cjx->cdx", ordering, stacked, preferred_element_type=jnp.float32
    ).astype(jnp.bfloat16)
    arrived = lax.all_to_all(outgoing, "ctx", split_axis=1, concat_axis=1, tiled=True)
    landing = all_targets == ctx_index
    source_slot = jnp.arange(ctx_count, dtype=jnp.int32)[:, None] * capacity + send_rank
    dest_slot = slot_table % pages_dev
    dest_onehot = ((dest_slot[:, :, None] == page_ids[None, None, :]) & landing[:, :, None]).astype(
        jnp.float32
    )
    source_onehot = (source_slot[:, :, None] == slot_ids[None, None, :]).astype(jnp.float32)
    placing = jnp.einsum("sip,sik->pk", dest_onehot, source_onehot).astype(jnp.bfloat16)
    paged = jnp.einsum("pk,ckx->cpx", placing, arrived, preferred_element_type=jnp.float32).astype(
        jnp.bfloat16
    )
    paged_keys = paged[0].reshape(pages_dev, page_rows, columns)
    paged_values = paged[1].reshape(pages_dev, page_rows, columns)
    row_count = decode_query_rows.shape[0]
    repeat_factor = QUERY_HEADS // KEY_VALUE_HEADS
    res_rows = resident_keys.shape[1]
    dec_queries = decode_query_rows.reshape(row_count, kv_dev, repeat_factor, HEAD_SIZE)
    half_rows = tok_rows // grp_count
    prefix_keys = lax.dynamic_slice_in_dim(
        paged[0].reshape(tok_rows, columns), grp_index * half_rows, half_rows, 0
    ).reshape(half_rows, kv_dev, HEAD_SIZE)
    prefix_values = lax.dynamic_slice_in_dim(
        paged[1].reshape(tok_rows, columns), grp_index * half_rows, half_rows, 0
    ).reshape(half_rows, kv_dev, HEAD_SIZE)
    resident_key_rows = resident_keys.reshape(row_count, res_rows, kv_dev, HEAD_SIZE)
    resident_value_rows = resident_values.reshape(row_count, res_rows, kv_dev, HEAD_SIZE)
    res_base = (ctx_index * grp_count + grp_index) * res_rows
    live = (res_base + jnp.arange(res_rows, dtype=jnp.int32))[None, :] < res_len[:, None]
    live_wide = live[:, None, None, :]
    prefix_scores = (
        jnp.einsum("rgqd,ngd->rgqn", dec_queries, prefix_keys, preferred_element_type=jnp.float32)
        * score_scale
    )
    res_scores = (
        jnp.einsum(
            "rgqd,rpgd->rgqp", dec_queries, resident_key_rows, preferred_element_type=jnp.float32
        )
        * score_scale
    )
    res_scores = jnp.where(live_wide, res_scores, NEG_FILL)
    local_max = jnp.maximum(jnp.max(prefix_scores, axis=-1), jnp.max(res_scores, axis=-1))
    prefix_weights = jnp.exp(prefix_scores - local_max[..., None]).astype(jnp.bfloat16)
    res_weights = jnp.where(live_wide, jnp.exp(res_scores - local_max[..., None]), 0.0).astype(
        jnp.bfloat16
    )
    local_sum = jnp.sum(prefix_weights.astype(jnp.float32), axis=-1) + jnp.sum(
        res_weights.astype(jnp.float32), axis=-1
    )
    local_weighted = jnp.einsum(
        "rgqn,ngd->rgqd", prefix_weights, prefix_values, preferred_element_type=jnp.float32
    )
    local_weighted = local_weighted + jnp.einsum(
        "rgqp,rpgd->rgqd", res_weights, resident_value_rows, preferred_element_type=jnp.float32
    )
    joined_max, joined_sum, joined_weighted = joined(
        (local_max, local_sum, local_weighted), ("ctx", "grp"), combine_states
    )
    decoded = (joined_weighted / joined_sum[..., None]).astype(jnp.bfloat16)
    decode_out = decoded.reshape(row_count, kv_dev * repeat_factor * HEAD_SIZE)
    return (prefill_out, paged_keys, paged_values, decode_out)


def solution(mesh):
    return jax.shard_map(
        local,
        mesh=mesh,
        in_specs=(
            P("ctx", ("head", "grp")),
            P("ctx", "head"),
            P("ctx", "head"),
            P(),
            P(),
            P(None, "head"),
            P(None, ("ctx", "grp"), "head"),
            P(None, ("ctx", "grp"), "head"),
            P(),
        ),
        out_specs=(
            P("ctx", ("head", "grp")),
            P("ctx", None, "head"),
            P("ctx", None, "head"),
            P(None, "head"),
        ),
        check_vma=False,
    )
```

profile of v0, /device:TPU:1, one launch (start us, length us, event | category | flops | bytes accessed | tf_op | source)
XLA Modules:
  0.0 502.3 jit_solution(15884205114364528410)
XLA Ops:
  12.5 16.8 %all-to-all-start = ((bf16[2,32,2048]{2,0,1:T(2,128)(2,1)}), bf16[2,32,2048]{2,0,1:T(2,128)(2,1)S(1)}, u32[]{:S(2)}, u32[]{:S(2)}) async-start(bf16[2,32,2048]{2,0,1:T(2,128)(2,1)} %copy.101), calls=%async_computation | async-start | bytes 524288 | tf_op jit(solution)/shard_map/all_to_all | solution.py:136
  31.6 19.6 %all-to-all-done = bf16[2,32,2048]{2,0,1:T(2,128)(2,1)S(1)} async-done(((bf16[2,32,2048]{2,0,1:T(2,128)(2,1)}), bf16[2,32,2048]{2,0,1:T(2,128)(2,1)S(1)}, u32[]{:S(2)}, u32[]{:S(2)}) %all-to-all-start) | async-done | bytes 262176 | tf_op jit(solution)/shard_map/all_to_all | solution.py:136
  53.3 1.1 fusion.23
  54.6 1.4 dynamic_slice.78
  55.9 32.4 %all_gather.20 = bf16[3072,128]{1,0:T(8,128)(2,1)} all-gather(bf16[96,128]{1,0:T(8,128)(2,1)S(1)} %copy-done.11), channel_id=1, replica_groups=mesh['ctx'=32,'head'=8,'grp'=2] {'ctx'}, dimensions={0}, use_global_device_ids=true | all-gather | bytes 811008 | tf_op jit(solution)/shard_map/all_gather | solution.py:85
  88.4 34.0 %all_gather.21 = bf16[3072,128]{1,0:T(8,128)(2,1)} all-gather(bf16[96,128]{1,0:T(8,128)(2,1)S(1)} %copy-done.12), channel_id=1, replica_groups=mesh['ctx'=32,'head'=8,'grp'=2] {'ctx'}, dimensions={0}, use_global_device_ids=true | all-gather | bytes 811008 | tf_op jit(solution)/shard_map/all_gather | solution.py:86
  122.4 29.1 %while.38 = (s32[]{:T(128)}, f32[96,1,8]{0,2,1:T(8,128)S(1)}, f32[96,1,8]{0,2,1:T(8,128)}, f32[96,1,8,128]{3,0,2,1:T(8,128)}, s32[3072]{0:T(1024)}, /*index=5*/s...) while((s32[]{:T(128)}, f32[96,1,8]{0,2,1:T(8,128)S(1)}, ...), condition=%wide.region_3.4_spmd.clone, body=%wide.region_0.3_spmd.clone.sunk | while | flops 311358816 | bytes 8839563 | solution.py:109
  124.0 1.6 fusion.75
  125.6 2.5 fusion.77
  131.1 1.6 fusion.75
  132.7 2.7 fusion.77
  138.4 1.6 fusion.75
  140.0 2.7 fusion.77
  145.7 1.6 fusion.75
  147.3 2.7 fusion.77
  151.4 1.2 divide_convert_fusion.1
  153.5 1.4 convert_reduce_fusion.1
  155.0 1.4 copy.144
  156.3 1.4 copy.145
  158.5 107.6 %all-gather.4 = f32[64,64,16]{1,2,0:T(8,128)S(1)} all-gather(f32[1,64,16]{1,2,0:T(8,128)S(1)} %add_bitcast_fusion), channel_id=3, replica_groups=mesh['ctx'=32,'head'=8,'grp'=2] {'ctx','grp'}, dimensions={0}, use_global_device_ids=true | all-gather | bytes 266240 | tf_op jit(solution)/shard_map/all_gather | solution.py:16
  266.1 105.8 %all-gather.3 = f32[64,64,16]{1,2,0:T(8,128)S(1)} all-gather(f32[1,64,16]{1,2,0:T(8,128)S(1)} %bitcast.208), channel_id=2, replica_groups=mesh['ctx'=32,'head'=8,'grp'=2] {'ctx','grp'}, dimensions={0}, use_global_device_ids=true | all-gather | bytes 266240 | tf_op jit(solution)/shard_map/all_gather | solution.py:16
  373.3 121.0 %while.37 = (s32[]{:T(128)}, f32[64,1,16]{0,2,1:T(8,128)S(1)}, f32[64,1,16]{0,2,1:T(8,128)S(1)}, f32[64,1,16,128]{3,2,1,0:T(8,128)S(1)}, f32[64,64,1,16]{1,3,2,0...) while((s32[]{:T(128)}, f32[64,1,16]{0,2,1:T(8,128)S(1)}, ...), condition=%wide.region_10.11_spmd, body=%wide.region_9.10_spmd.sunk | while | flops 400389 | bytes 2699419 | solution.py:21
  373.6 1.1 constant_dynamic-slice_fusion.2
  375.5 1.1 constant_dynamic-slice_fusion.2
  379.3 1.1 constant_dynamic-slice_fusion.2
  381.2 1.1 constant_dynamic-slice_fusion.2
  383.2 1.1 constant_dynamic-slice_fusion.2
  385.1 1.1 constant_dynamic-slice_fusion.2
  388.9 1.1 constant_dynamic-slice_fusion.2
  390.9 1.1 constant_dynamic-slice_fusion.2
  394.7 1.1 constant_dynamic-slice_fusion.2
  396.6 1.1 constant_dynamic-slice_fusion.2
  400.5 1.1 constant_dynamic-slice_fusion.2
  402.4 1.1 constant_dynamic-slice_fusion.2
  404.3 1.1 constant_dynamic-slice_fusion.2
  406.2 1.1 constant_dynamic-slice_fusion.2
  410.1 1.1 constant_dynamic-slice_fusion.2
  412.0 1.1 constant_dynamic-slice_fusion.2
  415.8 1.1 constant_dynamic-slice_fusion.2
  417.7 1.1 constant_dynamic-slice_fusion.2
  419.7 1.1 constant_dynamic-slice_fusion.2
  421.6 1.1 constant_dynamic-slice_fusion.2
  425.4 1.1 constant_dynamic-slice_fusion.2
  427.4 1.1 constant_dynamic-slice_fusion.2
  431.2 1.1 constant_dynamic-slice_fusion.2
  433.1 1.1 constant_dynamic-slice_fusion.2
  437.0 1.1 constant_dynamic-slice_fusion.2
  438.9 1.1 constant_dynamic-slice_fusion.2
  440.8 1.1 constant_dynamic-slice_fusion.2
  442.7 1.1 constant_dynamic-slice_fusion.2
  446.6 1.1 constant_dynamic-slice_fusion.2
  448.5 1.1 constant_dynamic-slice_fusion.2
  452.3 1.1 constant_dynamic-slice_fusion.2
  454.2 1.1 constant_dynamic-slice_fusion.2
  456.2 1.1 constant_dynamic-slice_fusion.2
  458.1 1.1 constant_dynamic-slice_fusion.2
  461.9 1.1 constant_dynamic-slice_fusion.2
  463.9 1.1 constant_dynamic-slice_fusion.2
  467.7 1.1 constant_dynamic-slice_fusion.2
  469.6 1.1 constant_dynamic-slice_fusion.2
  473.5 1.1 constant_dynamic-slice_fusion.2
  475.4 1.1 constant_dynamic-slice_fusion.2
  477.3 1.1 constant_dynamic-slice_fusion.2
  479.2 1.1 constant_dynamic-slice_fusion.2
  (519 shorter events, 97.4 us)
Async XLA Ops:
  7.2 45.7 %copy-start = (bf16[64,32,128]{2,1,0:T(8,128)(2,1)S(1)}, bf16[64,32,128]{2,1,0:T(8,128)(2,1)}, u32[]{:S(2)}) copy-start(bf16[64,32,128]{2,1,0:T(8,128)(2,1)} %param.20) | copy-start | bytes 1572868
  7.2 45.2 %copy-start.2 = (bf16[64,2048]{1,0:T(8,128)(2,1)S(1)}, bf16[64,2048]{1,0:T(8,128)(2,1)}, u32[]{:S(2)}) copy-start(bf16[64,2048]{1,0:T(8,128)(2,1)} %param.18) | copy-start | bytes 786436
  7.2 23.9 %copy-start.3 = (bf16[64,32,128]{2,1,0:T(8,128)(2,1)S(1)}, bf16[64,32,128]{2,1,0:T(8,128)(2,1)}, u32[]{:S(2)}) copy-start(bf16[64,32,128]{2,1,0:T(8,128)(2,1)} %param.19) | copy-start | bytes 1572868
  12.5 38.8 %all-to-all-start = ((bf16[2,32,2048]{2,0,1:T(2,128)(2,1)}), bf16[2,32,2048]{2,0,1:T(2,128)(2,1)S(1)}, u32[]{:S(2)}, u32[]{:S(2)}) async-start(bf16[2,32,2048]{2,0,1:T(2,128)(2,1)} %copy.101), calls=%async_computation | async-start | bytes 524288 | tf_op jit(solution)/shard_map/all_to_all | solution.py:136
  29.3 342.7 %all-gather.7.cloned.1.call-start = ((), (), s32[]{:S(2)}) async-start(), calls=%async_computation.1 | async-start | bytes 34078720 | tf_op jit(solution)/shard_map/all_gather | solution.py:16
  31.1 23.4 %copy-start.10 = (pred[64,32]{1,0:T(8,128)(4,1)}, pred[64,32]{1,0:T(8,128)(4,1)S(1)}, u32[]{:S(2)}) copy-start(pred[64,32]{1,0:T(8,128)(4,1)S(1)} %broadcast_compare_fusion) | copy-start | bytes 6148
  31.6 22.9 %copy-start.1 = (f32[64,16,32]{2,1,0:T(8,128)}, f32[64,16,32]{2,1,0:T(8,128)S(1)}, u32[]{:S(2)}) copy-start(f32[64,16,32]{2,1,0:T(8,128)S(1)} %get-tuple-element.536) | copy-start | bytes 393220
  51.6 2.9 copy-start.7
  52.7 3.2 copy-start.11
  52.7 35.6 %copy-start.5 = (f32[64,16]{0,1:T(8,128)}, f32[64,16]{0,1:T(8,128)S(1)}, u32[]{:S(2)}) copy-start(f32[64,16]{0,1:T(8,128)S(1)} %max.36) | copy-start | bytes 12292
  52.8 35.6 %copy-start.4 = (f32[64,16]{1,0:T(8,128)}, f32[64,16]{1,0:T(8,128)S(1)}, u32[]{:S(2)}) copy-start(f32[64,16]{1,0:T(8,128)S(1)} %copy.108) | copy-start | bytes 12292
  52.9 35.5 %copy-start.12 = (bf16[96,128]{1,0:T(8,128)(2,1)S(1)}, bf16[96,128]{1,0:T(8,128)(2,1)}, u32[]{:S(2)}) copy-start(bf16[96,128]{1,0:T(8,128)(2,1)} %param.15) | copy-start | bytes 73732
  128.1 0.8 copy-start.8
  128.9 0.6 copy-start.9
  135.4 0.8 copy-start.8
  136.2 0.6 copy-start.9
  142.7 0.8 copy-start.8
  143.5 0.6 copy-start.9
  150.0 0.8 copy-start.8
  150.8 0.6 copy-start.9
  151.4 114.7 %copy-start.6 = (f32[64,16]{0,1:T(8,128)S(1)}, f32[64,16]{0,1:T(8,128)}, u32[]{:S(2)}) copy-start(f32[64,16]{0,1:T(8,128)} %copy-done.5) | copy-start | bytes 12292
Sparse Core Ops, SparseCore 0:
  54.6 223.5 all-gather.6
where the time goes:
time: 507 us; the launch traced here: 502 us
  blocking collectives  280 us (55%)
  local copies, waits for them, and re-layouts  96.9 us (19%)
  other arithmetic  51 us (10%)
  matrix products  20.1 us (4%)
  waiting for transfers between devices  19.6 us (4%)
  starting transfers between devices  16.8 us (3%)
  between operations  14.4 us (3%)
    all_gather x2, blocking collectives, joined(): gathered = jax.tree.map(lambda a: lax.all_gather(a, axis), part)  213 us
    dynamic_slice x64, local copies, waits for them, and re-layouts, take(): lax.dynamic_index_in_dim(a, source, 0, False)  69.6 us
    add x63, other arithmetic, combine_states(): weighted_a * factor_a[..., None] + weighted_b * factor_b[..., None]  36.4 us
    all_gather x1, blocking collectives, local(): value_part = lax.all_gather(new_values, 'ctx', axis=0, tiled=True)  34 us
    all_gather x1, blocking collectives, local(): key_part = lax.all_gather(new_keys, 'ctx', axis=0, tiled=True)  32.4 us
    all_to_all x1, waiting for transfers between devices, local(): lax.all_to_all(outgoing, 'ctx', split_axis=1, concat_axis=1, tiled=True)  19.6 us
    all_to_all x1, starting transfers between devices, local(): lax.all_to_all(outgoing, 'ctx', split_axis=1, concat_axis=1, tiled=True)  16.8 us
    dot_general x4, matrix products, attend_keys(): jnp.einsum('tgqn,ngd->tgqd', weights, value_rows, preferred_element_type=...  10.7 us
  transfers between devices with their start and end apart: 2, of which 1 were waited for; matrix products, arithmetic and copies ran while one was open for 7% of the time, Pallas kernels for 0%

commit v1 on v0

v1 whole, which is shorter than its diff:
```python
import jax
import jax.numpy as jnp
import numpy as np
from jax import lax
from jax.experimental import pallas as pl
from jax.experimental.pallas import tpu as pltpu
from jax.sharding import Mesh, PartitionSpec as P

HEAD_SIZE = 128
PAGE_TOKENS = 16
NEG_FILL = -1e30
LOG2_SCALE = HEAD_SIZE**-0.5 * 1.4426950408889634
VMEM = pl.BlockSpec(memory_space=pltpu.VMEM)
SMEM = pl.BlockSpec(memory_space=pltpu.SMEM)
PARAMS = pltpu.CompilerParams(vmem_limit_bytes=48 * 1024 * 1024)


def dot_t(a, b):
    return lax.dot_general(a, b, (((1,), (1,)), ((), ())), preferred_element_type=jnp.float32)


def dot(a, b):
    return jnp.dot(a, b, preferred_element_type=jnp.float32)


def as_rows(column):
    eye = lax.broadcasted_iota(jnp.int32, (128, 128), 0) == lax.broadcasted_iota(
        jnp.int32, (128, 128), 1
    )
    return [
        jnp.sum(jnp.where(eye, column[i : i + 128], 0.0), axis=0, keepdims=True) for i in (0, 128)
    ]


def stat_rows(top, total):
    high = total.astype(jnp.bfloat16).astype(jnp.float32)
    rows = [top, high, total - high, jnp.zeros((10, 128), jnp.float32)]
    return jnp.concatenate(rows, axis=0).astype(jnp.bfloat16)


def partial_kernel(len_ref, where_ref, dq_ref, rk_ref, rv_ref, nk_ref, nv_ref, out_ref):
    groups = out_ref.shape[0]
    res_rows = rk_ref.shape[1]
    heads = dq_ref.shape[1] // HEAD_SIZE
    tokens = nk_ref.shape[0]
    base, grp, half_rows = where_ref[0], where_ref[1], where_ref[2]
    keys = 16 * res_rows
    queries = 16 * heads
    col = lax.broadcasted_iota(jnp.int32, (1, keys), 1)
    col_row = col // res_rows
    col_pos = base + col % res_rows
    same_row = (lax.broadcasted_iota(jnp.int32, (queries, keys), 0) % 16) == (
        lax.broadcasted_iota(jnp.int32, (queries, keys), 1) // res_rows
    )
    token = lax.broadcasted_iota(jnp.int32, (1, tokens), 1) - grp * half_rows
    token_bias = jnp.where((token >= 0) & (token < half_rows), 0.0, NEG_FILL)
    nk = nk_ref[...]
    nv = nv_ref[...]
    for g in range(groups):
        lens = jnp.zeros((1, keys), jnp.int32)
        for r in range(16):
            lens = jnp.where(col_row == r, len_ref[16 * g + r], lens)
        live = jnp.where(col_pos < lens, 0.0, NEG_FILL)
        q = jnp.concatenate(
            [
                dq_ref[16 * g : 16 * g + 16, h * HEAD_SIZE : (h + 1) * HEAD_SIZE]
                for h in range(heads)
            ],
            axis=0,
        )
        rk = rk_ref[16 * g : 16 * g + 16].reshape(keys, HEAD_SIZE)
        rv = rv_ref[16 * g : 16 * g + 16].reshape(keys, HEAD_SIZE)
        s1 = jnp.where(same_row, dot_t(q, rk) * LOG2_SCALE + live, NEG_FILL)
        s2 = dot_t(q, nk) * LOG2_SCALE + token_bias
        top = jnp.maximum(
            jnp.max(s1, axis=1, keepdims=True), jnp.max(s2, axis=1, keepdims=True)
        )
        top = top.astype(jnp.bfloat16).astype(jnp.float32)
        p1 = jnp.exp2(s1 - top).astype(jnp.bfloat16)
        p2 = jnp.exp2(s2 - top).astype(jnp.bfloat16)
        total = jnp.sum(p1.astype(jnp.float32), axis=1, keepdims=True) + jnp.sum(
            p2.astype(jnp.float32), axis=1, keepdims=True
        )
        out_ref[g, :queries] = (dot(p1, rv) + dot(p2, nv)).astype(jnp.bfloat16)
        out_ref[g, queries : queries + 16] = stat_rows(
            jnp.concatenate(as_rows(top), axis=0), jnp.concatenate(as_rows(total), axis=0)
        )


def joined(parts, begin, queries, normal):
    count = parts.shape[0]
    stats = [
        parts[d, begin + queries : begin + queries + 16].astype(jnp.float32) for d in range(count)
    ]
    top = stats[0][0:2]
    for d in range(1, count):
        top = jnp.maximum(top, stats[d][0:2])
    factors = [jnp.exp2(stats[d][0:2] - top) for d in range(count)]
    total = factors[0] * (stats[0][2:4] + stats[0][4:6])
    for d in range(1, count):
        total = total + factors[d] * (stats[d][2:4] + stats[d][4:6])
    if normal:
        factors = [f / total for f in factors]
    columns = jnp.concatenate(factors, axis=0).T
    halves = []
    for half in range(2):
        rows = slice(begin + 128 * half, begin + 128 * half + 128)
        acc = jnp.zeros((128, HEAD_SIZE), jnp.float32)
        for d in range(count):
            acc = acc + parts[d, rows].astype(jnp.float32) * columns[:, 2 * d + half : 2 * d + half + 1]
        halves.append(acc)
    return halves, top, total


def pack_kernel(part_ref, nk_ref, nv_ref, out_ref):
    tokens = nk_ref.shape[0]
    queries = part_ref.shape[1] - 16
    halves, top, total = joined(part_ref, 0, queries, False)
    begin = 2 * tokens
    out_ref[:tokens] = nk_ref[...]
    out_ref[tokens:begin] = nv_ref[...]
    for half in range(2):
        out_ref[begin + 128 * half : begin + 128 * half + 128] = halves[half].astype(jnp.bfloat16)
    out_ref[begin + queries : begin + queries + 16] = stat_rows(top, total)


def decoded_kernel(tokens, all_ref, kv_ref, dec_ref):
    count = all_ref.shape[0]
    begin = 2 * tokens
    queries = all_ref.shape[1] - begin - 16
    for d in range(count):
        kv_ref[d * begin : (d + 1) * begin] = all_ref[d, :begin]
    halves, _, _ = joined(all_ref, begin, queries, True)
    for half in range(2):
        value = halves[half].astype(jnp.bfloat16)
        dec_ref[128 * half : 128 * half + 128] = value
        kv_ref[count * begin + 128 * half : count * begin + 128 * half + 128] = value


def prefill_kernel(
    where_ref, page_ref, q_ref, own_ref, peer_ref, out_ref, pk_ref, pv_ref, qs, acc, top
):
    ctx, core, bound = where_ref[0], where_ref[1], where_ref[2]
    tokens = q_ref.shape[0]
    heads = q_ref.shape[1] // HEAD_SIZE
    blocks_per = 2
    block = 2 * blocks_per * tokens
    row_block = 2 * tokens
    for s in range(pk_ref.shape[0]):
        source = page_ref[s] // (tokens // PAGE_TOKENS)
        row = pl.multiple_of(
            (source // 2) * (2 * tokens)
            + (page_ref[s] - source * (tokens // PAGE_TOKENS)) * PAGE_TOKENS,
            PAGE_TOKENS,
        )
        value_row = pl.multiple_of(row + tokens, PAGE_TOKENS)
        is_own = source % 2 == core

        @pl.when(is_own)
        def _():
            pk_ref[s] = own_ref[pl.ds(row, PAGE_TOKENS), :]
            pv_ref[s] = own_ref[pl.ds(value_row, PAGE_TOKENS), :]

        @pl.when(jnp.logical_not(is_own))
        def _():
            pk_ref[s] = peer_ref[pl.ds(row, PAGE_TOKENS), :]
            pv_ref[s] = peer_ref[pl.ds(value_row, PAGE_TOKENS), :]

    for h in range(heads):
        qs[h * tokens : (h + 1) * tokens] = q_ref[:, h * HEAD_SIZE : (h + 1) * HEAD_SIZE]
    acc[...] = jnp.zeros_like(acc)
    top[...] = jnp.full_like(top, NEG_FILL)
    first = ctx * tokens
    q_pos = first + lax.broadcasted_iota(jnp.int32, (row_block, 1), 0) % tokens
    begin = jnp.where(q_pos < bound, 0, bound)
    col = lax.broadcasted_iota(jnp.int32, (1, block), 1)
    piece = col // tokens
    side = jnp.where(piece < blocks_per, core, 1 - core)
    key_pos0 = (2 * (piece % blocks_per) + side) * tokens + col % tokens
    ones = jnp.ones((block, HEAD_SIZE), jnp.bfloat16)
    lowest = jnp.where(first < bound, 0, bound) // block
    highest = first // block + 1

    def one(step, carry):
        rows = [
            pl.multiple_of((step * blocks_per + i) * 2 * tokens, PAGE_TOKENS)
            for i in range(blocks_per)
        ]
        k = jnp.concatenate(
            [ref[pl.ds(r, tokens), :] for ref in (own_ref, peer_ref) for r in rows], axis=0
        )
        v = jnp.concatenate(
            [
                ref[pl.ds(pl.multiple_of(r + tokens, PAGE_TOKENS), tokens), :]
                for ref in (own_ref, peer_ref)
                for r in rows
            ],
            axis=0,
        )
        v = jnp.concatenate([v, ones], axis=1)
        key_pos = key_pos0 + step * block
        bias = jnp.where((key_pos <= q_pos) & (key_pos >= begin), 0.0, NEG_FILL)
        for b in range(heads * tokens // row_block):
            rows_b = slice(b * row_block, (b + 1) * row_block)
            s = dot_t(qs[rows_b], k) * LOG2_SCALE + bias
            before = top[rows_b]
            after = jnp.maximum(before, jnp.max(s, axis=1, keepdims=True))
            p = jnp.exp2(s - after).astype(jnp.bfloat16)
            acc[rows_b] = acc[rows_b] * jnp.exp2(before - after) + dot(p, v)
            top[rows_b] = after
        return carry

    lax.fori_loop(lowest, highest, one, 0)
    for h in range(heads):
        rows_h = slice(h * tokens, (h + 1) * tokens)
        out_ref[:, h * HEAD_SIZE : (h + 1) * HEAD_SIZE] = (
            acc[rows_h, :HEAD_SIZE] / acc[rows_h, HEAD_SIZE:]
        ).astype(jnp.bfloat16)


def place_kernel(where_ref, own_ref, core_ref, grp_ref, both_ref, out_ref):
    me = where_ref[3]
    for flip, ref in ((0, own_ref), (2, core_ref), (1, grp_ref), (3, both_ref)):
        target = me + flip - 2 * (me & flip)
        row = pl.multiple_of(target * 16, 16)
        begin = ref.shape[0] - 16 * (out_ref.shape[1] // HEAD_SIZE)
        for h in range(out_ref.shape[1] // HEAD_SIZE):
            out_ref[pl.ds(row, 16), h * HEAD_SIZE : (h + 1) * HEAD_SIZE] = ref[
                begin + 16 * h : begin + 16 * h + 16
            ]


def local(
    new_queries,
    new_keys,
    new_values,
    segment_ids,
    page_table,
    decode_query_rows,
    resident_keys,
    resident_values,
    res_len,
):
    bf = jnp.bfloat16
    tokens = new_keys.shape[0]
    ring = lax.axis_size("z")
    z, core, grp = (lax.axis_index(a) for a in ("z", "core", "grp"))
    ctx = z * 2 + core
    rows, width = decode_query_rows.shape
    queries = 16 * (width // HEAD_SIZE)
    res_rows = resident_keys.shape[1]
    pages = tokens // PAGE_TOKENS
    i32 = jnp.int32

    where_a = jnp.stack([(ctx * 2 + grp) * res_rows, grp, jnp.int32(tokens // 2)]).astype(i32)
    part = pl.pallas_call(
        partial_kernel,
        out_shape=jax.ShapeDtypeStruct((rows // 16, queries + 16, HEAD_SIZE), bf),
        in_specs=[SMEM, SMEM] + [VMEM] * 5,
        out_specs=VMEM,
        compiler_params=PARAMS,
    )(res_len, where_a, decode_query_rows, resident_keys, resident_values, new_keys, new_values)
    part = lax.all_to_all(part, ("core", "grp"), 0, 0, tiled=True)

    packed = pl.pallas_call(
        pack_kernel,
        out_shape=jax.ShapeDtypeStruct((2 * tokens + queries + 16, HEAD_SIZE), bf),
        in_specs=[VMEM] * 3,
        out_specs=VMEM,
        compiler_params=PARAMS,
    )(part, new_keys, new_values)
    gathered = lax.all_gather(packed, "z", axis=0)

    kv, dec = pl.pallas_call(
        lambda *refs: decoded_kernel(tokens, *refs),
        out_shape=(
            jax.ShapeDtypeStruct((ring * 2 * tokens + queries, HEAD_SIZE), bf),
            jax.ShapeDtypeStruct((queries, HEAD_SIZE), bf),
        ),
        in_specs=[VMEM],
        out_specs=(VMEM, VMEM),
        compiler_params=PARAMS,
    )(gathered)
    swap = [(0, 1), (1, 0)]
    peer_kv = lax.ppermute(kv, "core", swap)
    grp_dec = lax.ppermute(dec, "grp", swap)
    both_dec = lax.ppermute(grp_dec, "core", swap)

    bound = jnp.sum((segment_ids == 0).astype(i32))
    slots = ctx * pages + jnp.arange(pages, dtype=i32)
    ids = jnp.arange(page_table.shape[0], dtype=i32)
    page_from = jnp.sum(jnp.where(page_table[None, :] == slots[:, None], ids[None, :], 0), axis=1)
    where_b = jnp.stack([ctx, core, bound, core * 2 + grp]).astype(i32)
    prefill_out, paged_keys, paged_values = pl.pallas_call(
        prefill_kernel,
        out_shape=(
            jax.ShapeDtypeStruct(new_queries.shape, bf),
            jax.ShapeDtypeStruct((pages, PAGE_TOKENS, HEAD_SIZE), bf),
            jax.ShapeDtypeStruct((pages, PAGE_TOKENS, HEAD_SIZE), bf),
        ),
        in_specs=[SMEM, SMEM] + [VMEM] * 3,
        out_specs=(VMEM,) * 3,
        scratch_shapes=[
            pltpu.VMEM((tokens * (new_queries.shape[1] // HEAD_SIZE), HEAD_SIZE), bf),
            pltpu.VMEM(
                (tokens * (new_queries.shape[1] // HEAD_SIZE), 2 * HEAD_SIZE), jnp.float32
            ),
            pltpu.VMEM((tokens * (new_queries.shape[1] // HEAD_SIZE), 1), jnp.float32),
        ],
        compiler_params=PARAMS,
    )(where_b, page_from, new_queries, kv, peer_kv)

    decode_out = pl.pallas_call(
        place_kernel,
        out_shape=jax.ShapeDtypeStruct((rows, width), bf),
        in_specs=[SMEM] + [VMEM] * 4,
        out_specs=VMEM,
        compiler_params=PARAMS,
    )(where_b, dec, peer_kv, grp_dec, both_dec)
    return (prefill_out, paged_keys, paged_values, decode_out)


def solution(mesh):
    sizes = mesh.shape
    fine = Mesh(
        np.asarray(mesh.devices).reshape(sizes["ctx"] // 2, 2, sizes["head"], sizes["grp"]),
        ("z", "core", "head", "grp"),
    )
    ctx = ("z", "core")
    return jax.shard_map(
        local,
        mesh=fine,
        in_specs=(
            P(ctx, ("head", "grp")),
            P(ctx, "head"),
            P(ctx, "head"),
            P(),
            P(),
            P(None, "head"),
            P(None, ("z", "core", "grp"), "head"),
            P(None, ("z", "core", "grp"), "head"),
            P(),
        ),
        out_specs=(
            P(ctx, ("head", "grp")),
            P(ctx, None, "head"),
            P(ctx, None, "head"),
            P(None, "head"),
        ),
        check_vma=False,
    )
```

time: 507 us -> 129 us (0.25)
  blocking collectives: 280 us -> 15 us
  local copies, waits for them, and re-layouts: 96.9 us -> 6.7 us
  other arithmetic: 51 us -> 1.62 us
  waiting for transfers between devices: 19.6 us -> 65.1 us
  matrix products: 20.1 us -> 0 us
  Pallas kernels: 0 us -> 8.29 us
    all_gather x4 -> x0, blocking collectives: 280 us -> none  [the longest x2 213 us: joined(): gathered = jax.tree.map(lambda a: lax.all_gather(a, axis), part)]
    dynamic_slice x69 -> x0, local copies, waits for them, and re-layouts: 74.1 us -> none  [the longest x64 69.6 us: take(): lax.dynamic_index_in_dim(a, source, 0, False)]
    all_gather x1, waiting for transfers between devices: 0.01 us -> 63 us  [local(): gathered = lax.all_gather(packed, 'z', axis=0)]
    add x77 -> x1, other arithmetic: 36.7 us -> 0.01 us  [local(): slots = ctx * pages + jnp.arange(pages, dtype=i32)]
    dot_general x14 -> x0, matrix products: 20.1 us -> none  [the longest x4 10.7 us: attend_keys(): jnp.einsum('tgqn,ngd->tgqd', weights, value_rows, preferred_element_type=...]
    all_to_all x1 -> x0, waiting for transfers between devices: 19.6 us -> none  [local(): lax.all_to_all(outgoing, 'ctx', split_axis=1, concat_axis=1, tiled=True)]
    ppermute x0 -> x3, starting transfers between devices: none -> 17.4 us  [the longest x1 11.6 us: local(): peer_kv = lax.ppermute(kv, 'core', swap)]
    all_to_all x1 -> x0, starting transfers between devices: 16.8 us -> none  [local(): lax.all_to_all(outgoing, 'ctx', split_axis=1, concat_axis=1, tiled=True)]
  transfers between devices with their start and end apart: 2 -> 4, of which waited for: 1 -> 3; matrix products, arithmetic and copies ran while one was open for 7% -> 1% of each run, Pallas kernels for 0% -> 0%
where the time goes in v1:
time: 129 us; the launch traced here: 128 us
  waiting for transfers between devices  65.1 us (50%)
  starting transfers between devices  17.4 us (13%)
  blocking collectives  15 us (12%)
  between operations  14.1 us (11%)
  Pallas kernels  8.29 us (6%)
  local copies, waits for them, and re-layouts  6.7 us (5%)
  other arithmetic  1.62 us (1%)
    all_gather x1, waiting for transfers between devices, local(): gathered = lax.all_gather(packed, 'z', axis=0)  63 us
    all_to_all x1, blocking collectives, local(): part = lax.all_to_all(part, ('core', 'grp'), 0, 0, tiled=True)  15 us
    ppermute x1, starting transfers between devices, local(): peer_kv = lax.ppermute(kv, 'core', swap)  11.6 us
    unnamed x20, local copies, waits for them, and re-layouts  6.7 us
    ppermute x1, starting transfers between devices, local(): grp_dec = lax.ppermute(dec, 'grp', swap)  3.09 us
    pallas_call x1, Pallas kernels, local(): pl.pallas_call(prefill_kernel, out_shape=(jax.ShapeDtypeStruct(new_querie...  2.82 us
    ppermute x1, starting transfers between devices, local(): both_dec = lax.ppermute(grp_dec, 'core', swap)  2.69 us
  transfers between devices with their start and end apart: 4, of which 3 were waited for; matrix products, arithmetic and copies ran while one was open for 1% of the time, Pallas kernels for 0%

profile of v1, /device:TPU:1, one launch (start us, length us, event | category | flops | bytes accessed | tf_op | source)
XLA Modules:
  0.0 128.2 jit_solution(12395233726027095644)
XLA Ops:
  7.2 0.0 all-gather.3.cloned.1.call-start
  7.2 0.1 pad_add_fusion.1.where_ref
  7.3 0.0 copy-start.1
  7.3 1.0 copy-done.1
  8.3 0.0 copy-start.2
  8.3 1.0 copy-done.2
  9.4 0.0 copy-start.3
  9.4 0.9 copy-done.3
  10.3 0.0 copy-start.5
  10.3 0.7 copy-done.5
  11.1 0.0 copy-start.6
  11.1 0.7 copy-done.6
  11.8 0.0 copy-start.7
  11.8 0.7 copy-done.7
  12.5 2.3 %shard_map.120 = bf16[4,272,128]{2,1,0:T(8,128)(2,1)S(1)} custom-call(s32[64]{0:T(128)S(1)} %copy-done.7, s32[3]{0:T(128)S(1)} %pad_add_fusion.1.where_ref, bf16[64,2048]{1,0:T(8,128)(2,1)S(1)} %copy-done.3, bf16[64,32,128]{2,1,0:T(8,128)(2,1)S(1)} %copy-done.1, bf16[64,32,128]{2,1,0:T(8,128)(2,1)S(1)} %copy-done.2, bf16[96,128]{1,0:T(8,128)(2,1)S(1)} %copy-done.5, ...), custom_call_target="tpu_custom_call" | custom-call | tf_op jit(solution)/shard_map/pallas_call | solution.py:256
  14.7 0.0 copy-start.9
  14.7 0.0 copy-start.8
  14.8 15.0 %all_to_all.5.part_ref = bf16[4,272,128]{2,1,0:T(8,128)(2,1)S(1)} all-to-all(bf16[4,272,128]{2,1,0:T(8,128)(2,1)S(1)} %shard_map.120), channel_id=1, replica_groups=mesh['z'=16,'core'=2,'head'=8,'grp'=2] {'core','grp'}, dimensions={0} | all-to-all | bytes 557056 | tf_op jit(solution)/shard_map/all_to_all | solution.py:263
  29.7 0.0 copy-start.4
  29.7 1.0 shard_map.121
  30.7 0.0 all-gather.3.cloned.1.call-update
  30.7 63.0 %all-gather.3.cloned.1.call-done = bf16[7424,128]{1,0:T(8,128)(2,1)} async-done(((bf16[464,128]{1,0:T(8,128)(2,1)}), bf16[7424,128]{1,0:T(8,128)(2,1)}) %all-gather.3.cloned.1.call-update) | async-done | bytes 1900560 | tf_op jit(solution)/shard_map/all_gather | solution.py:272
  93.8 0.0 copy-start
  93.8 1.5 %copy-done = bf16[7424,128]{1,0:T(8,128)(2,1)S(1)} copy-done((bf16[7424,128]{1,0:T(8,128)(2,1)S(1)}, bf16[7424,128]{1,0:T(8,128)(2,1)}, u32[]{:S(2)}) %copy-start) | copy-done | bytes 1900568
  95.3 0.9 shard_map.122
  96.2 11.6 %collective-permute-start = (bf16[3328,128]{1,0:T(8,128)(2,1)S(1)}, bf16[3328,128]{1,0:T(8,128)(2,1)S(1)}, u32[]{:S(2)}, u32[]{:S(2)}) collective-permute-start(bf16[3328,128]{1,0:T(8,128)(2,1)S(1)} %get-tuple-element.9.own_ref), channel_id=1, source_target_pairs={{0,16},{16,0},{1,17},{17,1},{2,18},{18,2},{3,19},{19,3},{4,20},{20... | collective-permute-start | bytes 2555912 | tf_op jit(solution)/shard_map/ppermute | solution.py:285
  107.8 0.0 copy-done.9
  107.8 0.2 select_reduce_fusion.page_ref
  108.0 3.1 %collective-permute-start.1 = (bf16[256,128]{1,0:T(8,128)(2,1)S(1)}, bf16[256,128]{1,0:T(8,128)(2,1)S(1)}, u32[]{:S(2)}, u32[]{:S(2)}) collective-permute-start(bf16[256,128]{1,0:T(8,128)(2,1)S(1)} %get-tuple-element.13.own_ref), channel_id=1, source_target_pairs={{0,1},{1,0},{2,3},{3,2},{4,5},{5,4},{6,7},{7,6},{8,9},{9,8},{10,11... | collective-permute-start | bytes 196616 | tf_op jit(solution)/shard_map/ppermute | solution.py:286
  111.1 0.0 copy-done.8
  111.1 0.6 convert_reduce_fusion
  111.8 1.9 %collective-permute-done.1.grp_ref = bf16[256,128]{1,0:T(8,128)(2,1)S(1)} collective-permute-done((bf16[256,128]{1,0:T(8,128)(2,1)S(1)}, bf16[256,128]{1,0:T(8,128)(2,1)S(1)}, u32[]{:S(2)}, u32[]{:S(2)}) %collective-permute-start.1) | collective-permute-done | bytes 65568 | tf_op jit(solution)/shard_map/ppermute | solution.py:286
  113.6 2.7 %collective-permute-start.2 = (bf16[256,128]{1,0:T(8,128)(2,1)S(1)}, bf16[256,128]{1,0:T(8,128)(2,1)S(1)}, u32[]{:S(2)}, u32[]{:S(2)}) collective-permute-start(bf16[256,128]{1,0:T(8,128)(2,1)S(1)} %collective-permute-done.1.grp_ref), channel_id=1, source_target_pairs={{0,16},{16,0},{1,17},{17,1},{2,18},{18,2},{3,19},{19,3},{4,20},{20... | collective-permute-start | bytes 196616 | tf_op jit(solution)/shard_map/ppermute | solution.py:287
  116.3 0.7 pad_add_fusion.where_ref
  117.1 0.2 collective-permute-done.2.both_ref
  117.2 0.0 collective-permute-done.peer_ref.core_ref
  117.2 1.3 %shard_map.124 = bf16[64,2048]{1,0:T(8,128)(2,1)} custom-call(s32[4]{0:T(128)S(1)} %pad_add_fusion.where_ref, bf16[256,128]{1,0:T(8,128)(2,1)S(1)} %get-tuple-element.13.own_ref, bf16[3328,128]{1,0:T(8,128)(2,1)S(1)} %collective-permute-done.peer_ref.core_ref, bf16[256,128]{1,0:T(8,128)(2,1)S(1)} %collective-permute-done.1.grp_ref, ...), custom_call_target="tpu_custom_call" | custom-call | tf_op jit(solution)/shard_map/pallas_call | solution.py:313
  118.5 0.0 copy-done.4
  118.5 2.8 %shard_map.123 = (bf16[96,1024]{1,0:T(8,128)(2,1)}, bf16[6,16,128]{2,1,0:T(8,128)(2,1)}, bf16[6,16,128]{2,1,0:T(8,128)(2,1)}) custom-call(s32[4]{0:T(128)S(1)} %pad_add_fusion.where_ref, s32[6]{0:T(128)S(1)} %select_reduce_fusion.page_ref, bf16[96,1024]{1,0:T(8,128)(2,1)S(1)} %copy-done.4, bf16[3328,128]{1,0:T(8,128)(2,1)S(1)} %get-tuple-element.9.own_ref, ...), custom_call_target="tpu_custom_call" | custom-call | tf_op jit(solution)/shard_map/pallas_call | solution.py:294
  (1 shorter events, 0.0 us)
Async XLA Ops:
  7.2 86.6 %all-gather.3.cloned.1.call-start = ((), (), s32[]{:S(2)}) async-start(), calls=%async_computation.1 | async-start | bytes 2019328 | tf_op jit(solution)/shard_map/all_gather | solution.py:272
  7.3 1.0 copy-start.1
  8.3 1.0 copy-start.2
  9.4 0.9 copy-start.3
  10.3 0.7 copy-start.5
  11.1 0.7 copy-start.6
  11.8 0.7 copy-start.7
  14.7 93.1 %copy-start.9 = (s32[192]{0:T(256)S(1)}, s32[192]{0:T(256)}, u32[]{:S(2)}) copy-start(s32[192]{0:T(256)} %param.13) | copy-start | bytes 2308
  14.7 96.4 %copy-start.8 = (s32[3072]{0:T(1024)S(1)}, s32[3072]{0:T(1024)}, u32[]{:S(2)}) copy-start(s32[3072]{0:T(1024)} %param.12) | copy-start | bytes 36868
  29.7 88.8 %copy-start.4 = (bf16[96,1024]{1,0:T(8,128)(2,1)S(1)}, bf16[96,1024]{1,0:T(8,128)(2,1)}, u32[]{:S(2)}) copy-start(bf16[96,1024]{1,0:T(8,128)(2,1)} %q_ref.1) | copy-start | bytes 589828
  93.8 1.5 %copy-start = (bf16[7424,128]{1,0:T(8,128)(2,1)S(1)}, bf16[7424,128]{1,0:T(8,128)(2,1)}, u32[]{:S(2)}) copy-start(bf16[7424,128]{1,0:T(8,128)(2,1)} %all-gather.3.cloned.1.call-done) | copy-start | bytes 5701636
  96.2 21.0 %collective-permute-start = (bf16[3328,128]{1,0:T(8,128)(2,1)S(1)}, bf16[3328,128]{1,0:T(8,128)(2,1)S(1)}, u32[]{:S(2)}, u32[]{:S(2)}) collective-permute-start(bf16[3328,128]{1,0:T(8,128)(2,1)S(1)} %get-tuple-element.9.own_ref), channel_id=1, source_target_pairs={{0,16},{16,0},{1,17},{17,1},{2,18},{18,2},{3,19},{19,3},{4,20},{20... | collective-permute-start | bytes 2555912 | tf_op jit(solution)/shard_map/ppermute | solution.py:285
  108.0 5.6 %collective-permute-start.1 = (bf16[256,128]{1,0:T(8,128)(2,1)S(1)}, bf16[256,128]{1,0:T(8,128)(2,1)S(1)}, u32[]{:S(2)}, u32[]{:S(2)}) collective-permute-start(bf16[256,128]{1,0:T(8,128)(2,1)S(1)} %get-tuple-element.13.own_ref), channel_id=1, source_target_pairs={{0,1},{1,0},{2,3},{3,2},{4,5},{5,4},{6,7},{7,6},{8,9},{9,8},{10,11... | collective-permute-start | bytes 196616 | tf_op jit(solution)/shard_map/ppermute | solution.py:286
  113.6 3.6 %collective-permute-start.2 = (bf16[256,128]{1,0:T(8,128)(2,1)S(1)}, bf16[256,128]{1,0:T(8,128)(2,1)S(1)}, u32[]{:S(2)}, u32[]{:S(2)}) collective-permute-start(bf16[256,128]{1,0:T(8,128)(2,1)S(1)} %collective-permute-done.1.grp_ref), channel_id=1, source_target_pairs={{0,16},{16,0},{1,17},{17,1},{2,18},{18,2},{3,19},{19,3},{4,20},{20... | collective-permute-start | bytes 196616 | tf_op jit(solution)/shard_map/ppermute | solution.py:287
Sparse Core Ops, SparseCore 0:
  30.9 62.8 all-gather.2

commit v2 on v1

v2 whole, which is shorter than its diff:
```python
import jax
import jax.numpy as jnp
import numpy as np
from jax import lax
from jax.experimental import pallas as pl
from jax.experimental.pallas import tpu as pltpu
from jax.sharding import Mesh, PartitionSpec as P

HEAD_SIZE = 128
PAGE_TOKENS = 16
NEG_FILL = -1e30
LOG2_SCALE = HEAD_SIZE**-0.5 * 1.4426950408889634
VMEM = pl.BlockSpec(memory_space=pltpu.VMEM)
SMEM = pl.BlockSpec(memory_space=pltpu.SMEM)
PARAMS = pltpu.CompilerParams(vmem_limit_bytes=48 * 1024 * 1024)


def dot_t(a, b):
    return lax.dot_general(a, b, (((1,), (1,)), ((), ())), preferred_element_type=jnp.float32)


def dot(a, b):
    return jnp.dot(a, b, preferred_element_type=jnp.float32)


def as_rows(column):
    eye = lax.broadcasted_iota(jnp.int32, (128, 128), 0) == lax.broadcasted_iota(
        jnp.int32, (128, 128), 1
    )
    return [
        jnp.sum(jnp.where(eye, column[i : i + 128], 0.0), axis=0, keepdims=True) for i in (0, 128)
    ]


def partial_kernel(len_ref, where_ref, dq_ref, rk_ref, rv_ref, nk_ref, nv_ref, out_ref):
    g = pl.program_id(0)
    res_rows = rk_ref.shape[1]
    heads = dq_ref.shape[1] // HEAD_SIZE
    tokens = nk_ref.shape[0]
    base, grp, half_rows = where_ref[0], where_ref[1], where_ref[2]
    keys = 16 * res_rows
    queries = 16 * heads
    col = lax.broadcasted_iota(jnp.int32, (1, keys), 1)
    col_row = col // res_rows
    col_pos = base + col % res_rows
    same_row = (lax.broadcasted_iota(jnp.int32, (queries, keys), 0) % 16) == (
        lax.broadcasted_iota(jnp.int32, (queries, keys), 1) // res_rows
    )
    token = lax.broadcasted_iota(jnp.int32, (1, tokens), 1) - grp * half_rows
    token_bias = jnp.where((token >= 0) & (token < half_rows), 0.0, NEG_FILL)
    lens = jnp.zeros((1, keys), jnp.int32)
    for r in range(16):
        lens = jnp.where(col_row == r, len_ref[16 * g + r], lens)
    live = jnp.where(col_pos < lens, 0.0, NEG_FILL)
    q = jnp.concatenate(
        [dq_ref[:, h * HEAD_SIZE : (h + 1) * HEAD_SIZE] for h in range(heads)], axis=0
    )
    rk = rk_ref[...].reshape(keys, HEAD_SIZE)
    rv = rv_ref[...].reshape(keys, HEAD_SIZE)
    s1 = jnp.where(same_row, dot_t(q, rk) * LOG2_SCALE + live, NEG_FILL)
    s2 = dot_t(q, nk_ref[...]) * LOG2_SCALE + token_bias
    top = jnp.maximum(jnp.max(s1, axis=1, keepdims=True), jnp.max(s2, axis=1, keepdims=True))
    top = top.astype(jnp.bfloat16).astype(jnp.float32)
    p1 = jnp.exp2(s1 - top).astype(jnp.bfloat16)
    p2 = jnp.exp2(s2 - top).astype(jnp.bfloat16)
    total = jnp.sum(p1.astype(jnp.float32), axis=1, keepdims=True) + jnp.sum(
        p2.astype(jnp.float32), axis=1, keepdims=True
    )
    out_ref[0, :queries] = (dot(p1, rv) + dot(p2, nv_ref[...])).astype(jnp.bfloat16)
    high = total.astype(jnp.bfloat16).astype(jnp.float32)
    stats = as_rows(top) + as_rows(high) + as_rows(total - high)
    stats = jnp.concatenate(stats + [jnp.zeros((10, 128), jnp.float32)], axis=0)
    out_ref[0, queries : queries + 16] = stats.astype(jnp.bfloat16)


def pack_kernel(part_ref, out_ref):
    count = part_ref.shape[0]
    queries = part_ref.shape[1] - 16
    ring, rows = out_ref.shape[0], out_ref.shape[1] // 2
    stats = [part_ref[d, queries : queries + 16].astype(jnp.float32) for d in range(count)]
    top = stats[0][0:2]
    for d in range(1, count):
        top = jnp.maximum(top, stats[d][0:2])
    factors = [jnp.exp2(stats[d][0:2] - top) for d in range(count)]
    total = factors[0] * (stats[0][2:4] + stats[0][4:6])
    for d in range(1, count):
        total = total + factors[d] * (stats[d][2:4] + stats[d][4:6])
    high = total.astype(jnp.bfloat16).astype(jnp.float32)
    columns = factors + [top, high, total - high, jnp.zeros((2, 128), jnp.float32)]
    columns = jnp.concatenate(columns, axis=0).T
    lane = lax.broadcasted_iota(jnp.int32, (128, 128), 1)
    for half in range(2):
        acc = jnp.zeros((128, HEAD_SIZE), jnp.float32)
        for d in range(count):
            part = part_ref[d, 128 * half : 128 * half + 128].astype(jnp.float32)
            acc = acc + part * columns[:, 2 * d + half : 2 * d + half + 1]
        side = jnp.zeros((128, 128), jnp.float32)
        for i in range(3):
            at = 2 * (count + i) + half
            side = jnp.where(lane == i, columns[:, at : at + 1], side)
        out_ref[half * ring // 2 : (half + 1) * ring // 2, :rows] = acc.astype(
            jnp.bfloat16
        ).reshape(ring // 2, rows, HEAD_SIZE)
        out_ref[half * ring // 2 : (half + 1) * ring // 2, rows:] = side.astype(
            jnp.bfloat16
        ).reshape(ring // 2, rows, HEAD_SIZE)


def finish_kernel(part_ref, nk_ref, nv_ref, out_ref):
    tokens = nk_ref.shape[0]
    count = part_ref.shape[0]
    rows = part_ref.shape[1] // 2
    stats = [part_ref[d, rows:].astype(jnp.float32) for d in range(count)]
    top = stats[0][:, 0:1]
    for d in range(1, count):
        top = jnp.maximum(top, stats[d][:, 0:1])
    total = jnp.zeros((rows, 1), jnp.float32)
    acc = jnp.zeros((rows, HEAD_SIZE), jnp.float32)
    for d in range(count):
        factor = jnp.exp2(stats[d][:, 0:1] - top)
        total = total + factor * (stats[d][:, 1:2] + stats[d][:, 2:3])
        acc = acc + factor * part_ref[d, :rows].astype(jnp.float32)
    out_ref[:tokens] = nk_ref[...]
    out_ref[tokens : 2 * tokens] = nv_ref[...]
    out_ref[2 * tokens :] = (acc / total).astype(jnp.bfloat16)


def spread_kernel(tokens, all_ref, out_ref):
    rows = all_ref.shape[1] - 2 * tokens
    for d in range(out_ref.shape[0]):
        for i in range(all_ref.shape[0]):
            out_ref[d, rows * i : rows * (i + 1)] = all_ref[i, 2 * tokens :]


def prefill_kernel(
    where_ref, page_ref, q_ref, own_ref, peer_ref, out_ref, pk_ref, pv_ref, qs, acc, top
):
    ctx, core, bound = where_ref[0], where_ref[1], where_ref[2]
    tokens = q_ref.shape[0]
    heads = q_ref.shape[1] // HEAD_SIZE
    blocks_per = 2
    block = 2 * blocks_per * tokens
    row_block = 2 * tokens
    for s in range(pk_ref.shape[0]):
        source = page_ref[s] // (tokens // PAGE_TOKENS)
        z = source // 2
        row = (page_ref[s] - source * (tokens // PAGE_TOKENS)) * PAGE_TOKENS
        row = pl.multiple_of(row, PAGE_TOKENS)
        value_row = pl.multiple_of(row + tokens, PAGE_TOKENS)
        is_own = source % 2 == core

        @pl.when(is_own)
        def _():
            pk_ref[s] = own_ref[z, pl.ds(row, PAGE_TOKENS), :]
            pv_ref[s] = own_ref[z, pl.ds(value_row, PAGE_TOKENS), :]

        @pl.when(jnp.logical_not(is_own))
        def _():
            pk_ref[s] = peer_ref[z, pl.ds(row, PAGE_TOKENS), :]
            pv_ref[s] = peer_ref[z, pl.ds(value_row, PAGE_TOKENS), :]

    for h in range(heads):
        qs[h * tokens : (h + 1) * tokens] = q_ref[:, h * HEAD_SIZE : (h + 1) * HEAD_SIZE]
    acc[...] = jnp.zeros_like(acc)
    top[...] = jnp.full_like(top, NEG_FILL)
    first = ctx * tokens
    q_pos = first + lax.broadcasted_iota(jnp.int32, (row_block, 1), 0) % tokens
    begin = jnp.where(q_pos < bound, 0, bound)
    col = lax.broadcasted_iota(jnp.int32, (1, block), 1)
    piece = col // tokens
    side = jnp.where(piece < blocks_per, core, 1 - core)
    key_pos0 = (2 * (piece % blocks_per) + side) * tokens + col % tokens
    ones = jnp.ones((block, HEAD_SIZE), jnp.bfloat16)
    lowest = jnp.where(first < bound, 0, bound) // block
    highest = first // block + 1

    def one(step, carry):
        pairs = [(ref, step * blocks_per + i) for ref in (own_ref, peer_ref) for i in range(blocks_per)]
        k = jnp.concatenate([ref[z, :tokens] for ref, z in pairs], axis=0)
        v = jnp.concatenate([ref[z, tokens : 2 * tokens] for ref, z in pairs], axis=0)
        v = jnp.concatenate([v, ones], axis=1)
        key_pos = key_pos0 + step * block
        bias = jnp.where((key_pos <= q_pos) & (key_pos >= begin), 0.0, NEG_FILL)
        for b in range(heads * tokens // row_block):
            rows_b = slice(b * row_block, (b + 1) * row_block)
            s = dot_t(qs[rows_b], k) * LOG2_SCALE + bias
            before = top[rows_b]
            after = jnp.maximum(before, jnp.max(s, axis=1, keepdims=True))
            p = jnp.exp2(s - after).astype(jnp.bfloat16)
            acc[rows_b] = acc[rows_b] * jnp.exp2(before - after) + dot(p, v)
            top[rows_b] = after
        return carry

    lax.fori_loop(lowest, highest, one, 0)
    for h in range(heads):
        rows_h = slice(h * tokens, (h + 1) * tokens)
        out_ref[:, h * HEAD_SIZE : (h + 1) * HEAD_SIZE] = (
            acc[rows_h, :HEAD_SIZE] / acc[rows_h, HEAD_SIZE:]
        ).astype(jnp.bfloat16)


def place_kernel(in_ref, out_ref):
    for g in range(in_ref.shape[0]):
        for h in range(out_ref.shape[1] // HEAD_SIZE):
            out_ref[16 * g : 16 * g + 16, h * HEAD_SIZE : (h + 1) * HEAD_SIZE] = in_ref[
                g, 16 * h : 16 * h + 16
            ]


def local(
    new_queries,
    new_keys,
    new_values,
    segment_ids,
    page_table,
    decode_query_rows,
    resident_keys,
    resident_values,
    res_len,
):
    bf = jnp.bfloat16
    tokens = new_keys.shape[0]
    ring = lax.axis_size("z")
    z, core, grp = (lax.axis_index(a) for a in ("z", "core", "grp"))
    ctx = z * 2 + core
    rows, width = decode_query_rows.shape
    queries = 16 * (width // HEAD_SIZE)
    res_rows = resident_keys.shape[1]
    pages = tokens // PAGE_TOKENS
    i32 = jnp.int32

    where_a = jnp.stack([(ctx * 2 + grp) * res_rows, grp, jnp.int32(tokens // 2)]).astype(i32)
    groups = rows // 16
    resident = pl.BlockSpec((16, res_rows, HEAD_SIZE), lambda g: (g, 0, 0))
    whole = pl.BlockSpec((tokens, HEAD_SIZE), lambda g: (0, 0))
    part = pl.pallas_call(
        partial_kernel,
        grid=(groups,),
        out_shape=jax.ShapeDtypeStruct((groups, queries + 16, HEAD_SIZE), bf),
        in_specs=[SMEM, SMEM, pl.BlockSpec((16, width), lambda g: (g, 0))]
        + [resident] * 2
        + [whole] * 2,
        out_specs=pl.BlockSpec((1, queries + 16, HEAD_SIZE), lambda g: (g, 0, 0)),
        compiler_params=PARAMS,
    )(res_len, where_a, decode_query_rows, resident_keys, resident_values, new_keys, new_values)
    part = lax.all_to_all(part, ("core", "grp"), 0, 0, tiled=True)
    part = pl.pallas_call(
        pack_kernel,
        out_shape=jax.ShapeDtypeStruct((ring, 2 * queries // ring, HEAD_SIZE), bf),
        in_specs=[VMEM],
        out_specs=VMEM,
        compiler_params=PARAMS,
    )(part)
    part = lax.all_to_all(part, "z", 0, 0, tiled=True)
    packed = pl.pallas_call(
        finish_kernel,
        out_shape=jax.ShapeDtypeStruct((2 * tokens + queries // ring, HEAD_SIZE), bf),
        in_specs=[VMEM] * 3,
        out_specs=VMEM,
        compiler_params=PARAMS,
    )(part, new_keys, new_values)
    kv = lax.all_gather(packed, "z", axis=0)
    peer_kv = lax.ppermute(kv, "core", [(0, 1), (1, 0)])
    dec = pl.pallas_call(
        lambda *refs: spread_kernel(tokens, *refs),
        out_shape=jax.ShapeDtypeStruct((groups, queries, HEAD_SIZE), bf),
        in_specs=[VMEM],
        out_specs=VMEM,
        compiler_params=PARAMS,
    )(kv)
    dec = lax.all_to_all(dec, ("core", "grp"), 0, 0, tiled=True)

    bound = jnp.sum((segment_ids == 0).astype(i32))
    slots = ctx * pages + jnp.arange(pages, dtype=i32)
    ids = jnp.arange(page_table.shape[0], dtype=i32)
    page_from = jnp.sum(jnp.where(page_table[None, :] == slots[:, None], ids[None, :], 0), axis=1)
    where_b = jnp.stack([ctx, core, bound]).astype(i32)
    prefill_out, paged_keys, paged_values = pl.pallas_call(
        prefill_kernel,
        out_shape=(
            jax.ShapeDtypeStruct(new_queries.shape, bf),
            jax.ShapeDtypeStruct((pages, PAGE_TOKENS, HEAD_SIZE), bf),
            jax.ShapeDtypeStruct((pages, PAGE_TOKENS, HEAD_SIZE), bf),
        ),
        in_specs=[SMEM, SMEM] + [VMEM] * 3,
        out_specs=(VMEM,) * 3,
        scratch_shapes=[
            pltpu.VMEM((tokens * (new_queries.shape[1] // HEAD_SIZE), HEAD_SIZE), bf),
            pltpu.VMEM(
                (tokens * (new_queries.shape[1] // HEAD_SIZE), 2 * HEAD_SIZE), jnp.float32
            ),
            pltpu.VMEM((tokens * (new_queries.shape[1] // HEAD_SIZE), 1), jnp.float32),
        ],
        compiler_params=PARAMS,
    )(where_b, page_from, new_queries, kv, peer_kv)

    dec = lax.optimization_barrier((dec, paged_keys))[0]
    decode_out = pl.pallas_call(
        place_kernel,
        out_shape=jax.ShapeDtypeStruct((rows, width), bf),
        in_specs=[VMEM],
        out_specs=VMEM,
        compiler_params=PARAMS,
    )(dec)
    return (prefill_out, paged_keys, paged_values, decode_out)


def solution(mesh):
    sizes = mesh.shape
    fine = Mesh(
        np.asarray(mesh.devices).reshape(sizes["ctx"] // 2, 2, sizes["head"], sizes["grp"]),
        ("z", "core", "head", "grp"),
    )
    ctx = ("z", "core")
    return jax.shard_map(
        local,
        mesh=fine,
        in_specs=(
            P(ctx, ("head", "grp")),
            P(ctx, "head"),
            P(ctx, "head"),
            P(),
            P(),
            P(None, "head"),
            P(None, ("z", "core", "grp"), "head"),
            P(None, ("z", "core", "grp"), "head"),
            P(),
        ),
        out_specs=(
            P(ctx, ("head", "grp")),
            P(ctx, None, "head"),
            P(ctx, None, "head"),
            P(None, "head"),
        ),
        check_vma=False,
    )
```

time: 129 us -> 95.6 us (0.74)
  waiting for transfers between devices: 65.1 us -> 1.39 us
  blocking collectives: 15 us -> 63.8 us
  between operations: 14.1 us -> 0.74 us
  starting transfers between devices: 17.4 us -> 15.1 us
  local copies, waits for them, and re-layouts: 6.7 us -> 4.42 us
    all_gather x1 -> x0, waiting for transfers between devices: 63 us -> none  [local(): gathered = lax.all_gather(packed, 'z', axis=0)]
    all_gather x0 -> x1, blocking collectives: none -> 27.3 us  [local(): kv = lax.all_gather(packed, 'z', axis=0)]
    all_to_all x0 -> x1, blocking collectives: none -> 21.6 us  [local(): part = lax.all_to_all(part, 'z', 0, 0, tiled=True)]
    ppermute x3 -> x1, starting transfers between devices: 17.4 us -> 11.6 us  [local(): peer_kv = lax.ppermute(kv, 'core', [(0, 1), (1, 0)])]
    all_to_all x0 -> x1, starting transfers between devices: none -> 3.53 us  [local(): dec = lax.all_to_all(dec, ('core', 'grp'), 0, 0, tiled=True)]
    unnamed x20 -> x18, local copies, waits for them, and re-layouts: 6.7 us -> 4.42 us
    ppermute x3 -> x1, waiting for transfers between devices: 2.02 us -> 0.01 us  [local(): peer_kv = lax.ppermute(kv, 'core', [(0, 1), (1, 0)])]
    all_to_all x0 -> x1, waiting for transfers between devices: none -> 1.38 us  [local(): dec = lax.all_to_all(dec, ('core', 'grp'), 0, 0, tiled=True)]
  transfers between devices with their start and end apart: 4 -> 2, of which waited for: 3 -> 1; matrix products, arithmetic and copies ran while one was open for 1% -> 2% of each run, Pallas kernels for 0% -> 4%
where the time goes in v2:
time: 95.6 us; the launch traced here: 95 us
  blocking collectives  63.8 us (67%)
  starting transfers between devices  15.1 us (16%)
  Pallas kernels  7.89 us (8%)
  local copies, waits for them, and re-layouts  4.42 us (5%)
  other arithmetic  1.62 us (2%)
  waiting for transfers between devices  1.39 us (1%)
    all_gather x1, blocking collectives, local(): kv = lax.all_gather(packed, 'z', axis=0)  27.3 us
    all_to_all x1, blocking collectives, local(): part = lax.all_to_all(part, 'z', 0, 0, tiled=True)  21.6 us
    all_to_all x1, blocking collectives, local(): part = lax.all_to_all(part, ('core', 'grp'), 0, 0, tiled=True)  15 us
    ppermute x1, starting transfers between devices, local(): peer_kv = lax.ppermute(kv, 'core', [(0, 1), (1, 0)])  11.6 us
    unnamed x18, local copies, waits for them, and re-layouts  4.42 us
    all_to_all x1, starting transfers between devices, local(): dec = lax.all_to_all(dec, ('core', 'grp'), 0, 0, tiled=True)  3.53 us
    pallas_call x1, Pallas kernels, local(): pl.pallas_call(partial_kernel, grid=(groups,), out_shape=jax.ShapeDtypeSt...  2.94 us
    pallas_call x1, Pallas kernels, local(): pl.pallas_call(prefill_kernel, out_shape=(jax.ShapeDtypeStruct(new_querie...  2.83 us
  transfers between devices with their start and end apart: 2, of which 1 were waited for; matrix products, arithmetic and copies ran while one was open for 2% of the time, Pallas kernels for 4%

profile of v2, /device:TPU:1, one launch (start us, length us, event | category | flops | bytes accessed | tf_op | source)
XLA Modules:
  0.0 95.0 jit_solution(15667122845279001288)
XLA Ops:
  0.6 0.0 copy-start.4
  0.7 0.0 copy-start.6
  0.7 0.1 pad_add_fusion.1.where_ref
  0.7 0.6 copy-done.4
  1.4 0.0 copy-done.6
  1.4 0.0 copy-start
  1.4 1.0 %copy-done = bf16[64,32,128]{2,1,0:T(8,128)(2,1)S(1)} copy-done((bf16[64,32,128]{2,1,0:T(8,128)(2,1)S(1)}, bf16[64,32,128]{2,1,0:T(8,128)(2,1)}, u32[]{:S(2)}) %copy-start) | copy-done | bytes 524312
  2.4 0.0 copy-start.1
  2.4 1.0 %copy-done.1 = bf16[64,32,128]{2,1,0:T(8,128)(2,1)S(1)} copy-done((bf16[64,32,128]{2,1,0:T(8,128)(2,1)S(1)}, bf16[64,32,128]{2,1,0:T(8,128)(2,1)}, u32[]{:S(2)}) %copy-start.1) | copy-done | bytes 524312
  3.5 0.0 copy-start.2
  3.5 0.9 copy-done.2
  4.4 0.0 copy-start.5
  4.4 0.7 copy-done.5
  5.1 2.9 %shard_map.120 = bf16[4,272,128]{2,1,0:T(8,128)(2,1)S(1)} custom-call(s32[64]{0:T(128)S(1)} %copy-done.6, s32[3]{0:T(128)S(1)} %pad_add_fusion.1.where_ref, bf16[64,2048]{1,0:T(8,128)(2,1)S(1)} %copy-done.2, bf16[64,32,128]{2,1,0:T(8,128)(2,1)S(1)} %copy-done, bf16[64,32,128]{2,1,0:T(8,128)(2,1)S(1)} %copy-done.1, bf16[96,128]{1,0:T(8,128)(2,1)S(1)} %copy-done.4, ...), custom_call_target="tpu_custom_call" | custom-call | tf_op jit(solution)/shard_map/pallas_call | solution.py:236
  8.1 15.0 %all_to_all.15.part_ref = bf16[4,272,128]{2,1,0:T(8,128)(2,1)S(1)} all-to-all(bf16[4,272,128]{2,1,0:T(8,128)(2,1)S(1)} %shard_map.120), channel_id=1, replica_groups=mesh['z'=16,'core'=2,'head'=8,'grp'=2] {'core','grp'}, dimensions={0} | all-to-all | bytes 557056 | tf_op jit(solution)/shard_map/all_to_all | solution.py:246
  23.1 0.4 shard_map.121
  23.5 21.6 %all_to_all.16.part_ref = bf16[16,32,128]{2,1,0:T(8,128)(2,1)S(1)} all-to-all(bf16[16,32,128]{2,1,0:T(8,128)(2,1)S(1)} %shard_map.121), channel_id=1, replica_groups=mesh['z'=16,'core'=2,'head'=8,'grp'=2] {'z'}, dimensions={0} | all-to-all | bytes 262144 | tf_op jit(solution)/shard_map/all_to_all | solution.py:254
  45.0 0.2 shard_map.122
  45.3 0.0 copy-start.7
  45.3 27.3 %all-gather = bf16[3328,128]{1,0:T(8,128)(2,1)S(1)} all-gather(bf16[208,128]{1,0:T(8,128)(2,1)S(1)} %shard_map.122), channel_id=2, replica_groups=mesh['z'=16,'core'=2,'head'=8,'grp'=2] {'z'}, dimensions={0}, use_global_device_ids=true | all-gather | bytes 905216 | tf_op jit(solution)/shard_map/all_gather | solution.py:262
  72.6 11.6 %collective-permute-start = (bf16[16,208,128]{2,1,0:T(8,128)(2,1)S(1)}, bf16[16,208,128]{2,1,0:T(8,128)(2,1)S(1)}, u32[]{:S(2)}, u32[]{:S(2)}) collective-permute-start(bf16[16,208,128]{2,1,0:T(8,128)(2,1)S(1)} %bitcast.6), channel_id=1, source_target_pairs={{0,16},{16,0},{1,17},{17,1},{2,18},{18,2},{3,19},{19,3},{4,20},{20... | collective-permute-start | bytes 2555912 | tf_op jit(solution)/shard_map/ppermute | solution.py:263
  84.2 0.0 copy-done.7
  84.2 0.6 convert_reduce_fusion
  84.8 0.7 shard_map.124
  85.6 0.0 copy-start.3
  85.6 3.5 %all-to-all-start.2 = ((bf16[4,256,128]{2,1,0:T(8,128)(2,1)}), bf16[4,256,128]{2,1,0:T(8,128)(2,1)S(1)}, u32[]{:S(2)}, u32[]{:S(2)}) async-start(bf16[4,256,128]{2,1,0:T(8,128)(2,1)} %shard_map.124), calls=%async_computation.2 | async-start | bytes 524288 | tf_op jit(solution)/shard_map/all_to_all | solution.py:271
  89.1 0.0 copy-start.8
  89.1 0.7 pad_add_fusion.where_ref
  89.9 0.0 copy-done.8
  89.9 0.2 select_reduce_fusion.page_ref
  90.0 0.0 collective-permute-done.peer_ref
  90.1 0.0 copy-done.3
  90.1 2.8 %shard_map.123 = (bf16[96,1024]{1,0:T(8,128)(2,1)}, bf16[6,16,128]{2,1,0:T(8,128)(2,1)}, bf16[6,16,128]{2,1,0:T(8,128)(2,1)}) custom-call(s32[3]{0:T(128)S(1)} %pad_add_fusion.where_ref, s32[6]{0:T(128)S(1)} %select_reduce_fusion.page_ref, bf16[96,1024]{1,0:T(8,128)(2,1)S(1)} %copy-done.3, bf16[16,208,128]{2,1,0:T(8,128)(2,1)S(1)} %bitcast.8, ...), custom_call_target="tpu_custom_call" | custom-call | tf_op jit(solution)/shard_map/pallas_call | solution.py:278
  92.9 1.4 %all-to-all-done.2.in_ref = bf16[4,256,128]{2,1,0:T(8,128)(2,1)S(1)} async-done(((bf16[4,256,128]{2,1,0:T(8,128)(2,1)}), bf16[4,256,128]{2,1,0:T(8,128)(2,1)S(1)}, u32[]{:S(2)}, u32[]{:S(2)}) %all-to-all-start.2) | async-done | bytes 262176 | tf_op jit(solution)/shard_map/all_to_all | solution.py:271
  94.3 0.7 shard_map.125
  (1 shorter events, 0.0 us)
Async XLA Ops:
  0.6 0.7 copy-start.4
  0.7 0.7 copy-start.6
  1.4 1.0 %copy-start = (bf16[64,32,128]{2,1,0:T(8,128)(2,1)S(1)}, bf16[64,32,128]{2,1,0:T(8,128)(2,1)}, u32[]{:S(2)}) copy-start(bf16[64,32,128]{2,1,0:T(8,128)(2,1)} %rk_ref.1) | copy-start | bytes 1572868
  2.4 1.0 %copy-start.1 = (bf16[64,32,128]{2,1,0:T(8,128)(2,1)S(1)}, bf16[64,32,128]{2,1,0:T(8,128)(2,1)}, u32[]{:S(2)}) copy-start(bf16[64,32,128]{2,1,0:T(8,128)(2,1)} %rv_ref.1) | copy-start | bytes 1572868
  3.5 0.9 copy-start.2
  4.4 0.7 copy-start.5
  45.3 38.9 %copy-start.7 = (s32[3072]{0:T(1024)S(1)}, s32[3072]{0:T(1024)}, u32[]{:S(2)}) copy-start(s32[3072]{0:T(1024)} %param.12) | copy-start | bytes 36868
  72.6 17.5 %collective-permute-start = (bf16[16,208,128]{2,1,0:T(8,128)(2,1)S(1)}, bf16[16,208,128]{2,1,0:T(8,128)(2,1)S(1)}, u32[]{:S(2)}, u32[]{:S(2)}) collective-permute-start(bf16[16,208,128]{2,1,0:T(8,128)(2,1)S(1)} %bitcast.6), channel_id=1, source_target_pairs={{0,16},{16,0},{1,17},{17,1},{2,18},{18,2},{3,19},{19,3},{4,20},{20... | collective-permute-start | bytes 2555912 | tf_op jit(solution)/shard_map/ppermute | solution.py:263
  85.6 4.5 %copy-start.3 = (bf16[96,1024]{1,0:T(8,128)(2,1)S(1)}, bf16[96,1024]{1,0:T(8,128)(2,1)}, u32[]{:S(2)}) copy-start(bf16[96,1024]{1,0:T(8,128)(2,1)} %q_ref.1) | copy-start | bytes 589828
  85.6 8.7 %all-to-all-start.2 = ((bf16[4,256,128]{2,1,0:T(8,128)(2,1)}), bf16[4,256,128]{2,1,0:T(8,128)(2,1)S(1)}, u32[]{:S(2)}, u32[]{:S(2)}) async-start(bf16[4,256,128]{2,1,0:T(8,128)(2,1)} %shard_map.124), calls=%async_computation.2 | async-start | bytes 524288 | tf_op jit(solution)/shard_map/all_to_all | solution.py:271
  89.1 0.7 copy-start.8

commit v3 on v2

--- a/solution.py
+++ b/solution.py
@@ -11,6 +11,7 @@
 NEG_FILL = -1e30
 LOG2_SCALE = HEAD_SIZE**-0.5 * 1.4426950408889634
 VMEM = pl.BlockSpec(memory_space=pltpu.VMEM)
+HBM = pl.BlockSpec(memory_space=pltpu.HBM)
 SMEM = pl.BlockSpec(memory_space=pltpu.SMEM)
 PARAMS = pltpu.CompilerParams(vmem_limit_bytes=48 * 1024 * 1024)
 
@@ -32,11 +33,28 @@
     ]
 
 
-def partial_kernel(len_ref, where_ref, dq_ref, rk_ref, rv_ref, nk_ref, nv_ref, out_ref):
-    g = pl.program_id(0)
-    res_rows = rk_ref.shape[1]
-    heads = dq_ref.shape[1] // HEAD_SIZE
-    tokens = nk_ref.shape[0]
+def partial_kernel(
+    len_ref, where_ref, dq_hbm, rk_hbm, rv_hbm, nk_hbm, nv_hbm, out_ref, dq, rk, rv, nk, nv, sems
+):
+    groups = out_ref.shape[0]
+    res_rows = rk.shape[1]
+    heads = dq.shape[1] // HEAD_SIZE
+    tokens = nk.shape[0]
+    loads = []
+    for g in range(groups):
+        rows = pl.ds(16 * g, 16)
+        loads.append(
+            [
+                pltpu.make_async_copy(src.at[rows], dst.at[rows], sems.at[3 * g + i])
+                for i, (src, dst) in enumerate(((dq_hbm, dq), (rk_hbm, rk), (rv_hbm, rv)))
+            ]
+        )
+    new_loads = [
+        pltpu.make_async_copy(src, dst, sems.at[3 * groups + i])
+        for i, (src, dst) in enumerate(((nk_hbm, nk), (nv_hbm, nv)))
+    ]
+    for copy in loads[0] + new_loads + [copy for group in loads[1:] for copy in group]:
+        copy.start()
     base, grp, half_rows = where_ref[0], where_ref[1], where_ref[2]
     keys = 16 * res_rows
     queries = 16 * heads
@@ -48,29 +66,36 @@
     )
     token = lax.broadcasted_iota(jnp.int32, (1, tokens), 1) - grp * half_rows
     token_bias = jnp.where((token >= 0) & (token < half_rows), 0.0, NEG_FILL)
-    lens = jnp.zeros((1, keys), jnp.int32)
-    for r in range(16):
-        lens = jnp.where(col_row == r, len_ref[16 * g + r], lens)
-    live = jnp.where(col_pos < lens, 0.0, NEG_FILL)
-    q = jnp.concatenate(
-        [dq_ref[:, h * HEAD_SIZE : (h + 1) * HEAD_SIZE] for h in range(heads)], axis=0
-    )
-    rk = rk_ref[...].reshape(keys, HEAD_SIZE)
-    rv = rv_ref[...].reshape(keys, HEAD_SIZE)
-    s1 = jnp.where(same_row, dot_t(q, rk) * LOG2_SCALE + live, NEG_FILL)
-    s2 = dot_t(q, nk_ref[...]) * LOG2_SCALE + token_bias
-    top = jnp.maximum(jnp.max(s1, axis=1, keepdims=True), jnp.max(s2, axis=1, keepdims=True))
-    top = top.astype(jnp.bfloat16).astype(jnp.float32)
-    p1 = jnp.exp2(s1 - top).astype(jnp.bfloat16)
-    p2 = jnp.exp2(s2 - top).astype(jnp.bfloat16)
-    total = jnp.sum(p1.astype(jnp.float32), axis=1, keepdims=True) + jnp.sum(
-        p2.astype(jnp.float32), axis=1, keepdims=True
-    )
-    out_ref[0, :queries] = (dot(p1, rv) + dot(p2, nv_ref[...])).astype(jnp.bfloat16)
-    high = total.astype(jnp.bfloat16).astype(jnp.float32)
-    stats = as_rows(top) + as_rows(high) + as_rows(total - high)
-    stats = jnp.concatenate(stats + [jnp.zeros((10, 128), jnp.float32)], axis=0)
-    out_ref[0, queries : queries + 16] = stats.astype(jnp.bfloat16)
+    for g in range(groups):
+        lens = jnp.zeros((1, keys), jnp.int32)
+        for r in range(16):
+            lens = jnp.where(col_row == r, len_ref[16 * g + r], lens)
+        live = jnp.where(col_pos < lens, 0.0, NEG_FILL)
+        for copy in loads[g] + (new_loads if g == 0 else []):
+            copy.wait()
+        q = jnp.concatenate(
+            [
+                dq[16 * g : 16 * g + 16, h * HEAD_SIZE : (h + 1) * HEAD_SIZE]
+                for h in range(heads)
+            ],
+            axis=0,
+        )
+        res_k = rk[16 * g : 16 * g + 16].reshape(keys, HEAD_SIZE)
+        res_v = rv[16 * g : 16 * g + 16].reshape(keys, HEAD_SIZE)
+        s1 = jnp.where(same_row, dot_t(q, res_k) * LOG2_SCALE + live, NEG_FILL)
+        s2 = dot_t(q, nk[...]) * LOG2_SCALE + token_bias
+        top = jnp.maximum(jnp.max(s1, axis=1, keepdims=True), jnp.max(s2, axis=1, keepdims=True))
+        top = top.astype(jnp.bfloat16).astype(jnp.float32)
+        p1 = jnp.exp2(s1 - top).astype(jnp.bfloat16)
+        p2 = jnp.exp2(s2 - top).astype(jnp.bfloat16)
+        total = jnp.sum(p1.astype(jnp.float32), axis=1, keepdims=True) + jnp.sum(
+            p2.astype(jnp.float32), axis=1, keepdims=True
+        )
+        out_ref[g, :queries] = (dot(p1, res_v) + dot(p2, nv[...])).astype(jnp.bfloat16)
+        high = total.astype(jnp.bfloat16).astype(jnp.float32)
+        stats = as_rows(top) + as_rows(high) + as_rows(total - high)
+        stats = jnp.concatenate(stats + [jnp.zeros((10, 128), jnp.float32)], axis=0)
+        out_ref[g, queries : queries + 16] = stats.astype(jnp.bfloat16)
 
 
 def pack_kernel(part_ref, out_ref):
@@ -138,7 +163,7 @@
     ctx, core, bound = where_ref[0], where_ref[1], where_ref[2]
     tokens = q_ref.shape[0]
     heads = q_ref.shape[1] // HEAD_SIZE
-    blocks_per = 2
+    blocks_per = min(4, own_ref.shape[0])
     block = 2 * blocks_per * tokens
     row_block = 2 * tokens
     for s in range(pk_ref.shape[0]):
@@ -231,19 +256,28 @@
 
     where_a = jnp.stack([(ctx * 2 + grp) * res_rows, grp, jnp.int32(tokens // 2)]).astype(i32)
     groups = rows // 16
-    resident = pl.BlockSpec((16, res_rows, HEAD_SIZE), lambda g: (g, 0, 0))
-    whole = pl.BlockSpec((tokens, HEAD_SIZE), lambda g: (0, 0))
     part = pl.pallas_call(
         partial_kernel,
-        grid=(groups,),
         out_shape=jax.ShapeDtypeStruct((groups, queries + 16, HEAD_SIZE), bf),
-        in_specs=[SMEM, SMEM, pl.BlockSpec((16, width), lambda g: (g, 0))]
-        + [resident] * 2
-        + [whole] * 2,
-        out_specs=pl.BlockSpec((1, queries + 16, HEAD_SIZE), lambda g: (g, 0, 0)),
-        compiler_params=PARAMS,
+        in_specs=[SMEM, SMEM] + [HBM] * 5,
+        out_specs=VMEM,
+        scratch_shapes=[
+            pltpu.VMEM(decode_query_rows.shape, bf),
+            pltpu.VMEM(resident_keys.shape, bf),
+            pltpu.VMEM(resident_values.shape, bf),
+            pltpu.VMEM(new_keys.shape, bf),
+            pltpu.VMEM(new_values.shape, bf),
+            pltpu.SemaphoreType.DMA((3 * groups + 2,)),
+        ],
+        compiler_params=pltpu.CompilerParams(vmem_limit_bytes=63 * 1024 * 1024),
     )(res_len, where_a, decode_query_rows, resident_keys, resident_values, new_keys, new_values)
+    bound = jnp.sum((segment_ids == 0).astype(i32))
+    slots = ctx * pages + jnp.arange(pages, dtype=i32)
+    ids = jnp.arange(page_table.shape[0], dtype=i32)
+    page_from = jnp.sum(jnp.where(page_table[None, :] == slots[:, None], ids[None, :], 0), axis=1)
+    where_b = jnp.stack([ctx, core, bound]).astype(i32)
     part = lax.all_to_all(part, ("core", "grp"), 0, 0, tiled=True)
+    part, where_b, page_from = lax.optimization_barrier((part, where_b, page_from))
     part = pl.pallas_call(
         pack_kernel,
         out_shape=jax.ShapeDtypeStruct((ring, 2 * queries // ring, HEAD_SIZE), bf),
@@ -270,11 +304,6 @@
     )(kv)
     dec = lax.all_to_all(dec, ("core", "grp"), 0, 0, tiled=True)
 
-    bound = jnp.sum((segment_ids == 0).astype(i32))
-    slots = ctx * pages + jnp.arange(pages, dtype=i32)
-    ids = jnp.arange(page_table.shape[0], dtype=i32)
-    page_from = jnp.sum(jnp.where(page_table[None, :] == slots[:, None], ids[None, :], 0), axis=1)
-    where_b = jnp.stack([ctx, core, bound]).astype(i32)
     prefill_out, paged_keys, paged_values = pl.pallas_call(
         prefill_kernel,
         out_shape=(

time: 95.6 us -> 93.1 us (0.974)
  blocking collectives: 63.8 us -> 48 us
  starting transfers between devices: 15.1 us -> 25.8 us
  waiting for transfers between devices: 1.39 us -> 5.83 us
  local copies, waits for them, and re-layouts: 4.42 us -> 0.03 us
  Pallas kernels: 7.89 us -> 10.1 us
    all_to_all x1 -> x0, blocking collectives: 15 us -> none  [local(): part = lax.all_to_all(part, ('core', 'grp'), 0, 0, tiled=True)]
    all_to_all x0 -> x1, starting transfers between devices: none -> 10.3 us  [local(): part = lax.all_to_all(part, ('core', 'grp'), 0, 0, tiled=True)]
    unnamed x18 -> x10, local copies, waits for them, and re-layouts: 4.42 us -> 0.03 us
    all_to_all x0 -> x1, waiting for transfers between devices: none -> 3.78 us  [local(): part = lax.all_to_all(part, ('core', 'grp'), 0, 0, tiled=True)]
    pallas_call x1, Pallas kernels: 2.94 us -> 4.86 us  [local(): pl.pallas_call(partial_kernel, out_shape=jax.ShapeDtypeStruct((groups, qu...]
  transfers between devices with their start and end apart: 2 -> 3, of which waited for: 1 -> 2; matrix products, arithmetic and copies ran while one was open for 2% -> 2% of each run, Pallas kernels for 4% -> 4%
where the time goes in v3:
time: 93.1 us; the launch traced here: 92.6 us
  blocking collectives  48 us (52%)
  starting transfers between devices  25.8 us (28%)
  Pallas kernels  10.1 us (11%)
  waiting for transfers between devices  5.83 us (6%)
  other arithmetic  2.17 us (2%)
    all_gather x1, blocking collectives, local(): kv = lax.all_gather(packed, 'z', axis=0)  26.7 us
    all_to_all x1, blocking collectives, local(): part = lax.all_to_all(part, 'z', 0, 0, tiled=True)  21.3 us
    ppermute x1, starting transfers between devices, local(): peer_kv = lax.ppermute(kv, 'core', [(0, 1), (1, 0)])  12 us
    all_to_all x1, starting transfers between devices, local(): part = lax.all_to_all(part, ('core', 'grp'), 0, 0, tiled=True)  10.3 us
    pallas_call x1, Pallas kernels, local(): pl.pallas_call(partial_kernel, out_shape=jax.ShapeDtypeStruct((groups, qu...  4.86 us
    all_to_all x1, waiting for transfers between devices, local(): part = lax.all_to_all(part, ('core', 'grp'), 0, 0, tiled=True)  3.78 us
    all_to_all x1, starting transfers between devices, local(): dec = lax.all_to_all(dec, ('core', 'grp'), 0, 0, tiled=True)  3.53 us
    pallas_call x1, Pallas kernels, local(): pl.pallas_call(prefill_kernel, out_shape=(jax.ShapeDtypeStruct(new_querie...  3.08 us
  transfers between devices with their start and end apart: 3, of which 2 were waited for; matrix products, arithmetic and copies ran while one was open for 2% of the time, Pallas kernels for 4%

profile of v3, /device:TPU:1, one launch (start us, length us, event | category | flops | bytes accessed | tf_op | source)
XLA Modules:
  0.0 92.6 jit_solution(14669490649242583818)
XLA Ops:
  0.6 0.6 pad_add_fusion.where_ref
  1.3 4.9 %shard_map.120 = bf16[4,272,128]{2,1,0:T(8,128)(2,1)} custom-call(s32[64]{0:T(128)} %len_ref.1, s32[3]{0:T(128)} %pad_add_fusion.where_ref, bf16[64,2048]{1,0:T(8,128)(2,1)} %dq_hbm.1, bf16[64,32,128]{2,1,0:T(8,128)(2,1)} %rk_hbm.1, bf16[64,32,128]{2,1,0:T(8,128)(2,1)} %rv_hbm.1, bf16[96,128]{1,0:T(8,128)(2,1)} %nk_ref.1, bf16[96,128]{1,0:T(8,128)(2,1)} %nv_ref.1), custom_call_target="tpu_custom_call" | custom-call | tf_op jit(solution)/shard_map/pallas_call | solution.py:259
  6.1 0.0 copy-start.3
  6.1 10.3 %all-to-all-start = ((bf16[4,272,128]{2,1,0:T(8,128)(2,1)}), bf16[4,272,128]{2,1,0:T(8,128)(2,1)S(1)}, u32[]{:S(2)}, u32[]{:S(2)}) async-start(bf16[4,272,128]{2,1,0:T(8,128)(2,1)} %shard_map.120), calls=%async_computation | async-start | bytes 557056 | tf_op jit(solution)/shard_map/all_to_all | solution.py:279
  16.4 0.0 copy-done.3
  16.4 0.6 convert_reduce_fusion
  17.1 0.0 copy-start.4
  17.1 0.7 pad_add_fusion.1.where_ref
  17.8 0.0 copy-done.4
  17.8 0.2 select_reduce_fusion.page_ref
  18.0 3.8 %all-to-all-done.part_ref = bf16[4,272,128]{2,1,0:T(8,128)(2,1)S(1)} async-done(((bf16[4,272,128]{2,1,0:T(8,128)(2,1)}), bf16[4,272,128]{2,1,0:T(8,128)(2,1)S(1)}, u32[]{:S(2)}, u32[]{:S(2)}) %all-to-all-start) | async-done | bytes 278560 | tf_op jit(solution)/shard_map/all_to_all | solution.py:279
  21.8 0.4 shard_map.121
  22.2 0.0 copy-start.1
  22.2 0.0 copy-start.2
  22.2 21.3 %all_to_all.15.part_ref = bf16[16,32,128]{2,1,0:T(8,128)(2,1)S(1)} all-to-all(bf16[16,32,128]{2,1,0:T(8,128)(2,1)S(1)} %shard_map.121), channel_id=1, replica_groups=mesh['z'=16,'core'=2,'head'=8,'grp'=2] {'z'}, dimensions={0} | all-to-all | bytes 262144 | tf_op jit(solution)/shard_map/all_to_all | solution.py:288
  43.5 0.0 copy-done.1
  43.5 0.0 copy-done.2
  43.5 0.2 shard_map.122
  43.8 26.7 %all-gather = bf16[3328,128]{1,0:T(8,128)(2,1)S(1)} all-gather(bf16[208,128]{1,0:T(8,128)(2,1)S(1)} %shard_map.122), channel_id=2, replica_groups=mesh['z'=16,'core'=2,'head'=8,'grp'=2] {'z'}, dimensions={0}, use_global_device_ids=true | all-gather | bytes 905216 | tf_op jit(solution)/shard_map/all_gather | solution.py:296
  70.5 12.0 %collective-permute-start = (bf16[16,208,128]{2,1,0:T(8,128)(2,1)S(1)}, bf16[16,208,128]{2,1,0:T(8,128)(2,1)S(1)}, u32[]{:S(2)}, u32[]{:S(2)}) collective-permute-start(bf16[16,208,128]{2,1,0:T(8,128)(2,1)S(1)} %bitcast.6), channel_id=1, source_target_pairs={{0,16},{16,0},{1,17},{17,1},{2,18},{18,2},{3,19},{19,3},{4,20},{20... | collective-permute-start | bytes 2555912 | tf_op jit(solution)/shard_map/ppermute | solution.py:297
  82.5 0.7 shard_map.124
  83.2 0.0 copy-start
  83.2 3.5 %all-to-all-start.2 = ((bf16[4,256,128]{2,1,0:T(8,128)(2,1)}), bf16[4,256,128]{2,1,0:T(8,128)(2,1)S(1)}, u32[]{:S(2)}, u32[]{:S(2)}) async-start(bf16[4,256,128]{2,1,0:T(8,128)(2,1)} %shard_map.124), calls=%async_computation.2 | async-start | bytes 524288 | tf_op jit(solution)/shard_map/all_to_all | solution.py:305
  86.7 0.0 collective-permute-done.peer_ref
  86.7 0.0 copy-done
  86.8 3.1 %shard_map.123 = (bf16[96,1024]{1,0:T(8,128)(2,1)}, bf16[6,16,128]{2,1,0:T(8,128)(2,1)}, bf16[6,16,128]{2,1,0:T(8,128)(2,1)}) custom-call(s32[3]{0:T(128)S(1)} %pad_add_fusion.1.where_ref, s32[6]{0:T(128)S(1)} %select_reduce_fusion.page_ref, bf16[96,1024]{1,0:T(8,128)(2,1)S(1)} %copy-done, bf16[16,208,128]{2,1,0:T(8,128)(2,1)S(1)} %bitcast.8, ...), custom_call_target="tpu_custom_call" | custom-call | tf_op jit(solution)/shard_map/pallas_call | solution.py:307
  89.8 2.0 %all-to-all-done.2.in_ref = bf16[4,256,128]{2,1,0:T(8,128)(2,1)S(1)} async-done(((bf16[4,256,128]{2,1,0:T(8,128)(2,1)}), bf16[4,256,128]{2,1,0:T(8,128)(2,1)S(1)}, u32[]{:S(2)}, u32[]{:S(2)}) %all-to-all-start.2) | async-done | bytes 262176 | tf_op jit(solution)/shard_map/all_to_all | solution.py:305
  91.9 0.7 shard_map.125
  (1 shorter events, 0.0 us)
Async XLA Ops:
  6.1 10.3 %copy-start.3 = (s32[3072]{0:T(1024)S(1)}, s32[3072]{0:T(1024)}, u32[]{:S(2)}) copy-start(s32[3072]{0:T(1024)} %param.12) | copy-start | bytes 36868
  6.1 15.6 %all-to-all-start = ((bf16[4,272,128]{2,1,0:T(8,128)(2,1)}), bf16[4,272,128]{2,1,0:T(8,128)(2,1)S(1)}, u32[]{:S(2)}, u32[]{:S(2)}) async-start(bf16[4,272,128]{2,1,0:T(8,128)(2,1)} %shard_map.120), calls=%async_computation | async-start | bytes 557056 | tf_op jit(solution)/shard_map/all_to_all | solution.py:279
  17.1 0.7 copy-start.4
  22.2 21.3 %copy-start.1 = (bf16[96,128]{1,0:T(8,128)(2,1)S(1)}, bf16[96,128]{1,0:T(8,128)(2,1)}, u32[]{:S(2)}) copy-start(bf16[96,128]{1,0:T(8,128)(2,1)} %nk_ref.1) | copy-start | bytes 73732
  22.2 21.3 %copy-start.2 = (bf16[96,128]{1,0:T(8,128)(2,1)S(1)}, bf16[96,128]{1,0:T(8,128)(2,1)}, u32[]{:S(2)}) copy-start(bf16[96,128]{1,0:T(8,128)(2,1)} %nv_ref.1) | copy-start | bytes 73732
  70.5 16.3 %collective-permute-start = (bf16[16,208,128]{2,1,0:T(8,128)(2,1)S(1)}, bf16[16,208,128]{2,1,0:T(8,128)(2,1)S(1)}, u32[]{:S(2)}, u32[]{:S(2)}) collective-permute-start(bf16[16,208,128]{2,1,0:T(8,128)(2,1)S(1)} %bitcast.6), channel_id=1, source_target_pairs={{0,16},{16,0},{1,17},{17,1},{2,18},{18,2},{3,19},{19,3},{4,20},{20... | collective-permute-start | bytes 2555912 | tf_op jit(solution)/shard_map/ppermute | solution.py:297
  83.2 3.6 %copy-start = (bf16[96,1024]{1,0:T(8,128)(2,1)S(1)}, bf16[96,1024]{1,0:T(8,128)(2,1)}, u32[]{:S(2)}) copy-start(bf16[96,1024]{1,0:T(8,128)(2,1)} %q_ref.1) | copy-start | bytes 589828
  83.2 8.7 %all-to-all-start.2 = ((bf16[4,256,128]{2,1,0:T(8,128)(2,1)}), bf16[4,256,128]{2,1,0:T(8,128)(2,1)S(1)}, u32[]{:S(2)}, u32[]{:S(2)}) async-start(bf16[4,256,128]{2,1,0:T(8,128)(2,1)} %shard_map.124), calls=%async_computation.2 | async-start | bytes 524288 | tf_op jit(solution)/shard_map/all_to_all | solution.py:305

commit v4 on v3

v4 whole, which is shorter than its diff:
```python
import jax
import jax.numpy as jnp
import numpy as np
from jax import lax
from jax.experimental import pallas as pl
from jax.experimental.pallas import tpu as pltpu
from jax.sharding import Mesh, PartitionSpec as P

HEAD_SIZE = 128
PAGE_TOKENS = 16
NEG_FILL = -1e30
LOG2_SCALE = HEAD_SIZE**-0.5 * 1.4426950408889634
VMEM = pl.BlockSpec(memory_space=pltpu.VMEM)
HBM = pl.BlockSpec(memory_space=pltpu.HBM)
SMEM = pl.BlockSpec(memory_space=pltpu.SMEM)
PARAMS = pltpu.CompilerParams(vmem_limit_bytes=48 * 1024 * 1024)


def dot_t(a, b):
    return lax.dot_general(a, b, (((1,), (1,)), ((), ())), preferred_element_type=jnp.float32)


def dot(a, b):
    return jnp.dot(a, b, preferred_element_type=jnp.float32)


def as_row(column, pick):
    return jnp.sum(jnp.where(pick, column, 0.0), axis=0, keepdims=True)


def partial_kernel(
    len_ref, where_ref, dq_hbm, rk_hbm, rv_hbm, nk_hbm, nv_hbm, out_ref, dq, rk, rv, nk, nv, sems
):
    groups = dq.shape[0] // 16
    res_rows = rk.shape[1]
    heads = dq.shape[1] // HEAD_SIZE
    tokens = nk.shape[0]
    loads = []
    for g in range(groups):
        rows = pl.ds(16 * g, 16)
        loads.append(
            [
                pltpu.make_async_copy(src.at[rows], dst.at[rows], sems.at[3 * g + i])
                for i, (src, dst) in enumerate(((dq_hbm, dq), (rk_hbm, rk), (rv_hbm, rv)))
            ]
        )
    new_loads = [
        pltpu.make_async_copy(src, dst, sems.at[3 * groups + i])
        for i, (src, dst) in enumerate(((nk_hbm, nk), (nv_hbm, nv)))
    ]
    for copy in loads[0] + new_loads + [copy for group in loads[1:] for copy in group]:
        copy.start()
    base, grp, half_rows = where_ref[0], where_ref[1], where_ref[2]
    keys = 16 * res_rows
    queries = 16 * heads
    col = lax.broadcasted_iota(jnp.int32, (1, keys), 1)
    col_row = col // res_rows
    col_pos = base + col % res_rows
    same_row = (lax.broadcasted_iota(jnp.int32, (queries, keys), 0) % 16) == (
        lax.broadcasted_iota(jnp.int32, (queries, keys), 1) // res_rows
    )
    token = lax.broadcasted_iota(jnp.int32, (1, tokens), 1) - grp * half_rows
    token_bias = jnp.where((token >= 0) & (token < half_rows), 0.0, NEG_FILL)
    entry = lax.broadcasted_iota(jnp.int32, (queries, 128), 0)
    lane = lax.broadcasted_iota(jnp.int32, (queries, 128), 1)
    picks = [entry == (lane // 8) * 16 + side * 8 + lane % 8 for side in range(2)]
    for g in range(groups):
        lens = jnp.zeros((1, keys), jnp.int32)
        for r in range(16):
            lens = jnp.where(col_row == r, len_ref[16 * g + r], lens)
        live = jnp.where(col_pos < lens, 0.0, NEG_FILL)
        for copy in loads[g] + (new_loads if g == 0 else []):
            copy.wait()
        q = jnp.concatenate(
            [
                dq[16 * g : 16 * g + 16, h * HEAD_SIZE : (h + 1) * HEAD_SIZE]
                for h in range(heads)
            ],
            axis=0,
        )
        res_k = rk[16 * g : 16 * g + 16].reshape(keys, HEAD_SIZE)
        res_v = rv[16 * g : 16 * g + 16].reshape(keys, HEAD_SIZE)
        s1 = jnp.where(same_row, dot_t(q, res_k) * LOG2_SCALE + live, NEG_FILL)
        s2 = dot_t(q, nk[...]) * LOG2_SCALE + token_bias
        top = jnp.maximum(jnp.max(s1, axis=1, keepdims=True), jnp.max(s2, axis=1, keepdims=True))
        top = top.astype(jnp.bfloat16).astype(jnp.float32)
        p1 = jnp.exp2(s1 - top).astype(jnp.bfloat16)
        p2 = jnp.exp2(s2 - top).astype(jnp.bfloat16)
        total = jnp.sum(p1.astype(jnp.float32), axis=1, keepdims=True) + jnp.sum(
            p2.astype(jnp.float32), axis=1, keepdims=True
        )
        values = (dot(p1, res_v) + dot(p2, nv[...])).reshape(heads, 2, 8, HEAD_SIZE)
        high = total.astype(jnp.bfloat16).astype(jnp.float32)
        for side in range(2):
            stats = [as_row(x, picks[side]) for x in (top, high, total - high)]
            stats = jnp.concatenate(stats + [jnp.zeros((13, 128), jnp.float32)], axis=0)
            at = side * groups + g
            out_ref[at, :128] = values[:, side].reshape(128, HEAD_SIZE).astype(jnp.bfloat16)
            out_ref[at, 128:] = stats.astype(jnp.bfloat16)


def factors_of(stats):
    top = stats[0][0:1]
    for part in stats[1:]:
        top = jnp.maximum(top, part[0:1])
    factors = [jnp.exp2(part[0:1] - top) for part in stats]
    total = factors[0] * (stats[0][1:2] + stats[0][2:3])
    for factor, part in zip(factors[1:], stats[1:]):
        total = total + factor * (part[1:2] + part[2:3])
    return factors, top, total


def pack_kernel(where_ref, part_ref, nk_ref, nv_ref, out_ref):
    tokens = nk_ref.shape[0]
    count = part_ref.shape[0]

    @pl.when(where_ref[1] == 0)
    def _():
        out_ref[:tokens] = nk_ref[...]

    @pl.when(where_ref[1] != 0)
    def _():
        out_ref[:tokens] = nv_ref[...]

    factors, top, total = factors_of(
        [part_ref[d, 128:].astype(jnp.float32) for d in range(count)]
    )
    columns = jnp.concatenate(factors, axis=0).T
    acc = jnp.zeros((128, HEAD_SIZE), jnp.float32)
    for d in range(count):
        acc = acc + part_ref[d, :128].astype(jnp.float32) * columns[:, d : d + 1]
    out_ref[tokens : tokens + 128] = acc.astype(jnp.bfloat16)
    high = total.astype(jnp.bfloat16).astype(jnp.float32)
    stats = [top, high, total - high, jnp.zeros((13, 128), jnp.float32)]
    out_ref[tokens + 128 :] = jnp.concatenate(stats, axis=0).astype(jnp.bfloat16)


def half_kernel(all_ref, out_ref):
    tokens = out_ref.shape[1]
    for d in range(out_ref.shape[0]):
        out_ref[d] = all_ref[d, :tokens]


def finish_kernel(all_ref, out_ref):
    count = all_ref.shape[0]
    begin = all_ref.shape[1] - 144
    sides = []
    for side in range(2):
        parts = range(side, count, 2)
        factors, _, total = factors_of(
            [all_ref[d, begin + 128 :].astype(jnp.float32) for d in parts]
        )
        columns = jnp.concatenate([factor / total for factor in factors], axis=0)
        columns = columns.T
        acc = jnp.zeros((128, HEAD_SIZE), jnp.float32)
        for i, d in enumerate(parts):
            part = all_ref[d, begin : begin + 128].astype(jnp.float32)
            acc = acc + part * columns[:, i : i + 1]
        sides.append(acc.reshape(16, 8, HEAD_SIZE))
    value = jnp.stack(sides, axis=1).reshape(256, HEAD_SIZE).astype(jnp.bfloat16)
    for d in range(out_ref.shape[0]):
        out_ref[d] = value


def prefill_kernel(
    where_ref, page_ref, q_ref, a_own, b_own, a_peer, b_peer, out_ref, pk_ref, pv_ref, qs, acc, top
):
    outs = (out_ref, pk_ref, pv_ref, qs, acc, top)

    @pl.when(where_ref[3] == 0)
    def _():
        attend(where_ref, page_ref, q_ref, a_own, b_own, a_peer, b_peer, *outs)

    @pl.when(where_ref[3] != 0)
    def _():
        attend(where_ref, page_ref, q_ref, b_own, a_own, b_peer, a_peer, *outs)


def attend(where_ref, page_ref, q_ref, k_own, v_own, k_peer, v_peer, out_ref, pk_ref, pv_ref, qs, acc, top):
    ctx, core, bound = where_ref[0], where_ref[1], where_ref[2]
    tokens = q_ref.shape[0]
    heads = q_ref.shape[1] // HEAD_SIZE
    ring = k_own.shape[0]
    blocks_per = min(4, ring)
    block = 2 * blocks_per * tokens
    row_block = 2 * tokens
    for s in range(pk_ref.shape[0]):
        source = page_ref[s] // (tokens // PAGE_TOKENS)
        z = source // 2
        row = (page_ref[s] - source * (tokens // PAGE_TOKENS)) * PAGE_TOKENS
        row = pl.multiple_of(row, PAGE_TOKENS)
        is_own = source % 2 == core

        @pl.when(is_own)
        def _():
            pk_ref[s] = k_own[z, pl.ds(row, PAGE_TOKENS), :]
            pv_ref[s] = v_own[z, pl.ds(row, PAGE_TOKENS), :]

        @pl.when(jnp.logical_not(is_own))
        def _():
            pk_ref[s] = k_peer[z, pl.ds(row, PAGE_TOKENS), :]
            pv_ref[s] = v_peer[z, pl.ds(row, PAGE_TOKENS), :]

    for h in range(heads):
        qs[h * tokens : (h + 1) * tokens] = q_ref[:, h * HEAD_SIZE : (h + 1) * HEAD_SIZE]
    acc[...] = jnp.zeros_like(acc)
    top[...] = jnp.full_like(top, NEG_FILL)
    first = ctx * tokens
    q_pos = first + lax.broadcasted_iota(jnp.int32, (row_block, 1), 0) % tokens
    begin = jnp.where(q_pos < bound, 0, bound)
    col = lax.broadcasted_iota(jnp.int32, (1, block), 1)
    piece = col // tokens
    side = jnp.where(piece < blocks_per, core, 1 - core)
    key_pos0 = (2 * (piece % blocks_per) + side) * tokens + col % tokens
    ones = jnp.ones((block, HEAD_SIZE), jnp.bfloat16)
    lowest = jnp.where(first < bound, 0, bound) // (2 * tokens)
    steps = (ctx // 2 - lowest) // blocks_per + 1

    def one(step, carry):
        low = lowest + step * blocks_per
        places = [jnp.minimum(low + i, ring - 1) for i in range(blocks_per)]
        k = jnp.concatenate([ref[z] for ref in (k_own, k_peer) for z in places], axis=0)
        v = jnp.concatenate([ref[z] for ref in (v_own, v_peer) for z in places], axis=0)
        v = jnp.concatenate([v, ones], axis=1)
        key_pos = key_pos0 + low * (2 * tokens)
        bias = jnp.where((key_pos <= q_pos) & (key_pos >= begin), 0.0, NEG_FILL)
        for b in range(heads * tokens // row_block):
            rows_b = slice(b * row_block, (b + 1) * row_block)
            s = dot_t(qs[rows_b], k) * LOG2_SCALE + bias
            before = top[rows_b]
            after = jnp.maximum(before, jnp.max(s, axis=1, keepdims=True))
            p = jnp.exp2(s - after).astype(jnp.bfloat16)
            acc[rows_b] = acc[rows_b] * jnp.exp2(before - after) + dot(p, v)
            top[rows_b] = after
        return carry

    lax.fori_loop(0, steps, one, 0)
    for h in range(heads):
        rows_h = slice(h * tokens, (h + 1) * tokens)
        out_ref[:, h * HEAD_SIZE : (h + 1) * HEAD_SIZE] = (
            acc[rows_h, :HEAD_SIZE] / acc[rows_h, HEAD_SIZE:]
        ).astype(jnp.bfloat16)


def place_kernel(in_ref, out_ref):
    for g in range(in_ref.shape[0]):
        for h in range(out_ref.shape[1] // HEAD_SIZE):
            out_ref[16 * g : 16 * g + 16, h * HEAD_SIZE : (h + 1) * HEAD_SIZE] = in_ref[
                g, 16 * h : 16 * h + 16
            ]


def local(
    new_queries,
    new_keys,
    new_values,
    segment_ids,
    page_table,
    decode_query_rows,
    resident_keys,
    resident_values,
    res_len,
):
    bf = jnp.bfloat16
    tokens = new_keys.shape[0]
    ring = lax.axis_size("far") * 2
    far, near, core, grp = (lax.axis_index(a) for a in ("far", "near", "core", "grp"))
    ctx = (far * 2 + near) * 2 + core
    rows, width = decode_query_rows.shape
    queries = 16 * (width // HEAD_SIZE)
    res_rows = resident_keys.shape[1]
    pages = tokens // PAGE_TOKENS
    i32 = jnp.int32

    where_a = jnp.stack([(ctx * 2 + grp) * res_rows, grp, jnp.int32(tokens // 2)]).astype(i32)
    groups = rows // 16
    part = pl.pallas_call(
        partial_kernel,
        out_shape=jax.ShapeDtypeStruct((2 * groups, 144, HEAD_SIZE), bf),
        in_specs=[SMEM, SMEM] + [HBM] * 5,
        out_specs=VMEM,
        scratch_shapes=[
            pltpu.VMEM(decode_query_rows.shape, bf),
            pltpu.VMEM(resident_keys.shape, bf),
            pltpu.VMEM(resident_values.shape, bf),
            pltpu.VMEM(new_keys.shape, bf),
            pltpu.VMEM(new_values.shape, bf),
            pltpu.SemaphoreType.DMA((3 * groups + 2,)),
        ],
        compiler_params=pltpu.CompilerParams(vmem_limit_bytes=63 * 1024 * 1024),
    )(res_len, where_a, decode_query_rows, resident_keys, resident_values, new_keys, new_values)
    bound = jnp.sum((segment_ids == 0).astype(i32))
    slots = ctx * pages + jnp.arange(pages, dtype=i32)
    ids = jnp.arange(page_table.shape[0], dtype=i32)
    page_from = jnp.sum(jnp.where(page_table[None, :] == slots[:, None], ids[None, :], 0), axis=1)
    where_b = jnp.stack([ctx, core, bound, grp]).astype(i32)
    part = lax.all_to_all(part, ("near", "core", "grp"), 0, 0, tiled=True)
    part, where_b, page_from = lax.optimization_barrier((part, where_b, page_from))
    packed = pl.pallas_call(
        pack_kernel,
        out_shape=jax.ShapeDtypeStruct((tokens + 144, HEAD_SIZE), bf),
        in_specs=[SMEM] + [VMEM] * 3,
        out_specs=VMEM,
        compiler_params=PARAMS,
    )(where_a, part, new_keys, new_values)
    gathered = lax.all_gather(packed, ("far", "near"), axis=0)
    swap = [(0, 1), (1, 0)]
    a_own = pl.pallas_call(
        half_kernel,
        out_shape=jax.ShapeDtypeStruct((ring, tokens, HEAD_SIZE), bf),
        in_specs=[VMEM],
        out_specs=VMEM,
        compiler_params=PARAMS,
    )(gathered)
    b_own = lax.ppermute(a_own, "grp", swap)
    a_peer = lax.ppermute(a_own, "core", swap)
    dec = pl.pallas_call(
        finish_kernel,
        out_shape=jax.ShapeDtypeStruct((groups, queries, HEAD_SIZE), bf),
        in_specs=[VMEM],
        out_specs=VMEM,
        compiler_params=PARAMS,
    )(gathered)
    b_peer = lax.ppermute(lax.optimization_barrier((b_own, dec))[0], "core", swap)
    dec = lax.all_to_all(dec, ("core", "grp"), 0, 0, tiled=True)

    prefill_out, paged_keys, paged_values = pl.pallas_call(
        prefill_kernel,
        out_shape=(
            jax.ShapeDtypeStruct(new_queries.shape, bf),
            jax.ShapeDtypeStruct((pages, PAGE_TOKENS, HEAD_SIZE), bf),
            jax.ShapeDtypeStruct((pages, PAGE_TOKENS, HEAD_SIZE), bf),
        ),
        in_specs=[SMEM, SMEM] + [VMEM] * 5,
        out_specs=(VMEM,) * 3,
        scratch_shapes=[
            pltpu.VMEM((tokens * (new_queries.shape[1] // HEAD_SIZE), HEAD_SIZE), bf),
            pltpu.VMEM(
                (tokens * (new_queries.shape[1] // HEAD_SIZE), 2 * HEAD_SIZE), jnp.float32
            ),
            pltpu.VMEM((tokens * (new_queries.shape[1] // HEAD_SIZE), 1), jnp.float32),
        ],
        compiler_params=PARAMS,
    )(where_b, page_from, new_queries, a_own, b_own, a_peer, b_peer)

    dec = lax.optimization_barrier((dec, paged_keys))[0]
    decode_out = pl.pallas_call(
        place_kernel,
        out_shape=jax.ShapeDtypeStruct((rows, width), bf),
        in_specs=[VMEM],
        out_specs=VMEM,
        compiler_params=PARAMS,
    )(dec)
    return (prefill_out, paged_keys, paged_values, decode_out)


def solution(mesh):
    sizes = mesh.shape
    fine = Mesh(
        np.asarray(mesh.devices).reshape(
            sizes["ctx"] // 4, 2, 2, sizes["head"], sizes["grp"]
        ),
        ("far", "near", "core", "head", "grp"),
    )
    ctx = ("far", "near", "core")
    return jax.shard_map(
        local,
        mesh=fine,
        in_specs=(
            P(ctx, ("head", "grp")),
            P(ctx, "head"),
            P(ctx, "head"),
            P(),
            P(),
            P(None, "head"),
            P(None, ctx + ("grp",), "head"),
            P(None, ctx + ("grp",), "head"),
            P(),
        ),
        out_specs=(
            P(ctx, ("head", "grp")),
            P(ctx, None, "head"),
            P(ctx, None, "head"),
            P(None, "head"),
        ),
        check_vma=False,
    )
```

time: 93.1 us -> 81.5 us (0.88)
  blocking collectives: 48 us -> 28.9 us
  starting transfers between devices: 25.8 us -> 31.6 us
    all_to_all x1 -> x0, blocking collectives: 21.3 us -> none  [local(): part = lax.all_to_all(part, 'z', 0, 0, tiled=True)]
    ppermute x1 -> x3, starting transfers between devices: 12 us -> 17.9 us  [the longest x1 9.66 us: local(): a_peer = lax.ppermute(a_own, 'core', swap)]
    all_gather x1, blocking collectives: 26.7 us -> 28.9 us  [local(): gathered = lax.all_gather(packed, ('far', 'near'), axis=0)]
  transfers between devices with their start and end apart: 3 -> 5, of which waited for: 2 -> 2; matrix products, arithmetic and copies ran while one was open for 2% -> 2% of each run, Pallas kernels for 4% -> 5%
where the time goes in v4:
time: 81.5 us; the launch traced here: 81 us
  starting transfers between devices  31.6 us (39%)
  blocking collectives  28.9 us (35%)
  Pallas kernels  10.8 us (13%)
  waiting for transfers between devices  6.7 us (8%)
  other arithmetic  2.13 us (3%)
    all_gather x1, blocking collectives, local(): gathered = lax.all_gather(packed, ('far', 'near'), axis=0)  28.9 us
    all_to_all x1, starting transfers between devices, local(): part = lax.all_to_all(part, ('near', 'core', 'grp'), 0, 0, tiled=True)  10.4 us
    ppermute x1, starting transfers between devices, local(): a_peer = lax.ppermute(a_own, 'core', swap)  9.66 us
    ppermute x1, starting transfers between devices, local(): lax.ppermute(lax.optimization_barrier((b_own, dec))[0], 'core', swap)  5.93 us
    pallas_call x1, Pallas kernels, local(): pl.pallas_call(partial_kernel, out_shape=jax.ShapeDtypeStruct((2 * groups...  4.87 us
    all_to_all x1, waiting for transfers between devices, local(): part = lax.all_to_all(part, ('near', 'core', 'grp'), 0, 0, tiled=True)  4.66 us
    all_to_all x1, starting transfers between devices, local(): dec = lax.all_to_all(dec, ('core', 'grp'), 0, 0, tiled=True)  3.41 us
    pallas_call x1, Pallas kernels, local(): pl.pallas_call(prefill_kernel, out_shape=(jax.ShapeDtypeStruct(new_querie...  3.09 us
  transfers between devices with their start and end apart: 5, of which 2 were waited for; matrix products, arithmetic and copies ran while one was open for 2% of the time, Pallas kernels for 5%

profile of v4, /device:TPU:1, one launch (start us, length us, event | category | flops | bytes accessed | tf_op | source)
XLA Modules:
  0.0 81.0 jit_solution(9863240726485342373)
XLA Ops:
  0.6 0.6 pad_add_fusion.where_ref
  1.2 4.9 %shard_map.120 = bf16[8,144,128]{2,1,0:T(8,128)(2,1)} custom-call(s32[64]{0:T(128)} %len_ref.1, s32[3]{0:T(128)} %pad_add_fusion.where_ref, bf16[64,2048]{1,0:T(8,128)(2,1)} %dq_hbm.1, bf16[64,32,128]{2,1,0:T(8,128)(2,1)} %rk_hbm.1, bf16[64,32,128]{2,1,0:T(8,128)(2,1)} %rv_hbm.1, bf16[96,128]{1,0:T(8,128)(2,1)} %nk_ref.1, bf16[96,128]{1,0:T(8,128)(2,1)} %nv_ref.1), custom_call_target="tpu_custom_call" | custom-call | tf_op jit(solution)/shard_map/pallas_call | solution.py:277
  6.1 0.0 copy-start.4
  6.1 0.0 copy-start.5
  6.1 0.0 copy-start.2
  6.2 10.4 %all-to-all-start = ((bf16[8,144,128]{2,1,0:T(8,128)(2,1)}), bf16[8,144,128]{2,1,0:T(8,128)(2,1)S(1)}, u32[]{:S(2)}, u32[]{:S(2)}) async-start(bf16[8,144,128]{2,1,0:T(8,128)(2,1)} %shard_map.120), calls=%async_computation | async-start | bytes 589824 | tf_op jit(solution)/shard_map/all_to_all | solution.py:297
  16.5 0.0 copy-start.1
  16.5 0.0 copy-done.4
  16.5 0.6 convert_reduce_fusion
  17.2 0.7 pad_add_fusion.1.where_ref
  17.9 0.0 copy-done.5
  17.9 0.0 copy-start.3
  17.9 0.2 select_reduce_fusion.page_ref
  18.1 4.7 %all-to-all-done.part_ref = bf16[8,144,128]{2,1,0:T(8,128)(2,1)S(1)} async-done(((bf16[8,144,128]{2,1,0:T(8,128)(2,1)}), bf16[8,144,128]{2,1,0:T(8,128)(2,1)S(1)}, u32[]{:S(2)}, u32[]{:S(2)}) %all-to-all-start) | async-done | bytes 294944 | tf_op jit(solution)/shard_map/all_to_all | solution.py:297
  22.7 0.0 copy-done.2
  22.7 0.0 copy-done.1
  22.7 0.0 copy-done.3
  22.7 0.9 %shard_map.121 = bf16[240,128]{1,0:T(8,128)(2,1)S(1)} custom-call(s32[3]{0:T(128)S(1)} %copy-done.3, bf16[8,144,128]{2,1,0:T(8,128)(2,1)S(1)} %all-to-all-done.part_ref, bf16[96,128]{1,0:T(8,128)(2,1)S(1)} %copy-done.1, bf16[96,128]{1,0:T(8,128)(2,1)S(1)} %copy-done.2), custom_call_target="tpu_custom_call" | custom-call | tf_op jit(solution)/shard_map/pallas_call | solution.py:299
  23.7 28.9 %all-gather = bf16[3840,128]{1,0:T(8,128)(2,1)S(1)} all-gather(bf16[240,128]{1,0:T(8,128)(2,1)S(1)} %shard_map.121), channel_id=2, replica_groups=mesh['far'=8,'near'=2,'core'=2,'head'=8,'grp'=2] {'far','near'}, dimensions={0}, use_global_device_ids=true | all-gather | bytes 1044480 | tf_op jit(solution)/shard_map/all_gather | solution.py:306
  52.6 2.3 %collective-permute-start = (bf16[16,96,128]{2,1,0:T(8,128)(2,1)S(1)}, bf16[16,96,128]{2,1,0:T(8,128)(2,1)S(1)}, u32[]{:S(2)}, u32[]{:S(2)}) collective-permute-start(bf16[16,96,128]{2,1,0:T(8,128)(2,1)S(1)} %shard_map.122.a_own), channel_id=1, source_target_pairs={{0,1},{1,0},{2,3},{3,2},{4,5},{5,4},{6,7},{7,6},{8,9},{9,8},{10,11... | collective-permute-start | bytes 1179656 | tf_op jit(solution)/shard_map/ppermute | solution.py:315
  54.9 1.2 %shard_map.123 = bf16[4,256,128]{2,1,0:T(8,128)(2,1)} custom-call(bf16[16,240,128]{2,1,0:T(8,128)(2,1)S(1)} %bitcast.7), custom_call_target="tpu_custom_call" | custom-call | tf_op jit(solution)/shard_map/pallas_call | solution.py:317
  56.1 0.0 copy-start
  56.1 9.7 %collective-permute-start.1 = (bf16[16,96,128]{2,1,0:T(8,128)(2,1)S(1)}, bf16[16,96,128]{2,1,0:T(8,128)(2,1)S(1)}, u32[]{:S(2)}, u32[]{:S(2)}) collective-permute-start(bf16[16,96,128]{2,1,0:T(8,128)(2,1)S(1)} %shard_map.122.a_own), channel_id=1, source_target_pairs={{0,16},{16,0},{1,17},{17,1},{2,18},{18,2},{3,19},{19,3},{4,20},{20... | collective-permute-start | bytes 1179656 | tf_op jit(solution)/shard_map/ppermute | solution.py:316
  65.7 0.0 collective-permute-done.b_own
  65.8 5.9 %collective-permute-start.2 = (bf16[16,96,128]{2,1,0:T(8,128)(2,1)S(1)}, bf16[16,96,128]{2,1,0:T(8,128)(2,1)S(1)}, u32[]{:S(2)}, u32[]{:S(2)}) collective-permute-start(bf16[16,96,128]{2,1,0:T(8,128)(2,1)S(1)} %collective-permute-done.b_own), channel_id=1, source_target_pairs={{0,16},{16,0},{1,17},{17,1},{2,18},{18,2},{3,19},{19,3},{4,20},{20... | collective-permute-start | bytes 1179656 | tf_op jit(solution)/shard_map/ppermute | solution.py:324
  71.7 3.4 %all-to-all-start.1 = ((bf16[4,256,128]{2,1,0:T(8,128)(2,1)}), bf16[4,256,128]{2,1,0:T(8,128)(2,1)S(1)}, u32[]{:S(2)}, u32[]{:S(2)}) async-start(bf16[4,256,128]{2,1,0:T(8,128)(2,1)} %shard_map.123), calls=%async_computation.1 | async-start | bytes 524288 | tf_op jit(solution)/shard_map/all_to_all | solution.py:325
  75.1 0.0 collective-permute-done.1.a_peer
  75.1 0.0 collective-permute-done.2.b_peer
  75.1 0.0 copy-done
  75.1 3.1 %shard_map.124 = (bf16[96,1024]{1,0:T(8,128)(2,1)}, bf16[6,16,128]{2,1,0:T(8,128)(2,1)}, bf16[6,16,128]{2,1,0:T(8,128)(2,1)}) custom-call(s32[4]{0:T(128)S(1)} %pad_add_fusion.1.where_ref, s32[6]{0:T(128)S(1)} %select_reduce_fusion.page_ref, bf16[96,1024]{1,0:T(8,128)(2,1)S(1)} %copy-done, bf16[16,96,128]{2,1,0:T(8,128)(2,1)S(1)} %shard_map.122.a_own, ...), custom_call_target="tpu_custom_call" | custom-call | tf_op jit(solution)/shard_map/pallas_call | solution.py:327
  78.2 2.0 %all-to-all-done.1.in_ref = bf16[4,256,128]{2,1,0:T(8,128)(2,1)S(1)} async-done(((bf16[4,256,128]{2,1,0:T(8,128)(2,1)}), bf16[4,256,128]{2,1,0:T(8,128)(2,1)S(1)}, u32[]{:S(2)}, u32[]{:S(2)}) %all-to-all-start.1) | async-done | bytes 262176 | tf_op jit(solution)/shard_map/all_to_all | solution.py:325
  80.3 0.7 shard_map.125
  (2 shorter events, 0.0 us)
Async XLA Ops:
  6.1 10.4 %copy-start.4 = (s32[3072]{0:T(1024)S(1)}, s32[3072]{0:T(1024)}, u32[]{:S(2)}) copy-start(s32[3072]{0:T(1024)} %param.12) | copy-start | bytes 36868
  6.1 11.8 %copy-start.5 = (s32[192]{0:T(256)S(1)}, s32[192]{0:T(256)}, u32[]{:S(2)}) copy-start(s32[192]{0:T(256)} %param.13) | copy-start | bytes 2308
  6.1 16.6 %copy-start.2 = (bf16[96,128]{1,0:T(8,128)(2,1)S(1)}, bf16[96,128]{1,0:T(8,128)(2,1)}, u32[]{:S(2)}) copy-start(bf16[96,128]{1,0:T(8,128)(2,1)} %nv_ref.1) | copy-start | bytes 73732
  6.2 16.6 %all-to-all-start = ((bf16[8,144,128]{2,1,0:T(8,128)(2,1)}), bf16[8,144,128]{2,1,0:T(8,128)(2,1)S(1)}, u32[]{:S(2)}, u32[]{:S(2)}) async-start(bf16[8,144,128]{2,1,0:T(8,128)(2,1)} %shard_map.120), calls=%async_computation | async-start | bytes 589824 | tf_op jit(solution)/shard_map/all_to_all | solution.py:297
  16.5 6.2 %copy-start.1 = (bf16[96,128]{1,0:T(8,128)(2,1)S(1)}, bf16[96,128]{1,0:T(8,128)(2,1)}, u32[]{:S(2)}) copy-start(bf16[96,128]{1,0:T(8,128)(2,1)} %nk_ref.1) | copy-start | bytes 73732
  17.9 4.9 %copy-start.3 = (s32[3]{0:T(128)S(1)}, s32[3]{0:T(128)}, u32[]{:S(2)}) copy-start(s32[3]{0:T(128)} %pad_add_fusion.where_ref) | copy-start | bytes 40
  52.6 13.2 %collective-permute-start = (bf16[16,96,128]{2,1,0:T(8,128)(2,1)S(1)}, bf16[16,96,128]{2,1,0:T(8,128)(2,1)S(1)}, u32[]{:S(2)}, u32[]{:S(2)}) collective-permute-start(bf16[16,96,128]{2,1,0:T(8,128)(2,1)S(1)} %shard_map.122.a_own), channel_id=1, source_target_pairs={{0,1},{1,0},{2,3},{3,2},{4,5},{5,4},{6,7},{7,6},{8,9},{9,8},{10,11... | collective-permute-start | bytes 1179656 | tf_op jit(solution)/shard_map/ppermute | solution.py:315
  56.1 19.1 %copy-start = (bf16[96,1024]{1,0:T(8,128)(2,1)S(1)}, bf16[96,1024]{1,0:T(8,128)(2,1)}, u32[]{:S(2)}) copy-start(bf16[96,1024]{1,0:T(8,128)(2,1)} %q_ref.1) | copy-start | bytes 589828
  56.1 19.0 %collective-permute-start.1 = (bf16[16,96,128]{2,1,0:T(8,128)(2,1)S(1)}, bf16[16,96,128]{2,1,0:T(8,128)(2,1)S(1)}, u32[]{:S(2)}, u32[]{:S(2)}) collective-permute-start(bf16[16,96,128]{2,1,0:T(8,128)(2,1)S(1)} %shard_map.122.a_own), channel_id=1, source_target_pairs={{0,16},{16,0},{1,17},{17,1},{2,18},{18,2},{3,19},{19,3},{4,20},{20... | collective-permute-start | bytes 1179656 | tf_op jit(solution)/shard_map/ppermute | solution.py:316
  65.8 9.4 %collective-permute-start.2 = (bf16[16,96,128]{2,1,0:T(8,128)(2,1)S(1)}, bf16[16,96,128]{2,1,0:T(8,128)(2,1)S(1)}, u32[]{:S(2)}, u32[]{:S(2)}) collective-permute-start(bf16[16,96,128]{2,1,0:T(8,128)(2,1)S(1)} %collective-permute-done.b_own), channel_id=1, source_target_pairs={{0,16},{16,0},{1,17},{17,1},{2,18},{18,2},{3,19},{19,3},{4,20},{20... | collective-permute-start | bytes 1179656 | tf_op jit(solution)/shard_map/ppermute | solution.py:324
  71.7 8.6 %all-to-all-start.1 = ((bf16[4,256,128]{2,1,0:T(8,128)(2,1)}), bf16[4,256,128]{2,1,0:T(8,128)(2,1)S(1)}, u32[]{:S(2)}, u32[]{:S(2)}) async-start(bf16[4,256,128]{2,1,0:T(8,128)(2,1)} %shard_map.123), calls=%async_computation.1 | async-start | bytes 524288 | tf_op jit(solution)/shard_map/all_to_all | solution.py:325

commit v5 on v4

--- a/solution.py
+++ b/solution.py
@@ -114,13 +114,13 @@
     tokens = nk_ref.shape[0]
     count = part_ref.shape[0]
 
-    @pl.when(where_ref[1] == 0)
-    def _():
-        out_ref[:tokens] = nk_ref[...]
-
-    @pl.when(where_ref[1] != 0)
-    def _():
-        out_ref[:tokens] = nv_ref[...]
+    half = tokens // 2
+    for side in range(2):
+
+        @pl.when(where_ref[1] == side)
+        def _():
+            out_ref[:half] = nk_ref[side * half : (side + 1) * half]
+            out_ref[half:tokens] = nv_ref[side * half : (side + 1) * half]
 
     factors, top, total = factors_of(
         [part_ref[d, 128:].astype(jnp.float32) for d in range(count)]
@@ -135,15 +135,11 @@
     out_ref[tokens + 128 :] = jnp.concatenate(stats, axis=0).astype(jnp.bfloat16)
 
 
-def half_kernel(all_ref, out_ref):
-    tokens = out_ref.shape[1]
-    for d in range(out_ref.shape[0]):
-        out_ref[d] = all_ref[d, :tokens]
-
-
 def finish_kernel(all_ref, out_ref):
     count = all_ref.shape[0]
     begin = all_ref.shape[1] - 144
+    for d in range(count):
+        out_ref[begin * d : begin * (d + 1)] = all_ref[d, :begin]
     sides = []
     for side in range(2):
         parts = range(side, count, 2)
@@ -158,73 +154,49 @@
             acc = acc + part * columns[:, i : i + 1]
         sides.append(acc.reshape(16, 8, HEAD_SIZE))
     value = jnp.stack(sides, axis=1).reshape(256, HEAD_SIZE).astype(jnp.bfloat16)
-    for d in range(out_ref.shape[0]):
-        out_ref[d] = value
-
-
-def prefill_kernel(
-    where_ref, page_ref, q_ref, a_own, b_own, a_peer, b_peer, out_ref, pk_ref, pv_ref, qs, acc, top
-):
-    outs = (out_ref, pk_ref, pv_ref, qs, acc, top)
-
-    @pl.when(where_ref[3] == 0)
-    def _():
-        attend(where_ref, page_ref, q_ref, a_own, b_own, a_peer, b_peer, *outs)
-
-    @pl.when(where_ref[3] != 0)
-    def _():
-        attend(where_ref, page_ref, q_ref, b_own, a_own, b_peer, a_peer, *outs)
-
-
-def attend(where_ref, page_ref, q_ref, k_own, v_own, k_peer, v_peer, out_ref, pk_ref, pv_ref, qs, acc, top):
+    out_ref[begin * count :] = value
+
+
+def attend(where_ref, grp, own_ref, peer_ref, qs, acc, top):
     ctx, core, bound = where_ref[0], where_ref[1], where_ref[2]
-    tokens = q_ref.shape[0]
-    heads = q_ref.shape[1] // HEAD_SIZE
-    ring = k_own.shape[0]
-    blocks_per = min(4, ring)
-    block = 2 * blocks_per * tokens
+    tokens = 96
+    half = tokens // 2
+    ring = own_ref.shape[0] // tokens
+    blocks_per = min(8, ring)
+    block = 2 * blocks_per * half
     row_block = 2 * tokens
-    for s in range(pk_ref.shape[0]):
-        source = page_ref[s] // (tokens // PAGE_TOKENS)
-        z = source // 2
-        row = (page_ref[s] - source * (tokens // PAGE_TOKENS)) * PAGE_TOKENS
-        row = pl.multiple_of(row, PAGE_TOKENS)
-        is_own = source % 2 == core
-
-        @pl.when(is_own)
-        def _():
-            pk_ref[s] = k_own[z, pl.ds(row, PAGE_TOKENS), :]
-            pv_ref[s] = v_own[z, pl.ds(row, PAGE_TOKENS), :]
-
-        @pl.when(jnp.logical_not(is_own))
-        def _():
-            pk_ref[s] = k_peer[z, pl.ds(row, PAGE_TOKENS), :]
-            pv_ref[s] = v_peer[z, pl.ds(row, PAGE_TOKENS), :]
-
-    for h in range(heads):
-        qs[h * tokens : (h + 1) * tokens] = q_ref[:, h * HEAD_SIZE : (h + 1) * HEAD_SIZE]
-    acc[...] = jnp.zeros_like(acc)
-    top[...] = jnp.full_like(top, NEG_FILL)
     first = ctx * tokens
     q_pos = first + lax.broadcasted_iota(jnp.int32, (row_block, 1), 0) % tokens
     begin = jnp.where(q_pos < bound, 0, bound)
     col = lax.broadcasted_iota(jnp.int32, (1, block), 1)
-    piece = col // tokens
+    piece = col // half
     side = jnp.where(piece < blocks_per, core, 1 - core)
-    key_pos0 = (2 * (piece % blocks_per) + side) * tokens + col % tokens
+    key_pos0 = (2 * (piece % blocks_per) + side) * tokens + grp * half + col % half
     ones = jnp.ones((block, HEAD_SIZE), jnp.bfloat16)
     lowest = jnp.where(first < bound, 0, bound) // (2 * tokens)
     steps = (ctx // 2 - lowest) // blocks_per + 1
 
     def one(step, carry):
         low = lowest + step * blocks_per
-        places = [jnp.minimum(low + i, ring - 1) for i in range(blocks_per)]
-        k = jnp.concatenate([ref[z] for ref in (k_own, k_peer) for z in places], axis=0)
-        v = jnp.concatenate([ref[z] for ref in (v_own, v_peer) for z in places], axis=0)
+        places = [
+            pl.multiple_of(jnp.minimum(low + i, ring - 1) * tokens, PAGE_TOKENS)
+            for i in range(blocks_per)
+        ]
+        k = jnp.concatenate(
+            [ref[pl.ds(z, half), :] for ref in (own_ref, peer_ref) for z in places], axis=0
+        )
+        v = jnp.concatenate(
+            [
+                ref[pl.ds(pl.multiple_of(z + half, PAGE_TOKENS), half), :]
+                for ref in (own_ref, peer_ref)
+                for z in places
+            ],
+            axis=0,
+        )
         v = jnp.concatenate([v, ones], axis=1)
         key_pos = key_pos0 + low * (2 * tokens)
         bias = jnp.where((key_pos <= q_pos) & (key_pos >= begin), 0.0, NEG_FILL)
-        for b in range(heads * tokens // row_block):
+        for b in range(qs.shape[0] // row_block):
             rows_b = slice(b * row_block, (b + 1) * row_block)
             s = dot_t(qs[rows_b], k) * LOG2_SCALE + bias
             before = top[rows_b]
@@ -235,19 +207,61 @@
         return carry
 
     lax.fori_loop(0, steps, one, 0)
+
+
+def first_kernel(where_ref, q_ref, own_ref, peer_ref, qs, acc, top):
+    tokens = q_ref.shape[0]
+    for h in range(q_ref.shape[1] // HEAD_SIZE):
+        qs[h * tokens : (h + 1) * tokens] = q_ref[:, h * HEAD_SIZE : (h + 1) * HEAD_SIZE]
+    acc[...] = jnp.zeros_like(acc)
+    top[...] = jnp.full_like(top, NEG_FILL)
+    attend(where_ref, where_ref[3], own_ref, peer_ref, qs, acc, top)
+
+
+def second_kernel(
+    where_ref, page_ref, a_own, a_peer, b_own, b_peer, qs, acc_in, top_in,
+    out_ref, pk_ref, pv_ref, dec_ref, acc, top,
+):
+    ctx, core, grp = where_ref[0], where_ref[1], where_ref[3]
+    tokens = out_ref.shape[0]
+    heads = out_ref.shape[1] // HEAD_SIZE
+    half = tokens // 2
+    pages = tokens // PAGE_TOKENS
+    for s in range(pk_ref.shape[0]):
+        source = page_ref[s] // pages
+        page = page_ref[s] - source * pages
+        side = page // (pages // 2)
+        row = (source // 2) * tokens + (page - side * (pages // 2)) * PAGE_TOKENS
+        row = pl.multiple_of(row, PAGE_TOKENS)
+        value_row = pl.multiple_of(row + half, PAGE_TOKENS)
+        for same_side, same_core, ref in (
+            (True, True, a_own), (True, False, a_peer), (False, True, b_own), (False, False, b_peer),
+        ):
+            there = ((side == grp) == same_side) & ((source % 2 == core) == same_core)
+
+            @pl.when(there)
+            def _():
+                pk_ref[s] = ref[pl.ds(row, PAGE_TOKENS), :]
+                pv_ref[s] = ref[pl.ds(value_row, PAGE_TOKENS), :]
+
+    columns = dec_ref.shape[1] // HEAD_SIZE
+    begin = a_own.shape[0] - 16 * columns
+    for at_core, at_grp, ref in (
+        (core, grp, a_own), (1 - core, grp, a_peer), (core, 1 - grp, b_own), (1 - core, 1 - grp, b_peer),
+    ):
+        row = pl.multiple_of((at_core * 2 + at_grp) * 16, 16)
+        for h in range(columns):
+            dec_ref[pl.ds(row, 16), h * HEAD_SIZE : (h + 1) * HEAD_SIZE] = ref[
+                begin + 16 * h : begin + 16 * h + 16
+            ]
+    acc[...] = acc_in[...]
+    top[...] = top_in[...]
+    attend(where_ref, 1 - grp, b_own, b_peer, qs, acc, top)
     for h in range(heads):
         rows_h = slice(h * tokens, (h + 1) * tokens)
         out_ref[:, h * HEAD_SIZE : (h + 1) * HEAD_SIZE] = (
             acc[rows_h, :HEAD_SIZE] / acc[rows_h, HEAD_SIZE:]
         ).astype(jnp.bfloat16)
-
-
-def place_kernel(in_ref, out_ref):
-    for g in range(in_ref.shape[0]):
-        for h in range(out_ref.shape[1] // HEAD_SIZE):
-            out_ref[16 * g : 16 * g + 16, h * HEAD_SIZE : (h + 1) * HEAD_SIZE] = in_ref[
-                g, 16 * h : 16 * h + 16
-            ]
 
 
 def local(
@@ -306,51 +320,43 @@
     gathered = lax.all_gather(packed, ("far", "near"), axis=0)
     swap = [(0, 1), (1, 0)]
     a_own = pl.pallas_call(
-        half_kernel,
-        out_shape=jax.ShapeDtypeStruct((ring, tokens, HEAD_SIZE), bf),
+        finish_kernel,
+        out_shape=jax.ShapeDtypeStruct((ring * tokens + queries, HEAD_SIZE), bf),
         in_specs=[VMEM],
         out_specs=VMEM,
         compiler_params=PARAMS,
     )(gathered)
     b_own = lax.ppermute(a_own, "grp", swap)
     a_peer = lax.ppermute(a_own, "core", swap)
-    dec = pl.pallas_call(
-        finish_kernel,
-        out_shape=jax.ShapeDtypeStruct((groups, queries, HEAD_SIZE), bf),
-        in_specs=[VMEM],
-        out_specs=VMEM,
+    b_peer = lax.ppermute(b_own, "core", swap)
+    stacked = tokens * (new_queries.shape[1] // HEAD_SIZE)
+    state = pl.pallas_call(
+        first_kernel,
+        out_shape=(
+            jax.ShapeDtypeStruct((stacked, HEAD_SIZE), bf),
+            jax.ShapeDtypeStruct((stacked, 2 * HEAD_SIZE), jnp.float32),
+            jax.ShapeDtypeStruct((stacked, 1), jnp.float32),
+        ),
+        in_specs=[SMEM] + [VMEM] * 3,
+        out_specs=(VMEM,) * 3,
         compiler_params=PARAMS,
-    )(gathered)
-    b_peer = lax.ppermute(lax.optimization_barrier((b_own, dec))[0], "core", swap)
-    dec = lax.all_to_all(dec, ("core", "grp"), 0, 0, tiled=True)
-
-    prefill_out, paged_keys, paged_values = pl.pallas_call(
-        prefill_kernel,
+    )(where_b, new_queries, a_own, a_peer)
+    prefill_out, paged_keys, paged_values, decode_out = pl.pallas_call(
+        second_kernel,
         out_shape=(
             jax.ShapeDtypeStruct(new_queries.shape, bf),
             jax.ShapeDtypeStruct((pages, PAGE_TOKENS, HEAD_SIZE), bf),
             jax.ShapeDtypeStruct((pages, PAGE_TOKENS, HEAD_SIZE), bf),
-        ),
-        in_specs=[SMEM, SMEM] + [VMEM] * 5,
-        out_specs=(VMEM,) * 3,
+            jax.ShapeDtypeStruct((rows, width), bf),
+        ),
+        in_specs=[SMEM, SMEM] + [VMEM] * 7,
+        out_specs=(VMEM,) * 4,
         scratch_shapes=[
-            pltpu.VMEM((tokens * (new_queries.shape[1] // HEAD_SIZE), HEAD_SIZE), bf),
-            pltpu.VMEM(
-                (tokens * (new_queries.shape[1] // HEAD_SIZE), 2 * HEAD_SIZE), jnp.float32
-            ),
-            pltpu.VMEM((tokens * (new_queries.shape[1] // HEAD_SIZE), 1), jnp.float32),
+            pltpu.VMEM((stacked, 2 * HEAD_SIZE), jnp.float32),
+            pltpu.VMEM((stacked, 1), jnp.float32),
         ],
         compiler_params=PARAMS,
-    )(where_b, page_from, new_queries, a_own, b_own, a_peer, b_peer)
-
-    dec = lax.optimization_barrier((dec, paged_keys))[0]
-    decode_out = pl.pallas_call(
-        place_kernel,
-        out_shape=jax.ShapeDtypeStruct((rows, width), bf),
-        in_specs=[VMEM],
-        out_specs=VMEM,
-        compiler_params=PARAMS,
-    )(dec)
+    )(where_b, page_from, a_own, a_peer, b_own, b_peer, *state)
     return (prefill_out, paged_keys, paged_values, decode_out)
 
 

time: 81.5 us -> 78.7 us (0.966)
  waiting for transfers between devices: 6.7 us -> 4.67 us
  starting transfers between devices: 31.6 us -> 30.1 us
    all_to_all x1 -> x0, starting transfers between devices: 3.41 us -> none  [local(): dec = lax.all_to_all(dec, ('core', 'grp'), 0, 0, tiled=True)]
    ppermute x1, starting transfers between devices: 5.93 us -> 7.96 us  [local(): b_peer = lax.ppermute(b_own, 'core', swap)]
    all_to_all x1 -> x0, waiting for transfers between devices: 2.03 us -> none  [local(): dec = lax.all_to_all(dec, ('core', 'grp'), 0, 0, tiled=True)]
    pallas_call x4 -> x3, Pallas kernels: 5.07 us -> 5.88 us  [the longest x1 3.23 us: local(): pl.pallas_call(second_kernel, out_shape=(jax.ShapeDtypeStruct(new_queries...]
  transfers between devices with their start and end apart: 5 -> 4, of which waited for: 2 -> 1; matrix products, arithmetic and copies ran while one was open for 2% -> 2% of each run, Pallas kernels for 5% -> 3%
where the time goes in v5:
time: 78.7 us; the launch traced here: 78.3 us
  starting transfers between devices  30.1 us (38%)
  blocking collectives  28.9 us (37%)
  Pallas kernels  11.6 us (15%)
  waiting for transfers between devices  4.67 us (6%)
  other arithmetic  2.14 us (3%)
    all_gather x1, blocking collectives, local(): gathered = lax.all_gather(packed, ('far', 'near'), axis=0)  28.9 us
    all_to_all x1, starting transfers between devices, local(): part = lax.all_to_all(part, ('near', 'core', 'grp'), 0, 0, tiled=True)  10.4 us
    ppermute x1, starting transfers between devices, local(): a_peer = lax.ppermute(a_own, 'core', swap)  9.54 us
    ppermute x1, starting transfers between devices, local(): b_peer = lax.ppermute(b_own, 'core', swap)  7.96 us
    pallas_call x1, Pallas kernels, local(): pl.pallas_call(partial_kernel, out_shape=jax.ShapeDtypeStruct((2 * groups...  4.86 us
    all_to_all x1, waiting for transfers between devices, local(): part = lax.all_to_all(part, ('near', 'core', 'grp'), 0, 0, tiled=True)  4.66 us
    pallas_call x1, Pallas kernels, local(): pl.pallas_call(second_kernel, out_shape=(jax.ShapeDtypeStruct(new_queries...  3.23 us
    ppermute x1, starting transfers between devices, local(): b_own = lax.ppermute(a_own, 'grp', swap)  2.28 us
  transfers between devices with their start and end apart: 4, of which 1 were waited for; matrix products, arithmetic and copies ran while one was open for 2% of the time, Pallas kernels for 3%

profile of v5, /device:TPU:1, one launch (start us, length us, event | category | flops | bytes accessed | tf_op | source)
XLA Modules:
  0.0 78.3 jit_solution(7206406659908756862)
XLA Ops:
  0.6 0.6 pad_add_fusion.where_ref
  1.2 4.9 %shard_map.120 = bf16[8,144,128]{2,1,0:T(8,128)(2,1)} custom-call(s32[64]{0:T(128)} %len_ref.1, s32[3]{0:T(128)} %pad_add_fusion.where_ref, bf16[64,2048]{1,0:T(8,128)(2,1)} %dq_hbm.1, bf16[64,32,128]{2,1,0:T(8,128)(2,1)} %rk_hbm.1, bf16[64,32,128]{2,1,0:T(8,128)(2,1)} %rv_hbm.1, bf16[96,128]{1,0:T(8,128)(2,1)} %nk_ref.1, bf16[96,128]{1,0:T(8,128)(2,1)} %nv_ref.1), custom_call_target="tpu_custom_call" | custom-call | tf_op jit(solution)/shard_map/pallas_call | solution.py:291
  6.1 0.0 copy-start.4
  6.1 0.0 copy-start.5
  6.1 0.0 copy-start.2
  6.1 10.4 %all-to-all-start = ((bf16[8,144,128]{2,1,0:T(8,128)(2,1)}), bf16[8,144,128]{2,1,0:T(8,128)(2,1)S(1)}, u32[]{:S(2)}, u32[]{:S(2)}) async-start(bf16[8,144,128]{2,1,0:T(8,128)(2,1)} %shard_map.120), calls=%async_computation | async-start | bytes 589824 | tf_op jit(solution)/shard_map/all_to_all | solution.py:311
  16.5 0.0 copy-start.1
  16.5 0.0 copy-done.4
  16.5 0.6 convert_reduce_fusion
  17.2 0.7 pad_add_fusion.1.where_ref
  17.9 0.0 copy-done.5
  17.9 0.0 copy-start.3
  17.9 0.2 select_reduce_fusion.page_ref
  18.1 4.7 %all-to-all-done.part_ref = bf16[8,144,128]{2,1,0:T(8,128)(2,1)S(1)} async-done(((bf16[8,144,128]{2,1,0:T(8,128)(2,1)}), bf16[8,144,128]{2,1,0:T(8,128)(2,1)S(1)}, u32[]{:S(2)}, u32[]{:S(2)}) %all-to-all-start) | async-done | bytes 294944 | tf_op jit(solution)/shard_map/all_to_all | solution.py:311
  22.7 0.0 copy-done.2
  22.7 0.0 copy-done.1
  22.7 0.0 copy-done.3
  22.7 0.9 %shard_map.121 = bf16[240,128]{1,0:T(8,128)(2,1)S(1)} custom-call(s32[3]{0:T(128)S(1)} %copy-done.3, bf16[8,144,128]{2,1,0:T(8,128)(2,1)S(1)} %all-to-all-done.part_ref, bf16[96,128]{1,0:T(8,128)(2,1)S(1)} %copy-done.1, bf16[96,128]{1,0:T(8,128)(2,1)S(1)} %copy-done.2), custom_call_target="tpu_custom_call" | custom-call | tf_op jit(solution)/shard_map/pallas_call | solution.py:313
  23.6 28.9 %all-gather = bf16[3840,128]{1,0:T(8,128)(2,1)S(1)} all-gather(bf16[240,128]{1,0:T(8,128)(2,1)S(1)} %shard_map.121), channel_id=2, replica_groups=mesh['far'=8,'near'=2,'core'=2,'head'=8,'grp'=2] {'far','near'}, dimensions={0}, use_global_device_ids=true | all-gather | bytes 1044480 | tf_op jit(solution)/shard_map/all_gather | solution.py:320
  52.5 0.0 copy-start
  52.5 0.5 shard_map.122.own_ref.a_own
  53.0 2.3 %collective-permute-start.1 = (bf16[1792,128]{1,0:T(8,128)(2,1)S(1)}, bf16[1792,128]{1,0:T(8,128)(2,1)S(1)}, u32[]{:S(2)}, u32[]{:S(2)}) collective-permute-start(bf16[1792,128]{1,0:T(8,128)(2,1)S(1)} %shard_map.122.own_ref.a_own), channel_id=1, source_target_pairs={{0,1},{1,0},{2,3},{3,2},{4,5},{5,4},{6,7},{7,6},{8,9},{9,8},{10,11... | collective-permute-start | bytes 1376264 | tf_op jit(solution)/shard_map/ppermute | solution.py:329
  55.3 9.5 %collective-permute-start = (bf16[1792,128]{1,0:T(8,128)(2,1)S(1)}, bf16[1792,128]{1,0:T(8,128)(2,1)S(1)}, u32[]{:S(2)}, u32[]{:S(2)}) collective-permute-start(bf16[1792,128]{1,0:T(8,128)(2,1)S(1)} %shard_map.122.own_ref.a_own), channel_id=1, source_target_pairs={{0,16},{16,0},{1,17},{17,1},{2,18},{18,2},{3,19},{19,3},{4,20},{20... | collective-permute-start | bytes 1376264 | tf_op jit(solution)/shard_map/ppermute | solution.py:330
  64.9 0.0 collective-permute-done.1.b_own
  64.9 8.0 %collective-permute-start.2 = (bf16[1792,128]{1,0:T(8,128)(2,1)S(1)}, bf16[1792,128]{1,0:T(8,128)(2,1)S(1)}, u32[]{:S(2)}, u32[]{:S(2)}) collective-permute-start(bf16[1792,128]{1,0:T(8,128)(2,1)S(1)} %collective-permute-done.1.b_own), channel_id=1, source_target_pairs={{0,16},{16,0},{1,17},{17,1},{2,18},{18,2},{3,19},{19,3},{4,20},{20... | collective-permute-start | bytes 1376264 | tf_op jit(solution)/shard_map/ppermute | solution.py:331
  72.9 0.0 collective-permute-done.peer_ref.a_peer
  72.9 0.0 copy-done
  72.9 2.1 %shard_map.123 = (bf16[768,128]{1,0:T(8,128)(2,1)S(1)}, f32[768,256]{1,0:T(8,128)S(1)}, f32[768,1]{1,0:T(8,128)S(1)}) custom-call(s32[4]{0:T(128)S(1)} %pad_add_fusion.1.where_ref, bf16[96,1024]{1,0:T(8,128)(2,1)S(1)} %copy-done, bf16[1792,128]{1,0:T(8,128)(2,1)S(1)} %shard_map.122.own_ref.a_own, bf16[1792,128]{1,0:T(8,128)(2,1)S(1)} %collective-permute-done.peer_ref.a_peer), custom_call_target="tpu_custom_call" | custom-call | tf_op jit(solution)/shard_map/pallas_call | solution.py:333
  75.0 0.0 collective-permute-done.2.b_peer
  75.0 3.2 %shard_map.124 = (bf16[96,1024]{1,0:T(8,128)(2,1)}, bf16[6,16,128]{2,1,0:T(8,128)(2,1)}, bf16[6,16,128]{2,1,0:T(8,128)(2,1)}, bf16[64,2048]{1,0:T(8,128)(2,1)}) custom-call(s32[4]{0:T(128)S(1)} %pad_add_fusion.1.where_ref, s32[6]{0:T(128)S(1)} %select_reduce_fusion.page_ref, bf16[1792,128]{1,0:T(8,128)(2,1)S(1)} %shard_map.122.own_ref.a_own, ...), custom_call_target="tpu_custom_call" | custom-call | tf_op jit(solution)/shard_map/pallas_call | solution.py:344
  (1 shorter events, 0.0 us)
Async XLA Ops:
  6.1 10.4 %copy-start.4 = (s32[3072]{0:T(1024)S(1)}, s32[3072]{0:T(1024)}, u32[]{:S(2)}) copy-start(s32[3072]{0:T(1024)} %param.12) | copy-start | bytes 36868
  6.1 11.8 %copy-start.5 = (s32[192]{0:T(256)S(1)}, s32[192]{0:T(256)}, u32[]{:S(2)}) copy-start(s32[192]{0:T(256)} %param.13) | copy-start | bytes 2308
  6.1 16.6 %copy-start.2 = (bf16[96,128]{1,0:T(8,128)(2,1)S(1)}, bf16[96,128]{1,0:T(8,128)(2,1)}, u32[]{:S(2)}) copy-start(bf16[96,128]{1,0:T(8,128)(2,1)} %nv_ref.1) | copy-start | bytes 73732
  6.1 16.6 %all-to-all-start = ((bf16[8,144,128]{2,1,0:T(8,128)(2,1)}), bf16[8,144,128]{2,1,0:T(8,128)(2,1)S(1)}, u32[]{:S(2)}, u32[]{:S(2)}) async-start(bf16[8,144,128]{2,1,0:T(8,128)(2,1)} %shard_map.120), calls=%async_computation | async-start | bytes 589824 | tf_op jit(solution)/shard_map/all_to_all | solution.py:311
  16.5 6.2 %copy-start.1 = (bf16[96,128]{1,0:T(8,128)(2,1)S(1)}, bf16[96,128]{1,0:T(8,128)(2,1)}, u32[]{:S(2)}) copy-start(bf16[96,128]{1,0:T(8,128)(2,1)} %nk_ref.1) | copy-start | bytes 73732
  17.9 4.9 %copy-start.3 = (s32[3]{0:T(128)S(1)}, s32[3]{0:T(128)}, u32[]{:S(2)}) copy-start(s32[3]{0:T(128)} %pad_add_fusion.where_ref) | copy-start | bytes 40
  52.5 20.3 %copy-start = (bf16[96,1024]{1,0:T(8,128)(2,1)S(1)}, bf16[96,1024]{1,0:T(8,128)(2,1)}, u32[]{:S(2)}) copy-start(bf16[96,1024]{1,0:T(8,128)(2,1)} %q_ref.1) | copy-start | bytes 589828
  53.0 11.8 %collective-permute-start.1 = (bf16[1792,128]{1,0:T(8,128)(2,1)S(1)}, bf16[1792,128]{1,0:T(8,128)(2,1)S(1)}, u32[]{:S(2)}, u32[]{:S(2)}) collective-permute-start(bf16[1792,128]{1,0:T(8,128)(2,1)S(1)} %shard_map.122.own_ref.a_own), channel_id=1, source_target_pairs={{0,1},{1,0},{2,3},{3,2},{4,5},{5,4},{6,7},{7,6},{8,9},{9,8},{10,11... | collective-permute-start | bytes 1376264 | tf_op jit(solution)/shard_map/ppermute | solution.py:329
  55.3 17.5 %collective-permute-start = (bf16[1792,128]{1,0:T(8,128)(2,1)S(1)}, bf16[1792,128]{1,0:T(8,128)(2,1)S(1)}, u32[]{:S(2)}, u32[]{:S(2)}) collective-permute-start(bf16[1792,128]{1,0:T(8,128)(2,1)S(1)} %shard_map.122.own_ref.a_own), channel_id=1, source_target_pairs={{0,16},{16,0},{1,17},{17,1},{2,18},{18,2},{3,19},{19,3},{4,20},{20... | collective-permute-start | bytes 1376264 | tf_op jit(solution)/shard_map/ppermute | solution.py:330
  64.9 10.1 %collective-permute-start.2 = (bf16[1792,128]{1,0:T(8,128)(2,1)S(1)}, bf16[1792,128]{1,0:T(8,128)(2,1)S(1)}, u32[]{:S(2)}, u32[]{:S(2)}) collective-permute-start(bf16[1792,128]{1,0:T(8,128)(2,1)S(1)} %collective-permute-done.1.b_own), channel_id=1, source_target_pairs={{0,16},{16,0},{1,17},{17,1},{2,18},{18,2},{3,19},{19,3},{4,20},{20... | collective-permute-start | bytes 1376264 | tf_op jit(solution)/shard_map/ppermute | solution.py:331

commit v6 on v5

--- a/solution.py
+++ b/solution.py
@@ -29,7 +29,7 @@
 
 
 def partial_kernel(
-    len_ref, where_ref, dq_hbm, rk_hbm, rv_hbm, nk_hbm, nv_hbm, out_ref, dq, rk, rv, nk, nv, sems
+    len_ref, dq_hbm, rk_hbm, rv_hbm, nk_hbm, nv_hbm, out_ref, dq, rk, rv, nk, nv, sems
 ):
     groups = dq.shape[0] // 16
     res_rows = rk.shape[1]
@@ -50,7 +50,10 @@
     ]
     for copy in loads[0] + new_loads + [copy for group in loads[1:] for copy in group]:
         copy.start()
-    base, grp, half_rows = where_ref[0], where_ref[1], where_ref[2]
+    grp = lax.axis_index("grp")
+    place = (lax.axis_index("far") * 2 + lax.axis_index("near")) * 2 + lax.axis_index("core")
+    base = (place * 2 + grp) * res_rows
+    half_rows = tokens // 2
     keys = 16 * res_rows
     queries = 16 * heads
     col = lax.broadcasted_iota(jnp.int32, (1, keys), 1)
@@ -110,14 +113,14 @@
     return factors, top, total
 
 
-def pack_kernel(where_ref, part_ref, nk_ref, nv_ref, out_ref):
+def pack_kernel(part_ref, nk_ref, nv_ref, out_ref):
     tokens = nk_ref.shape[0]
     count = part_ref.shape[0]
 
     half = tokens // 2
     for side in range(2):
 
-        @pl.when(where_ref[1] == side)
+        @pl.when(lax.axis_index("grp") == side)
         def _():
             out_ref[:half] = nk_ref[side * half : (side + 1) * half]
             out_ref[half:tokens] = nv_ref[side * half : (side + 1) * half]
@@ -286,12 +289,11 @@
     pages = tokens // PAGE_TOKENS
     i32 = jnp.int32
 
-    where_a = jnp.stack([(ctx * 2 + grp) * res_rows, grp, jnp.int32(tokens // 2)]).astype(i32)
     groups = rows // 16
     part = pl.pallas_call(
         partial_kernel,
         out_shape=jax.ShapeDtypeStruct((2 * groups, 144, HEAD_SIZE), bf),
-        in_specs=[SMEM, SMEM] + [HBM] * 5,
+        in_specs=[SMEM] + [HBM] * 5,
         out_specs=VMEM,
         scratch_shapes=[
             pltpu.VMEM(decode_query_rows.shape, bf),
@@ -302,7 +304,7 @@
             pltpu.SemaphoreType.DMA((3 * groups + 2,)),
         ],
         compiler_params=pltpu.CompilerParams(vmem_limit_bytes=63 * 1024 * 1024),
-    )(res_len, where_a, decode_query_rows, resident_keys, resident_values, new_keys, new_values)
+    )(res_len, decode_query_rows, resident_keys, resident_values, new_keys, new_values)
     bound = jnp.sum((segment_ids == 0).astype(i32))
     slots = ctx * pages + jnp.arange(pages, dtype=i32)
     ids = jnp.arange(page_table.shape[0], dtype=i32)
@@ -313,10 +315,10 @@
     packed = pl.pallas_call(
         pack_kernel,
         out_shape=jax.ShapeDtypeStruct((tokens + 144, HEAD_SIZE), bf),
-        in_specs=[SMEM] + [VMEM] * 3,
+        in_specs=[VMEM] * 3,
         out_specs=VMEM,
         compiler_params=PARAMS,
-    )(where_a, part, new_keys, new_values)
+    )(part, new_keys, new_values)
     gathered = lax.all_gather(packed, ("far", "near"), axis=0)
     swap = [(0, 1), (1, 0)]
     a_own = pl.pallas_call(

time: 78.7 us -> 77.3 us (0.982)
  no operation moved by 1% of the time
where the time goes in v6:
time: 77.3 us; the launch traced here: 76.9 us
  starting transfers between devices  30 us (39%)
  blocking collectives  28.9 us (37%)
  Pallas kernels  11.1 us (14%)
  waiting for transfers between devices  4.65 us (6%)
  other arithmetic  1.54 us (2%)
    all_gather x1, blocking collectives, local(): gathered = lax.all_gather(packed, ('far', 'near'), axis=0)  28.9 us
    all_to_all x1, starting transfers between devices, local(): part = lax.all_to_all(part, ('near', 'core', 'grp'), 0, 0, tiled=True)  10.2 us
    ppermute x1, starting transfers between devices, local(): a_peer = lax.ppermute(a_own, 'core', swap)  9.54 us
    ppermute x1, starting transfers between devices, local(): b_peer = lax.ppermute(b_own, 'core', swap)  7.96 us
    pallas_call x1, Pallas kernels, local(): pl.pallas_call(partial_kernel, out_shape=jax.ShapeDtypeStruct((2 * groups...  4.86 us
    all_to_all x1, waiting for transfers between devices, local(): part = lax.all_to_all(part, ('near', 'core', 'grp'), 0, 0, tiled=True)  4.64 us
    pallas_call x1, Pallas kernels, local(): pl.pallas_call(second_kernel, out_shape=(jax.ShapeDtypeStruct(new_queries...  3.23 us
    ppermute x1, starting transfers between devices, local(): b_own = lax.ppermute(a_own, 'grp', swap)  2.28 us
  transfers between devices with their start and end apart: 4, of which 1 were waited for; matrix products, arithmetic and copies ran while one was open for 2% of the time, Pallas kernels for 3%

profile of v6, /device:TPU:1, one launch (start us, length us, event | category | flops | bytes accessed | tf_op | source)
XLA Modules:
  0.0 76.9 jit_solution(15232033839946545793)
XLA Ops:
  0.6 4.9 %shard_map.120 = bf16[8,144,128]{2,1,0:T(8,128)(2,1)} custom-call(s32[64]{0:T(128)} %len_ref.1, bf16[64,2048]{1,0:T(8,128)(2,1)} %dq_hbm.1, bf16[64,32,128]{2,1,0:T(8,128)(2,1)} %rk_hbm.1, bf16[64,32,128]{2,1,0:T(8,128)(2,1)} %rv_hbm.1, bf16[96,128]{1,0:T(8,128)(2,1)} %nk_ref.1, bf16[96,128]{1,0:T(8,128)(2,1)} %nv_ref.1), custom_call_target="tpu_custom_call" | custom-call | tf_op jit(solution)/shard_map/pallas_call | solution.py:293
  5.5 0.0 copy-start.3
  5.5 10.2 %all-to-all-start = ((bf16[8,144,128]{2,1,0:T(8,128)(2,1)}), bf16[8,144,128]{2,1,0:T(8,128)(2,1)S(1)}, u32[]{:S(2)}, u32[]{:S(2)}) async-start(bf16[8,144,128]{2,1,0:T(8,128)(2,1)} %shard_map.120), calls=%async_computation | async-start | bytes 589824 | tf_op jit(solution)/shard_map/all_to_all | solution.py:313
  15.7 0.0 copy-start.4
  15.7 0.0 copy-start.2
  15.7 0.0 copy-start.1
  15.8 0.0 copy-done.3
  15.8 0.6 convert_reduce_fusion
  16.4 0.7 pad_add_fusion.where_ref
  17.1 0.0 copy-done.4
  17.1 0.2 select_reduce_fusion.page_ref
  17.3 4.6 %all-to-all-done.part_ref = bf16[8,144,128]{2,1,0:T(8,128)(2,1)S(1)} async-done(((bf16[8,144,128]{2,1,0:T(8,128)(2,1)}), bf16[8,144,128]{2,1,0:T(8,128)(2,1)S(1)}, u32[]{:S(2)}, u32[]{:S(2)}) %all-to-all-start) | async-done | bytes 294944 | tf_op jit(solution)/shard_map/all_to_all | solution.py:313
  22.0 0.0 copy-done.2
  22.0 0.0 copy-done.1
  22.0 0.4 shard_map.121
  22.3 28.9 %all-gather = bf16[3840,128]{1,0:T(8,128)(2,1)S(1)} all-gather(bf16[240,128]{1,0:T(8,128)(2,1)S(1)} %shard_map.121), channel_id=2, replica_groups=mesh['far'=8,'near'=2,'core'=2,'head'=8,'grp'=2] {'far','near'}, dimensions={0}, use_global_device_ids=true | all-gather | bytes 1044480 | tf_op jit(solution)/shard_map/all_gather | solution.py:322
  51.2 0.0 copy-start
  51.2 0.5 shard_map.122.own_ref.a_own
  51.7 2.3 %collective-permute-start.1 = (bf16[1792,128]{1,0:T(8,128)(2,1)S(1)}, bf16[1792,128]{1,0:T(8,128)(2,1)S(1)}, u32[]{:S(2)}, u32[]{:S(2)}) collective-permute-start(bf16[1792,128]{1,0:T(8,128)(2,1)S(1)} %shard_map.122.own_ref.a_own), channel_id=1, source_target_pairs={{0,1},{1,0},{2,3},{3,2},{4,5},{5,4},{6,7},{7,6},{8,9},{9,8},{10,11... | collective-permute-start | bytes 1376264 | tf_op jit(solution)/shard_map/ppermute | solution.py:331
  54.0 9.5 %collective-permute-start = (bf16[1792,128]{1,0:T(8,128)(2,1)S(1)}, bf16[1792,128]{1,0:T(8,128)(2,1)S(1)}, u32[]{:S(2)}, u32[]{:S(2)}) collective-permute-start(bf16[1792,128]{1,0:T(8,128)(2,1)S(1)} %shard_map.122.own_ref.a_own), channel_id=1, source_target_pairs={{0,16},{16,0},{1,17},{17,1},{2,18},{18,2},{3,19},{19,3},{4,20},{20... | collective-permute-start | bytes 1376264 | tf_op jit(solution)/shard_map/ppermute | solution.py:332
  63.6 0.0 collective-permute-done.1.b_own
  63.6 8.0 %collective-permute-start.2 = (bf16[1792,128]{1,0:T(8,128)(2,1)S(1)}, bf16[1792,128]{1,0:T(8,128)(2,1)S(1)}, u32[]{:S(2)}, u32[]{:S(2)}) collective-permute-start(bf16[1792,128]{1,0:T(8,128)(2,1)S(1)} %collective-permute-done.1.b_own), channel_id=1, source_target_pairs={{0,16},{16,0},{1,17},{17,1},{2,18},{18,2},{3,19},{19,3},{4,20},{20... | collective-permute-start | bytes 1376264 | tf_op jit(solution)/shard_map/ppermute | solution.py:333
  71.5 0.0 collective-permute-done.peer_ref.a_peer
  71.5 0.0 copy-done
  71.6 2.1 %shard_map.123 = (bf16[768,128]{1,0:T(8,128)(2,1)S(1)}, f32[768,256]{1,0:T(8,128)S(1)}, f32[768,1]{1,0:T(8,128)S(1)}) custom-call(s32[4]{0:T(128)S(1)} %pad_add_fusion.where_ref, bf16[96,1024]{1,0:T(8,128)(2,1)S(1)} %copy-done, bf16[1792,128]{1,0:T(8,128)(2,1)S(1)} %shard_map.122.own_ref.a_own, bf16[1792,128]{1,0:T(8,128)(2,1)S(1)} %collective-permute-done.peer_ref.a_peer), custom_call_target="tpu_custom_call" | custom-call | tf_op jit(solution)/shard_map/pallas_call | solution.py:335
  73.7 0.0 collective-permute-done.2.b_peer
  73.7 3.2 %shard_map.124 = (bf16[96,1024]{1,0:T(8,128)(2,1)}, bf16[6,16,128]{2,1,0:T(8,128)(2,1)}, bf16[6,16,128]{2,1,0:T(8,128)(2,1)}, bf16[64,2048]{1,0:T(8,128)(2,1)}) custom-call(s32[4]{0:T(128)S(1)} %pad_add_fusion.where_ref, s32[6]{0:T(128)S(1)} %select_reduce_fusion.page_ref, bf16[1792,128]{1,0:T(8,128)(2,1)S(1)} %shard_map.122.own_ref.a_own, ...), custom_call_target="tpu_custom_call" | custom-call | tf_op jit(solution)/shard_map/pallas_call | solution.py:346
  (1 shorter events, 0.0 us)
Async XLA Ops:
  5.5 10.3 %copy-start.3 = (s32[3072]{0:T(1024)S(1)}, s32[3072]{0:T(1024)}, u32[]{:S(2)}) copy-start(s32[3072]{0:T(1024)} %param.12) | copy-start | bytes 36868
  5.5 16.4 %all-to-all-start = ((bf16[8,144,128]{2,1,0:T(8,128)(2,1)}), bf16[8,144,128]{2,1,0:T(8,128)(2,1)S(1)}, u32[]{:S(2)}, u32[]{:S(2)}) async-start(bf16[8,144,128]{2,1,0:T(8,128)(2,1)} %shard_map.120), calls=%async_computation | async-start | bytes 589824 | tf_op jit(solution)/shard_map/all_to_all | solution.py:313
  15.7 1.4 %copy-start.4 = (s32[192]{0:T(256)S(1)}, s32[192]{0:T(256)}, u32[]{:S(2)}) copy-start(s32[192]{0:T(256)} %param.13) | copy-start | bytes 2308
  15.7 6.2 %copy-start.2 = (bf16[96,128]{1,0:T(8,128)(2,1)S(1)}, bf16[96,128]{1,0:T(8,128)(2,1)}, u32[]{:S(2)}) copy-start(bf16[96,128]{1,0:T(8,128)(2,1)} %nv_ref.1) | copy-start | bytes 73732
  15.7 6.2 %copy-start.1 = (bf16[96,128]{1,0:T(8,128)(2,1)S(1)}, bf16[96,128]{1,0:T(8,128)(2,1)}, u32[]{:S(2)}) copy-start(bf16[96,128]{1,0:T(8,128)(2,1)} %nk_ref.1) | copy-start | bytes 73732
  51.2 20.3 %copy-start = (bf16[96,1024]{1,0:T(8,128)(2,1)S(1)}, bf16[96,1024]{1,0:T(8,128)(2,1)}, u32[]{:S(2)}) copy-start(bf16[96,1024]{1,0:T(8,128)(2,1)} %q_ref.1) | copy-start | bytes 589828
  51.7 11.8 %collective-permute-start.1 = (bf16[1792,128]{1,0:T(8,128)(2,1)S(1)}, bf16[1792,128]{1,0:T(8,128)(2,1)S(1)}, u32[]{:S(2)}, u32[]{:S(2)}) collective-permute-start(bf16[1792,128]{1,0:T(8,128)(2,1)S(1)} %shard_map.122.own_ref.a_own), channel_id=1, source_target_pairs={{0,1},{1,0},{2,3},{3,2},{4,5},{5,4},{6,7},{7,6},{8,9},{9,8},{10,11... | collective-permute-start | bytes 1376264 | tf_op jit(solution)/shard_map/ppermute | solution.py:331
  54.0 17.5 %collective-permute-start = (bf16[1792,128]{1,0:T(8,128)(2,1)S(1)}, bf16[1792,128]{1,0:T(8,128)(2,1)S(1)}, u32[]{:S(2)}, u32[]{:S(2)}) collective-permute-start(bf16[1792,128]{1,0:T(8,128)(2,1)S(1)} %shard_map.122.own_ref.a_own), channel_id=1, source_target_pairs={{0,16},{16,0},{1,17},{17,1},{2,18},{18,2},{3,19},{19,3},{4,20},{20... | collective-permute-start | bytes 1376264 | tf_op jit(solution)/shard_map/ppermute | solution.py:332
  63.6 10.1 %collective-permute-start.2 = (bf16[1792,128]{1,0:T(8,128)(2,1)S(1)}, bf16[1792,128]{1,0:T(8,128)(2,1)S(1)}, u32[]{:S(2)}, u32[]{:S(2)}) collective-permute-start(bf16[1792,128]{1,0:T(8,128)(2,1)S(1)} %collective-permute-done.1.b_own), channel_id=1, source_target_pairs={{0,16},{16,0},{1,17},{17,1},{2,18},{18,2},{3,19},{19,3},{4,20},{20... | collective-permute-start | bytes 1376264 | tf_op jit(solution)/shard_map/ppermute | solution.py:333

commit v7 on v6

--- a/solution.py
+++ b/solution.py
@@ -67,7 +67,8 @@
     entry = lax.broadcasted_iota(jnp.int32, (queries, 128), 0)
     lane = lax.broadcasted_iota(jnp.int32, (queries, 128), 1)
     picks = [entry == (lane // 8) * 16 + side * 8 + lane % 8 for side in range(2)]
-    for g in range(groups):
+
+    def scores(g):
         lens = jnp.zeros((1, keys), jnp.int32)
         for r in range(16):
             lens = jnp.where(col_row == r, len_ref[16 * g + r], lens)
@@ -82,9 +83,15 @@
             axis=0,
         )
         res_k = rk[16 * g : 16 * g + 16].reshape(keys, HEAD_SIZE)
+        s1 = jnp.where(same_row, dot_t(q, res_k) * LOG2_SCALE + live, NEG_FILL)
+        return s1, dot_t(q, nk[...]) * LOG2_SCALE + token_bias
+
+    ahead = scores(0)
+    for g in range(groups):
+        s1, s2 = ahead
+        if g + 1 < groups:
+            ahead = scores(g + 1)
         res_v = rv[16 * g : 16 * g + 16].reshape(keys, HEAD_SIZE)
-        s1 = jnp.where(same_row, dot_t(q, res_k) * LOG2_SCALE + live, NEG_FILL)
-        s2 = dot_t(q, nk[...]) * LOG2_SCALE + token_bias
         top = jnp.maximum(jnp.max(s1, axis=1, keepdims=True), jnp.max(s2, axis=1, keepdims=True))
         top = top.astype(jnp.bfloat16).astype(jnp.float32)
         p1 = jnp.exp2(s1 - top).astype(jnp.bfloat16)
@@ -199,9 +206,12 @@
         v = jnp.concatenate([v, ones], axis=1)
         key_pos = key_pos0 + low * (2 * tokens)
         bias = jnp.where((key_pos <= q_pos) & (key_pos >= begin), 0.0, NEG_FILL)
+        ahead = dot_t(qs[:row_block], k)
         for b in range(qs.shape[0] // row_block):
             rows_b = slice(b * row_block, (b + 1) * row_block)
-            s = dot_t(qs[rows_b], k) * LOG2_SCALE + bias
+            s = ahead * LOG2_SCALE + bias
+            if b + 1 < qs.shape[0] // row_block:
+                ahead = dot_t(qs[(b + 1) * row_block : (b + 2) * row_block], k)
             before = top[rows_b]
             after = jnp.maximum(before, jnp.max(s, axis=1, keepdims=True))
             p = jnp.exp2(s - after).astype(jnp.bfloat16)

time: 77.3 us -> 76.5 us (0.990)
  Pallas kernels: 11.1 us -> 10.2 us
where the time goes in v7:
time: 76.5 us; the launch traced here: 76.1 us
  starting transfers between devices  30 us (39%)
  blocking collectives  28.9 us (38%)
  Pallas kernels  10.2 us (13%)
  waiting for transfers between devices  4.65 us (6%)
  other arithmetic  1.54 us (2%)
    all_gather x1, blocking collectives, local(): gathered = lax.all_gather(packed, ('far', 'near'), axis=0)  28.9 us
    all_to_all x1, starting transfers between devices, local(): part = lax.all_to_all(part, ('near', 'core', 'grp'), 0, 0, tiled=True)  10.2 us
    ppermute x1, starting transfers between devices, local(): a_peer = lax.ppermute(a_own, 'core', swap)  9.54 us
    ppermute x1, starting transfers between devices, local(): b_peer = lax.ppermute(b_own, 'core', swap)  7.96 us
    all_to_all x1, waiting for transfers between devices, local(): part = lax.all_to_all(part, ('near', 'core', 'grp'), 0, 0, tiled=True)  4.64 us
    pallas_call x1, Pallas kernels, local(): pl.pallas_call(partial_kernel, out_shape=jax.ShapeDtypeStruct((2 * groups...  4.27 us
    pallas_call x1, Pallas kernels, local(): pl.pallas_call(second_kernel, out_shape=(jax.ShapeDtypeStruct(new_queries...  3.09 us
    ppermute x1, starting transfers between devices, local(): b_own = lax.ppermute(a_own, 'grp', swap)  2.28 us
  transfers between devices with their start and end apart: 4, of which 1 were waited for; matrix products, arithmetic and copies ran while one was open for 2% of the time, Pallas kernels for 3%

profile of v7, /device:TPU:1, one launch (start us, length us, event | category | flops | bytes accessed | tf_op | source)
XLA Modules:
  0.0 76.1 jit_solution(12557126268008295734)
XLA Ops:
  0.6 4.3 %shard_map.120 = bf16[8,144,128]{2,1,0:T(8,128)(2,1)} custom-call(s32[64]{0:T(128)} %len_ref.1, bf16[64,2048]{1,0:T(8,128)(2,1)} %dq_hbm.1, bf16[64,32,128]{2,1,0:T(8,128)(2,1)} %rk_hbm.1, bf16[64,32,128]{2,1,0:T(8,128)(2,1)} %rv_hbm.1, bf16[96,128]{1,0:T(8,128)(2,1)} %nk_ref.1, bf16[96,128]{1,0:T(8,128)(2,1)} %nv_ref.1), custom_call_target="tpu_custom_call" | custom-call | tf_op jit(solution)/shard_map/pallas_call | solution.py:303
  4.9 0.0 copy-start.3
  4.9 10.2 %all-to-all-start = ((bf16[8,144,128]{2,1,0:T(8,128)(2,1)}), bf16[8,144,128]{2,1,0:T(8,128)(2,1)S(1)}, u32[]{:S(2)}, u32[]{:S(2)}) async-start(bf16[8,144,128]{2,1,0:T(8,128)(2,1)} %shard_map.120), calls=%async_computation | async-start | bytes 589824 | tf_op jit(solution)/shard_map/all_to_all | solution.py:323
  15.1 0.0 copy-start.4
  15.1 0.0 copy-start.2
  15.1 0.0 copy-start.1
  15.2 0.0 copy-done.3
  15.2 0.6 convert_reduce_fusion
  15.8 0.7 pad_add_fusion.where_ref
  16.5 0.0 copy-done.4
  16.5 0.2 select_reduce_fusion.page_ref
  16.7 4.6 %all-to-all-done.part_ref = bf16[8,144,128]{2,1,0:T(8,128)(2,1)S(1)} async-done(((bf16[8,144,128]{2,1,0:T(8,128)(2,1)}), bf16[8,144,128]{2,1,0:T(8,128)(2,1)S(1)}, u32[]{:S(2)}, u32[]{:S(2)}) %all-to-all-start) | async-done | bytes 294944 | tf_op jit(solution)/shard_map/all_to_all | solution.py:323
  21.4 0.0 copy-done.2
  21.4 0.0 copy-done.1
  21.4 0.4 shard_map.121
  21.7 28.9 %all-gather = bf16[3840,128]{1,0:T(8,128)(2,1)S(1)} all-gather(bf16[240,128]{1,0:T(8,128)(2,1)S(1)} %shard_map.121), channel_id=2, replica_groups=mesh['far'=8,'near'=2,'core'=2,'head'=8,'grp'=2] {'far','near'}, dimensions={0}, use_global_device_ids=true | all-gather | bytes 1044480 | tf_op jit(solution)/shard_map/all_gather | solution.py:332
  50.6 0.0 copy-start
  50.6 0.5 shard_map.122.own_ref.a_own
  51.1 2.3 %collective-permute-start.1 = (bf16[1792,128]{1,0:T(8,128)(2,1)S(1)}, bf16[1792,128]{1,0:T(8,128)(2,1)S(1)}, u32[]{:S(2)}, u32[]{:S(2)}) collective-permute-start(bf16[1792,128]{1,0:T(8,128)(2,1)S(1)} %shard_map.122.own_ref.a_own), channel_id=1, source_target_pairs={{0,1},{1,0},{2,3},{3,2},{4,5},{5,4},{6,7},{7,6},{8,9},{9,8},{10,11... | collective-permute-start | bytes 1376264 | tf_op jit(solution)/shard_map/ppermute | solution.py:341
  53.4 9.5 %collective-permute-start = (bf16[1792,128]{1,0:T(8,128)(2,1)S(1)}, bf16[1792,128]{1,0:T(8,128)(2,1)S(1)}, u32[]{:S(2)}, u32[]{:S(2)}) collective-permute-start(bf16[1792,128]{1,0:T(8,128)(2,1)S(1)} %shard_map.122.own_ref.a_own), channel_id=1, source_target_pairs={{0,16},{16,0},{1,17},{17,1},{2,18},{18,2},{3,19},{19,3},{4,20},{20... | collective-permute-start | bytes 1376264 | tf_op jit(solution)/shard_map/ppermute | solution.py:342
  63.0 0.0 collective-permute-done.1.b_own
  63.0 8.0 %collective-permute-start.2 = (bf16[1792,128]{1,0:T(8,128)(2,1)S(1)}, bf16[1792,128]{1,0:T(8,128)(2,1)S(1)}, u32[]{:S(2)}, u32[]{:S(2)}) collective-permute-start(bf16[1792,128]{1,0:T(8,128)(2,1)S(1)} %collective-permute-done.1.b_own), channel_id=1, source_target_pairs={{0,16},{16,0},{1,17},{17,1},{2,18},{18,2},{3,19},{19,3},{4,20},{20... | collective-permute-start | bytes 1376264 | tf_op jit(solution)/shard_map/ppermute | solution.py:343
  70.9 0.0 collective-permute-done.peer_ref.a_peer
  71.0 0.0 copy-done
  71.0 2.0 %shard_map.123 = (bf16[768,128]{1,0:T(8,128)(2,1)S(1)}, f32[768,256]{1,0:T(8,128)S(1)}, f32[768,1]{1,0:T(8,128)S(1)}) custom-call(s32[4]{0:T(128)S(1)} %pad_add_fusion.where_ref, bf16[96,1024]{1,0:T(8,128)(2,1)S(1)} %copy-done, bf16[1792,128]{1,0:T(8,128)(2,1)S(1)} %shard_map.122.own_ref.a_own, bf16[1792,128]{1,0:T(8,128)(2,1)S(1)} %collective-permute-done.peer_ref.a_peer), custom_call_target="tpu_custom_call" | custom-call | tf_op jit(solution)/shard_map/pallas_call | solution.py:345
  73.0 0.0 collective-permute-done.2.b_peer
  73.0 3.1 %shard_map.124 = (bf16[96,1024]{1,0:T(8,128)(2,1)}, bf16[6,16,128]{2,1,0:T(8,128)(2,1)}, bf16[6,16,128]{2,1,0:T(8,128)(2,1)}, bf16[64,2048]{1,0:T(8,128)(2,1)}) custom-call(s32[4]{0:T(128)S(1)} %pad_add_fusion.where_ref, s32[6]{0:T(128)S(1)} %select_reduce_fusion.page_ref, bf16[1792,128]{1,0:T(8,128)(2,1)S(1)} %shard_map.122.own_ref.a_own, ...), custom_call_target="tpu_custom_call" | custom-call | tf_op jit(solution)/shard_map/pallas_call | solution.py:356
  (1 shorter events, 0.0 us)
Async XLA Ops:
  4.9 10.3 %copy-start.3 = (s32[3072]{0:T(1024)S(1)}, s32[3072]{0:T(1024)}, u32[]{:S(2)}) copy-start(s32[3072]{0:T(1024)} %param.12) | copy-start | bytes 36868
  4.9 16.4 %all-to-all-start = ((bf16[8,144,128]{2,1,0:T(8,128)(2,1)}), bf16[8,144,128]{2,1,0:T(8,128)(2,1)S(1)}, u32[]{:S(2)}, u32[]{:S(2)}) async-start(bf16[8,144,128]{2,1,0:T(8,128)(2,1)} %shard_map.120), calls=%async_computation | async-start | bytes 589824 | tf_op jit(solution)/shard_map/all_to_all | solution.py:323
  15.1 1.4 %copy-start.4 = (s32[192]{0:T(256)S(1)}, s32[192]{0:T(256)}, u32[]{:S(2)}) copy-start(s32[192]{0:T(256)} %param.13) | copy-start | bytes 2308
  15.1 6.2 %copy-start.2 = (bf16[96,128]{1,0:T(8,128)(2,1)S(1)}, bf16[96,128]{1,0:T(8,128)(2,1)}, u32[]{:S(2)}) copy-start(bf16[96,128]{1,0:T(8,128)(2,1)} %nv_ref.1) | copy-start | bytes 73732
  15.1 6.2 %copy-start.1 = (bf16[96,128]{1,0:T(8,128)(2,1)S(1)}, bf16[96,128]{1,0:T(8,128)(2,1)}, u32[]{:S(2)}) copy-start(bf16[96,128]{1,0:T(8,128)(2,1)} %nk_ref.1) | copy-start | bytes 73732
  50.6 20.3 %copy-start = (bf16[96,1024]{1,0:T(8,128)(2,1)S(1)}, bf16[96,1024]{1,0:T(8,128)(2,1)}, u32[]{:S(2)}) copy-start(bf16[96,1024]{1,0:T(8,128)(2,1)} %q_ref.1) | copy-start | bytes 589828
  51.1 11.8 %collective-permute-start.1 = (bf16[1792,128]{1,0:T(8,128)(2,1)S(1)}, bf16[1792,128]{1,0:T(8,128)(2,1)S(1)}, u32[]{:S(2)}, u32[]{:S(2)}) collective-permute-start(bf16[1792,128]{1,0:T(8,128)(2,1)S(1)} %shard_map.122.own_ref.a_own), channel_id=1, source_target_pairs={{0,1},{1,0},{2,3},{3,2},{4,5},{5,4},{6,7},{7,6},{8,9},{9,8},{10,11... | collective-permute-start | bytes 1376264 | tf_op jit(solution)/shard_map/ppermute | solution.py:341
  53.4 17.5 %collective-permute-start = (bf16[1792,128]{1,0:T(8,128)(2,1)S(1)}, bf16[1792,128]{1,0:T(8,128)(2,1)S(1)}, u32[]{:S(2)}, u32[]{:S(2)}) collective-permute-start(bf16[1792,128]{1,0:T(8,128)(2,1)S(1)} %shard_map.122.own_ref.a_own), channel_id=1, source_target_pairs={{0,16},{16,0},{1,17},{17,1},{2,18},{18,2},{3,19},{19,3},{4,20},{20... | collective-permute-start | bytes 1376264 | tf_op jit(solution)/shard_map/ppermute | solution.py:342
  63.0 10.0 %collective-permute-start.2 = (bf16[1792,128]{1,0:T(8,128)(2,1)S(1)}, bf16[1792,128]{1,0:T(8,128)(2,1)S(1)}, u32[]{:S(2)}, u32[]{:S(2)}) collective-permute-start(bf16[1792,128]{1,0:T(8,128)(2,1)S(1)} %collective-permute-done.1.b_own), channel_id=1, source_target_pairs={{0,16},{16,0},{1,17},{17,1},{2,18},{18,2},{3,19},{19,3},{4,20},{20... | collective-permute-start | bytes 1376264 | tf_op jit(solution)/shard_map/ppermute | solution.py:343

commit v8 on v7

--- a/solution.py
+++ b/solution.py
@@ -247,15 +247,12 @@
         row = (source // 2) * tokens + (page - side * (pages // 2)) * PAGE_TOKENS
         row = pl.multiple_of(row, PAGE_TOKENS)
         value_row = pl.multiple_of(row + half, PAGE_TOKENS)
-        for same_side, same_core, ref in (
-            (True, True, a_own), (True, False, a_peer), (False, True, b_own), (False, False, b_peer),
-        ):
-            there = ((side == grp) == same_side) & ((source % 2 == core) == same_core)
-
-            @pl.when(there)
-            def _():
-                pk_ref[s] = ref[pl.ds(row, PAGE_TOKENS), :]
-                pv_ref[s] = ref[pl.ds(value_row, PAGE_TOKENS), :]
+        own_side = side == grp
+        own_core = source % 2 == core
+        for out, at in ((pk_ref, row), (pv_ref, value_row)):
+            a = jnp.where(own_core, a_own[pl.ds(at, PAGE_TOKENS), :], a_peer[pl.ds(at, PAGE_TOKENS), :])
+            b = jnp.where(own_core, b_own[pl.ds(at, PAGE_TOKENS), :], b_peer[pl.ds(at, PAGE_TOKENS), :])
+            out[s] = jnp.where(own_side, a, b)
 
     columns = dec_ref.shape[1] // HEAD_SIZE
     begin = a_own.shape[0] - 16 * columns

time: 76.5 us -> 76.3 us (level)
  no operation moved by 1% of the time
where the time goes in v8:
time: 76.3 us; the launch traced here: 75.9 us
  starting transfers between devices  30 us (39%)
  blocking collectives  28.9 us (38%)
  Pallas kernels  10 us (13%)
  waiting for transfers between devices  4.65 us (6%)
  other arithmetic  1.54 us (2%)
    all_gather x1, blocking collectives, local(): gathered = lax.all_gather(packed, ('far', 'near'), axis=0)  28.9 us
    all_to_all x1, starting transfers between devices, local(): part = lax.all_to_all(part, ('near', 'core', 'grp'), 0, 0, tiled=True)  10.2 us
    ppermute x1, starting transfers between devices, local(): a_peer = lax.ppermute(a_own, 'core', swap)  9.54 us
    ppermute x1, starting transfers between devices, local(): b_peer = lax.ppermute(b_own, 'core', swap)  7.96 us
    all_to_all x1, waiting for transfers between devices, local(): part = lax.all_to_all(part, ('near', 'core', 'grp'), 0, 0, tiled=True)  4.64 us
    pallas_call x1, Pallas kernels, local(): pl.pallas_call(partial_kernel, out_shape=jax.ShapeDtypeStruct((2 * groups...  4.27 us
    pallas_call x1, Pallas kernels, local(): pl.pallas_call(second_kernel, out_shape=(jax.ShapeDtypeStruct(new_queries...  2.89 us
    ppermute x1, starting transfers between devices, local(): b_own = lax.ppermute(a_own, 'grp', swap)  2.28 us
  transfers between devices with their start and end apart: 4, of which 1 were waited for; matrix products, arithmetic and copies ran while one was open for 2% of the time, Pallas kernels for 3%

profile of v8, /device:TPU:1, one launch (start us, length us, event | category | flops | bytes accessed | tf_op | source)
XLA Modules:
  0.0 75.9 jit_solution(15960598927994660851)
XLA Ops:
  0.6 4.3 %shard_map.120 = bf16[8,144,128]{2,1,0:T(8,128)(2,1)} custom-call(s32[64]{0:T(128)} %len_ref.1, bf16[64,2048]{1,0:T(8,128)(2,1)} %dq_hbm.1, bf16[64,32,128]{2,1,0:T(8,128)(2,1)} %rk_hbm.1, bf16[64,32,128]{2,1,0:T(8,128)(2,1)} %rv_hbm.1, bf16[96,128]{1,0:T(8,128)(2,1)} %nk_ref.1, bf16[96,128]{1,0:T(8,128)(2,1)} %nv_ref.1), custom_call_target="tpu_custom_call" | custom-call | tf_op jit(solution)/shard_map/pallas_call | solution.py:300
  4.9 0.0 copy-start.3
  4.9 10.2 %all-to-all-start = ((bf16[8,144,128]{2,1,0:T(8,128)(2,1)}), bf16[8,144,128]{2,1,0:T(8,128)(2,1)S(1)}, u32[]{:S(2)}, u32[]{:S(2)}) async-start(bf16[8,144,128]{2,1,0:T(8,128)(2,1)} %shard_map.120), calls=%async_computation | async-start | bytes 589824 | tf_op jit(solution)/shard_map/all_to_all | solution.py:320
  15.1 0.0 copy-start.4
  15.1 0.0 copy-start.2
  15.1 0.0 copy-start.1
  15.2 0.0 copy-done.3
  15.2 0.6 convert_reduce_fusion
  15.8 0.7 pad_add_fusion.where_ref
  16.5 0.0 copy-done.4
  16.5 0.2 select_reduce_fusion.page_ref
  16.7 4.6 %all-to-all-done.part_ref = bf16[8,144,128]{2,1,0:T(8,128)(2,1)S(1)} async-done(((bf16[8,144,128]{2,1,0:T(8,128)(2,1)}), bf16[8,144,128]{2,1,0:T(8,128)(2,1)S(1)}, u32[]{:S(2)}, u32[]{:S(2)}) %all-to-all-start) | async-done | bytes 294944 | tf_op jit(solution)/shard_map/all_to_all | solution.py:320
  21.4 0.0 copy-done.2
  21.4 0.0 copy-done.1
  21.4 0.4 shard_map.121
  21.7 28.9 %all-gather = bf16[3840,128]{1,0:T(8,128)(2,1)S(1)} all-gather(bf16[240,128]{1,0:T(8,128)(2,1)S(1)} %shard_map.121), channel_id=2, replica_groups=mesh['far'=8,'near'=2,'core'=2,'head'=8,'grp'=2] {'far','near'}, dimensions={0}, use_global_device_ids=true | all-gather | bytes 1044480 | tf_op jit(solution)/shard_map/all_gather | solution.py:329
  50.6 0.0 copy-start
  50.6 0.5 shard_map.122.own_ref.a_own
  51.1 2.3 %collective-permute-start.1 = (bf16[1792,128]{1,0:T(8,128)(2,1)S(1)}, bf16[1792,128]{1,0:T(8,128)(2,1)S(1)}, u32[]{:S(2)}, u32[]{:S(2)}) collective-permute-start(bf16[1792,128]{1,0:T(8,128)(2,1)S(1)} %shard_map.122.own_ref.a_own), channel_id=1, source_target_pairs={{0,1},{1,0},{2,3},{3,2},{4,5},{5,4},{6,7},{7,6},{8,9},{9,8},{10,11... | collective-permute-start | bytes 1376264 | tf_op jit(solution)/shard_map/ppermute | solution.py:338
  53.4 9.5 %collective-permute-start = (bf16[1792,128]{1,0:T(8,128)(2,1)S(1)}, bf16[1792,128]{1,0:T(8,128)(2,1)S(1)}, u32[]{:S(2)}, u32[]{:S(2)}) collective-permute-start(bf16[1792,128]{1,0:T(8,128)(2,1)S(1)} %shard_map.122.own_ref.a_own), channel_id=1, source_target_pairs={{0,16},{16,0},{1,17},{17,1},{2,18},{18,2},{3,19},{19,3},{4,20},{20... | collective-permute-start | bytes 1376264 | tf_op jit(solution)/shard_map/ppermute | solution.py:339
  63.0 0.0 collective-permute-done.1.b_own
  63.0 8.0 %collective-permute-start.2 = (bf16[1792,128]{1,0:T(8,128)(2,1)S(1)}, bf16[1792,128]{1,0:T(8,128)(2,1)S(1)}, u32[]{:S(2)}, u32[]{:S(2)}) collective-permute-start(bf16[1792,128]{1,0:T(8,128)(2,1)S(1)} %collective-permute-done.1.b_own), channel_id=1, source_target_pairs={{0,16},{16,0},{1,17},{17,1},{2,18},{18,2},{3,19},{19,3},{4,20},{20... | collective-permute-start | bytes 1376264 | tf_op jit(solution)/shard_map/ppermute | solution.py:340
  70.9 0.0 collective-permute-done.peer_ref.a_peer
  71.0 0.0 copy-done
  71.0 2.0 %shard_map.123 = (bf16[768,128]{1,0:T(8,128)(2,1)S(1)}, f32[768,256]{1,0:T(8,128)S(1)}, f32[768,1]{1,0:T(8,128)S(1)}) custom-call(s32[4]{0:T(128)S(1)} %pad_add_fusion.where_ref, bf16[96,1024]{1,0:T(8,128)(2,1)S(1)} %copy-done, bf16[1792,128]{1,0:T(8,128)(2,1)S(1)} %shard_map.122.own_ref.a_own, bf16[1792,128]{1,0:T(8,128)(2,1)S(1)} %collective-permute-done.peer_ref.a_peer), custom_call_target="tpu_custom_call" | custom-call | tf_op jit(solution)/shard_map/pallas_call | solution.py:342
  73.0 0.0 collective-permute-done.2.b_peer
  73.0 2.9 %shard_map.124 = (bf16[96,1024]{1,0:T(8,128)(2,1)}, bf16[6,16,128]{2,1,0:T(8,128)(2,1)}, bf16[6,16,128]{2,1,0:T(8,128)(2,1)}, bf16[64,2048]{1,0:T(8,128)(2,1)}) custom-call(s32[4]{0:T(128)S(1)} %pad_add_fusion.where_ref, s32[6]{0:T(128)S(1)} %select_reduce_fusion.page_ref, bf16[1792,128]{1,0:T(8,128)(2,1)S(1)} %shard_map.122.own_ref.a_own, ...), custom_call_target="tpu_custom_call" | custom-call | tf_op jit(solution)/shard_map/pallas_call | solution.py:353
  (1 shorter events, 0.0 us)
Async XLA Ops:
  4.9 10.3 %copy-start.3 = (s32[3072]{0:T(1024)S(1)}, s32[3072]{0:T(1024)}, u32[]{:S(2)}) copy-start(s32[3072]{0:T(1024)} %param.12) | copy-start | bytes 36868
  4.9 16.4 %all-to-all-start = ((bf16[8,144,128]{2,1,0:T(8,128)(2,1)}), bf16[8,144,128]{2,1,0:T(8,128)(2,1)S(1)}, u32[]{:S(2)}, u32[]{:S(2)}) async-start(bf16[8,144,128]{2,1,0:T(8,128)(2,1)} %shard_map.120), calls=%async_computation | async-start | bytes 589824 | tf_op jit(solution)/shard_map/all_to_all | solution.py:320
  15.1 1.4 %copy-start.4 = (s32[192]{0:T(256)S(1)}, s32[192]{0:T(256)}, u32[]{:S(2)}) copy-start(s32[192]{0:T(256)} %param.13) | copy-start | bytes 2308
  15.1 6.2 %copy-start.2 = (bf16[96,128]{1,0:T(8,128)(2,1)S(1)}, bf16[96,128]{1,0:T(8,128)(2,1)}, u32[]{:S(2)}) copy-start(bf16[96,128]{1,0:T(8,128)(2,1)} %nv_ref.1) | copy-start | bytes 73732
  15.1 6.2 %copy-start.1 = (bf16[96,128]{1,0:T(8,128)(2,1)S(1)}, bf16[96,128]{1,0:T(8,128)(2,1)}, u32[]{:S(2)}) copy-start(bf16[96,128]{1,0:T(8,128)(2,1)} %nk_ref.1) | copy-start | bytes 73732
  50.6 20.3 %copy-start = (bf16[96,1024]{1,0:T(8,128)(2,1)S(1)}, bf16[96,1024]{1,0:T(8,128)(2,1)}, u32[]{:S(2)}) copy-start(bf16[96,1024]{1,0:T(8,128)(2,1)} %q_ref.1) | copy-start | bytes 589828
  51.1 11.8 %collective-permute-start.1 = (bf16[1792,128]{1,0:T(8,128)(2,1)S(1)}, bf16[1792,128]{1,0:T(8,128)(2,1)S(1)}, u32[]{:S(2)}, u32[]{:S(2)}) collective-permute-start(bf16[1792,128]{1,0:T(8,128)(2,1)S(1)} %shard_map.122.own_ref.a_own), channel_id=1, source_target_pairs={{0,1},{1,0},{2,3},{3,2},{4,5},{5,4},{6,7},{7,6},{8,9},{9,8},{10,11... | collective-permute-start | bytes 1376264 | tf_op jit(solution)/shard_map/ppermute | solution.py:338
  53.4 17.5 %collective-permute-start = (bf16[1792,128]{1,0:T(8,128)(2,1)S(1)}, bf16[1792,128]{1,0:T(8,128)(2,1)S(1)}, u32[]{:S(2)}, u32[]{:S(2)}) collective-permute-start(bf16[1792,128]{1,0:T(8,128)(2,1)S(1)} %shard_map.122.own_ref.a_own), channel_id=1, source_target_pairs={{0,16},{16,0},{1,17},{17,1},{2,18},{18,2},{3,19},{19,3},{4,20},{20... | collective-permute-start | bytes 1376264 | tf_op jit(solution)/shard_map/ppermute | solution.py:339
  63.0 10.0 %collective-permute-start.2 = (bf16[1792,128]{1,0:T(8,128)(2,1)S(1)}, bf16[1792,128]{1,0:T(8,128)(2,1)S(1)}, u32[]{:S(2)}, u32[]{:S(2)}) collective-permute-start(bf16[1792,128]{1,0:T(8,128)(2,1)S(1)} %collective-permute-done.1.b_own), channel_id=1, source_target_pairs={{0,16},{16,0},{1,17},{17,1},{2,18},{18,2},{3,19},{19,3},{4,20},{20... | collective-permute-start | bytes 1376264 | tf_op jit(solution)/shard_map/ppermute | solution.py:340
